TPU v7x, 32 devices: a whole 2x2x4 slice. The times are simulated.
32 devices in a mesh: section: 2 (over core), dp: 16 (over z, y, x).
Axes of the slice: x: 2, y: 2, z: 4, core: 2. Of those that a mesh axis runs over, the one named last changes fastest.
Arguments:
- latent: bfloat16 [32768, 256], P('dp'), may hold values from -6 to 6
- codes: int32 [2, 5, 32768], P(None, None, 'dp'), may hold values from 0 to 31, as said below
- targets: int32 [2, 5, 32768], P(None, None, 'dp'), may hold values from 0 to 600
- valid: int32 [5, 32768], P(None, 'dp'), may hold values from 0 to 1
- code_table: float32 [2, 32, 256], P('section'), may hold values from -6 to 6
- code_table_mom: float32 [2, 32, 256], P('section'), may hold values from -1.25 to 1.25
- code_table_avg: float32 [2, 32, 256], P('section'), may hold values from -6 to 6
- in_weight: float32 [2, 256, 256], P('section'), may hold values from -0.375 to 0.375
- in_weight_mom: float32 [2, 256, 256], P('section'), may hold values from -1.25 to 1.25
- in_weight_avg: float32 [2, 256, 256], P('section'), may hold values from -0.375 to 0.375
- gains: float32 [2, 2, 256], P('section'), may hold values from 0.5 to 1.5
- gains_mom: float32 [2, 2, 256], P('section'), may hold values from -8 to 8
- gains_avg: float32 [2, 2, 256], P('section'), may hold values from 0.5 to 1.5
- up_weight: float32 [2, 256, 256], P('section'), may hold values from -0.375 to 0.375
- up_weight_mom: float32 [2, 256, 256], P('section'), may hold values from -1.25 to 1.25
- up_weight_avg: float32 [2, 256, 256], P('section'), may hold values from -0.375 to 0.375
- down_weight: float32 [2, 256, 256], P('section'), may hold values from -0.375 to 0.375
- down_weight_mom: float32 [2, 256, 256], P('section'), may hold values from -1.25 to 1.25
- down_weight_avg: float32 [2, 256, 256], P('section'), may hold values from -0.375 to 0.375
- head_weight: float32 [2, 256, 601], P('section'), may hold values from -0.75 to 0.75
- head_weight_mom: float32 [2, 256, 601], P('section'), may hold values from -1.25 to 1.25
- head_weight_avg: float32 [2, 256, 601], P('section'), may hold values from -0.75 to 0.75
Outputs:
- ends: float32 [2, 32768, 256], P('section', 'dp')
- table_momentum: float32 [2, 32, 256], P('section')
- table_average: float32 [2, 32, 256], P('section')
- table_master: float32 [2, 32, 256], P('section')
- table_copy: bfloat16 [2, 32, 256], P('section')
- input_momentum: float32 [2, 256, 256], P('section')
- input_average: float32 [2, 256, 256], P('section')
- input_master: float32 [2, 256, 256], P('section')
- input_copy: bfloat16 [2, 256, 256], P('section')
- gain_momentum: float32 [2, 2, 256], P('section')
- gain_average: float32 [2, 2, 256], P('section')
- gain_master: float32 [2, 2, 256], P('section')
- gain_copy: bfloat16 [2, 2, 256], P('section')
- upper_momentum: float32 [2, 256, 256], P('section')
- upper_average: float32 [2, 256, 256], P('section')
- upper_master: float32 [2, 256, 256], P('section')
- upper_copy: bfloat16 [2, 256, 256], P('section')
- lower_momentum: float32 [2, 256, 256], P('section')
- lower_average: float32 [2, 256, 256], P('section')
- lower_master: float32 [2, 256, 256], P('section')
- lower_copy: bfloat16 [2, 256, 256], P('section')
- heads_momentum: float32 [2, 256, 601], P('section')
- heads_average: float32 [2, 256, 601], P('section')
- heads_master: float32 [2, 256, 601], P('section')
- heads_copy: bfloat16 [2, 256, 601], P('section')
Inputs may be any that keep to these rules, and one draw needn't show every extreme that they name: codes[0] holds actions below 4, codes[1] chance codes below 32.
All inputs are finite; a program needn't handle non-finite values.
Results may differ from a plain program's by a relative error of at most 0.012.
Values may be sent and summed in bfloat16 or wider, within the bound.
No kernel may reach another device: no remote copies, remote signals or barrier semaphores. Data moves between devices by JAX's collectives and lax.ppermute only.
A program may use at most 64 MiB of HBM per device.

v0:
```python
import jax
import jax.numpy as jnp
from jax import lax
from jax.sharding import PartitionSpec as P

EPS = 1e-05
MOMENTUM = 0.5
AVERAGE = 0.9
RATE = 0.2
GRAD_SCALE = 4.0


def shifted_2(array, axis, by):
    length = lax.axis_size(axis)
    return lax.ppermute(array, axis, [(i, (i + by) % length) for i in range(length)])


def layer_norm(value, gain):
    centered = value - jnp.mean(value, axis=-1, keepdims=True)
    scale = lax.rsqrt(jnp.mean(centered * centered, axis=-1, keepdims=True) + EPS)
    return centered * scale * gain


def norm_gelu(value, gain):
    return jax.nn.gelu(layer_norm(value, gain))


def pickers(code_ids, count_codes):
    return (code_ids[:, None] == jnp.arange(count_codes)[None, :]).astype(jnp.bfloat16)


def tower_front(inputs, code_ids, table_low, in_low, up_low, gain_in, gain_block):
    picker = pickers(code_ids, table_low.shape[0])
    pre_norm = jnp.dot(inputs, in_low, preferred_element_type=jnp.float32) + jnp.dot(
        picker, table_low, preferred_element_type=jnp.float32
    )
    hidden = norm_gelu(pre_norm, gain_in)
    normed = layer_norm(hidden, gain_block).astype(jnp.bfloat16)
    inner = jnp.dot(normed, up_low, preferred_element_type=jnp.float32)
    return (pre_norm, hidden, inner)


def tower_rear(hidden, inner, down_low):
    active = jax.nn.gelu(inner).astype(jnp.bfloat16)
    state = hidden + jnp.dot(active, down_low, preferred_element_type=jnp.float32)
    return (active, state)


def tower_back(
    inputs, pre_norm, hidden, inner, code_ids, goal_ids, weight, incoming, lows, gain_in, gain_block
):
    table_low, in_low, up_low, down_low, head_low = lows
    active, state = tower_rear(hidden, inner, down_low)
    sent = state.astype(jnp.bfloat16)
    logits = jnp.dot(sent, head_low, preferred_element_type=jnp.float32)
    probs = jax.nn.softmax(logits, axis=1)
    chosen = (goal_ids[:, None] == jnp.arange(logits.shape[1])[None, :]).astype(jnp.float32)
    logit_grad = ((probs - chosen) * weight[:, None]).astype(jnp.bfloat16)
    head_grad = jnp.dot(sent.T, logit_grad, preferred_element_type=jnp.float32)
    state_grad = jnp.dot(logit_grad, head_low.T, preferred_element_type=jnp.float32) + incoming
    branch_grad = state_grad.astype(jnp.bfloat16)
    down_grad = jnp.dot(active.T, branch_grad, preferred_element_type=jnp.float32)
    active_grad = jnp.dot(branch_grad, down_low.T, preferred_element_type=jnp.float32)
    leftover, gelu_pull = jax.vjp(jax.nn.gelu, inner)
    inner_grad = gelu_pull(active_grad)[0].astype(jnp.bfloat16)
    normed = layer_norm(hidden, gain_block).astype(jnp.bfloat16)
    up_grad = jnp.dot(normed.T, inner_grad, preferred_element_type=jnp.float32)
    normed_grad = jnp.dot(inner_grad, up_low.T, preferred_element_type=jnp.float32)
    leftover, norm_pull = jax.vjp(layer_norm, hidden, gain_block)
    hidden_part, block_gain_grad = norm_pull(normed_grad)
    hidden_grad = state_grad + hidden_part
    leftover, front_pull = jax.vjp(norm_gelu, pre_norm, gain_in)
    pre_grad, in_gain_grad = front_pull(hidden_grad)
    pre_low = pre_grad.astype(jnp.bfloat16)
    picker = pickers(code_ids, table_low.shape[0])
    table_grad = jnp.dot(picker.T, pre_low, preferred_element_type=jnp.float32)
    in_grad = jnp.dot(inputs.T, pre_low, preferred_element_type=jnp.float32)
    input_grad = jnp.dot(pre_low, in_low.T, preferred_element_type=jnp.float32).astype(jnp.bfloat16)
    gain_grad = jnp.stack([in_gain_grad, block_gain_grad])
    return ((table_grad, in_grad, gain_grad, up_grad, down_grad, head_grad), input_grad)


def update(weight, moment, average, grad, count):
    step_grad = GRAD_SCALE * grad[None] * lax.rsqrt(count)
    new_moment = MOMENTUM * moment + step_grad
    new_weight = weight - RATE * (step_grad + MOMENTUM * new_moment)
    new_average = AVERAGE * average + (1.0 - AVERAGE) * new_weight
    return (new_moment, new_average, new_weight, new_weight.astype(jnp.bfloat16))


def on_device(
    latent,
    codes,
    targets,
    valid,
    code_table,
    code_table_mom,
    code_table_avg,
    in_weight,
    in_weight_mom,
    in_weight_avg,
    gains,
    gains_mom,
    gains_avg,
    up_weight,
    up_weight_mom,
    up_weight_avg,
    down_weight,
    down_weight_mom,
    down_weight_avg,
    head_weight,
    head_weight_mom,
    head_weight_avg,
):
    section = lax.axis_index("section")
    rows = latent.shape[0]
    width = latent.shape[1]
    half = rows // 2
    unroll = codes.shape[1]
    ticks = 2 * unroll + 1
    count_local = jnp.sum(valid).astype(jnp.float32)
    count = lax.psum(count_local, "dp")
    lows = (
        code_table[0].astype(jnp.bfloat16),
        in_weight[0].astype(jnp.bfloat16),
        up_weight[0].astype(jnp.bfloat16),
        down_weight[0].astype(jnp.bfloat16),
        head_weight[0].astype(jnp.bfloat16),
    )
    table_low, in_low, up_low, down_low, head_low = lows
    gain_in = gains[0, 0]
    gain_block = gains[0, 1]
    code_rows = jnp.where(section == 0, codes[0], codes[1])
    goal_rows = jnp.where(section == 0, targets[0], targets[1])

    def place(tick):
        shifted = tick - section
        group = shifted % 2
        step = shifted // 2
        running = (shifted >= 0) & (step < unroll)
        step_clip = jnp.clip(step, 0, unroll - 1)
        start = group * half
        code_ids = lax.dynamic_slice(code_rows, (step_clip, start), (1, half))[0]
        goal_ids = lax.dynamic_slice(goal_rows, (step_clip, start), (1, half))[0]
        weight = lax.dynamic_slice(valid, (step_clip, start), (1, half))[0].astype(
            jnp.float32
        ) * running.astype(jnp.float32)
        return (start, step, running, code_ids, goal_ids, weight)

    def forward_tick(carry, tick):
        received, last_state = carry
        start, step, running, code_ids, goal_ids, weight = place(tick)
        first = lax.dynamic_slice_in_dim(latent, start, half, 0)
        inputs = jnp.where((section == 0) & (tick < 2), first, received)
        pre_norm, hidden, inner = tower_front(
            inputs, code_ids, table_low, in_low, up_low, gain_in, gain_block
        )
        active, state = tower_rear(hidden, inner, down_low)
        finishing = (section == 1) & (step == unroll - 1) & running
        former = lax.dynamic_slice_in_dim(last_state, start, half, 0)
        last_state = lax.dynamic_update_slice_in_dim(
            last_state, jnp.where(finishing, state, former), start, 0
        )
        passed = shifted_2(state.astype(jnp.bfloat16), "section", 1)
        saved = (inputs,)
        return ((passed, last_state), saved)

    start_carry = (jnp.zeros((half, width), jnp.bfloat16), jnp.zeros((rows, width), jnp.float32))
    tick_ids = jnp.arange(ticks, dtype=jnp.int32)
    (leftover, last_state), saved_all = lax.scan(forward_tick, start_carry, tick_ids)

    def backward_tick(carry, pieces):
        tick, saved = pieces
        received, totals, first_grad = carry
        start, step, running, code_ids, goal_ids, weight = place(tick)
        inputs = saved[0]
        pre_norm, hidden, inner = tower_front(
            inputs, code_ids, table_low, in_low, up_low, gain_in, gain_block
        )
        incoming = jnp.where(running, received.astype(jnp.float32), 0.0)
        grads, input_grad = tower_back(
            inputs,
            pre_norm,
            hidden,
            inner,
            code_ids,
            goal_ids,
            weight,
            incoming,
            lows,
            gain_in,
            gain_block,
        )
        totals = tuple((total + piece for total, piece in zip(totals, grads)))
        starting = (section == 0) & (step == 0) & running
        former = lax.dynamic_slice_in_dim(first_grad, start, half, 0)
        first_grad = lax.dynamic_update_slice_in_dim(
            first_grad, jnp.where(starting, input_grad.astype(jnp.float32), former), start, 0
        )
        passed = shifted_2(input_grad, "section", 1)
        return ((passed, totals, first_grad), None)

    zero_totals = (
        jnp.zeros(code_table.shape[1:], jnp.float32),
        jnp.zeros(in_weight.shape[1:], jnp.float32),
        jnp.zeros(gains.shape[1:], jnp.float32),
        jnp.zeros(up_weight.shape[1:], jnp.float32),
        jnp.zeros(down_weight.shape[1:], jnp.float32),
        jnp.zeros(head_weight.shape[1:], jnp.float32),
    )
    back_carry = (
        jnp.zeros((half, width), jnp.bfloat16),
        zero_totals,
        jnp.zeros((rows, width), jnp.float32),
    )
    (leftover, totals, first_grad), unused = lax.scan(
        backward_tick, back_carry, (tick_ids, saved_all), reverse=True
    )
    ends = jnp.where(section == 0, first_grad, last_state)[None]
    table_total, in_total, gain_total, up_total, down_total, head_total = totals
    table_sum, in_sum, gain_sum, up_sum, down_sum, head_sum = lax.psum(
        (table_total, in_total, gain_total, up_total, down_total, head_total), "dp"
    )
    table_m, table_a, table_w, table_c = update(
        code_table, code_table_mom, code_table_avg, table_sum, count
    )
    input_m, input_a, input_w, input_c = update(
        in_weight, in_weight_mom, in_weight_avg, in_sum, count
    )
    gain_m, gain_a, gain_w, gain_c = update(gains, gains_mom, gains_avg, gain_sum, count)
    upper_m, upper_a, upper_w, upper_c = update(
        up_weight, up_weight_mom, up_weight_avg, up_sum, count
    )
    lower_m, lower_a, lower_w, lower_c = update(
        down_weight, down_weight_mom, down_weight_avg, down_sum, count
    )
    heads_m, heads_a, heads_w, heads_c = update(
        head_weight, head_weight_mom, head_weight_avg, head_sum, count
    )
    return (
        ends,
        table_m,
        table_a,
        table_w,
        table_c,
        input_m,
        input_a,
        input_w,
        input_c,
        gain_m,
        gain_a,
        gain_w,
        gain_c,
        upper_m,
        upper_a,
        upper_w,
        upper_c,
        lower_m,
        lower_a,
        lower_w,
        lower_c,
        heads_m,
        heads_a,
        heads_w,
        heads_c,
    )


def solution(mesh):
    in_specs = (
        P("dp", None),
        P(None, None, "dp"),
        P(None, None, "dp"),
        P(None, "dp"),
        P("section", None, None),
        P("section", None, None),
        P("section", None, None),
        P("section", None, None),
        P("section", None, None),
        P("section", None, None),
        P("section", None, None),
        P("section", None, None),
        P("section", None, None),
        P("section", None, None),
        P("section", None, None),
        P("section", None, None),
        P("section", None, None),
        P("section", None, None),
        P("section", None, None),
        P("section", None, None),
        P("section", None, None),
        P("section", None, None),
    )
    out_specs = (
        P("section", "dp", None),
        P("section", None, None),
        P("section", None, None),
        P("section", None, None),
        P("section", None, None),
        P("section", None, None),
        P("section", None, None),
        P("section", None, None),
        P("section", None, None),
        P("section", None, None),
        P("section", None, None),
        P("section", None, None),
        P("section", None, None),
        P("section", None, None),
        P("section", None, None),
        P("section", None, None),
        P("section", None, None),
        P("section", None, None),
        P("section", None, None),
        P("section", None, None),
        P("section", None, None),
        P("section", None, None),
        P("section", None, None),
        P("section", None, None),
        P("section", None, None),
    )
    return jax.shard_map(
        on_device, mesh=mesh, in_specs=in_specs, out_specs=out_specs, check_vma=False
    )
```

profile of v0, /device:TPU:0, one launch (start us, length us, event | category | flops | bytes accessed | tf_op | source)
XLA Modules:
  0.0 726.7 jit_solution(10491124206516619918)
XLA Ops:
  12.5 1.9 copy.68
  18.4 170.7 %while.46 = (s32[]{:T(128)}, bf16[1024,256]{0,1:T(8,128)(2,1)S(1)}, f32[2048,256]{1,0:T(8,128)}, bf16[11,1024,256]{1,2,0:T(8,128)(2,1)}, s32[11]{0:T(128)S(1)}, ...) while((s32[]{:T(128)}, bf16[1024,256]{0,1:T(8,128)(2,1)S(1)}, ...), condition=%wide.region_5.6_spmd, body=%wide.region_0.5_spmd.sunk | while | flops 438077472 | bytes 35119744 | solution.py:170
  26.6 3.7 broadcast_select_fusion.6
  42.3 3.7 broadcast_select_fusion.6
  57.6 3.7 broadcast_select_fusion.6
  73.4 3.7 broadcast_select_fusion.6
  88.6 3.7 broadcast_select_fusion.6
  104.4 3.7 broadcast_select_fusion.6
  119.7 3.7 broadcast_select_fusion.6
  135.5 3.7 broadcast_select_fusion.6
  150.7 3.7 broadcast_select_fusion.6
  166.6 3.7 broadcast_select_fusion.6
  181.8 3.7 broadcast_select_fusion.6
  191.9 398.5 %while.47 = (s32[]{:T(128)}, bf16[1024,256]{1,0:T(8,128)(2,1)}, f32[32,256]{1,0:T(8,128)S(1)}, f32[256,256]{1,0:T(8,128)}, f32[2,256]{1,0:T(2,128)}, /*index=5*/...) while((s32[]{:T(128)}, bf16[1024,256]{1,0:T(8,128)(2,1)}, ...), condition=%wide.region_19.20_spmd.clone, body=%wide.region_6.19_spmd.clone.sunk | while | flops 2248316416 | bytes 85677136 | solution.py:216
  202.8 1.9 fusion.199
  209.8 1.9 fusion.202
  215.1 2.0 multiply_reduce_fusion.22
  217.9 2.7 select_dynamic-update-slice_fusion.2
  221.0 2.6 convolution_add_fusion.19
  239.0 1.9 fusion.199
  246.0 1.9 fusion.202
  251.4 2.0 multiply_reduce_fusion.22
  254.2 2.7 select_dynamic-update-slice_fusion.2
  257.1 2.7 convolution_add_fusion.19
  275.2 1.9 fusion.199
  282.2 1.9 fusion.202
  287.5 2.0 multiply_reduce_fusion.22
  290.3 2.7 select_dynamic-update-slice_fusion.2
  293.4 2.7 convolution_add_fusion.19
  311.5 1.9 fusion.199
  318.5 1.9 fusion.202
  323.8 2.0 multiply_reduce_fusion.22
  326.6 2.7 select_dynamic-update-slice_fusion.2
  329.6 2.7 convolution_add_fusion.19
  354.7 1.9 fusion.202
  360.0 2.0 multiply_reduce_fusion.22
  362.8 2.7 select_dynamic-update-slice_fusion.2
  365.9 2.7 convolution_add_fusion.19
  391.0 1.9 fusion.202
  396.3 2.0 multiply_reduce_fusion.22
  399.1 2.7 select_dynamic-update-slice_fusion.2
  402.0 2.7 convolution_add_fusion.19
  427.1 1.9 fusion.202
  432.4 2.0 multiply_reduce_fusion.22
  435.3 2.7 select_dynamic-update-slice_fusion.2
  438.3 2.7 convolution_add_fusion.19
  468.7 2.0 multiply_reduce_fusion.22
  471.6 2.7 select_dynamic-update-slice_fusion.2
  474.5 2.7 convolution_add_fusion.19
  504.9 2.0 multiply_reduce_fusion.22
  507.7 2.7 select_dynamic-update-slice_fusion.2
  510.8 2.7 convolution_add_fusion.19
  528.8 1.9 fusion.199
  541.2 2.0 multiply_reduce_fusion.22
  544.0 2.7 select_dynamic-update-slice_fusion.2
  546.9 2.7 convolution_add_fusion.19
  565.0 1.9 fusion.199
  577.3 2.0 multiply_reduce_fusion.22
  580.2 2.7 select_dynamic-update-slice_fusion.2
  583.2 2.7 convolution_add_fusion.19
  592.6 79.9 %all-reduce = (f32[32,256]{1,0:T(8,128)S(1)}, f32[]{:T(128)}, f32[2,256]{1,0:T(2,128)S(1)}) all-reduce(f32[32,256]{1,0:T(8,128)S(1)} %get-tuple-element.728, f32[]{:T(128)S(6)} %convert_element_type.218, f32[2,256]{1,0:T(2,128)} %get-tuple-element.730), channel_id=1, replica_groups=mesh['section'=2,'dp'=16] {'dp'}, use_global_device_ids=true, to_apply=%region_20.21 | all-reduce | flops 8705 | bytes 69640 | tf_op jit(solution)/shard_map/psum | solution.py:221
  678.6 3.3 select_bitcast_fusion
  681.9 27.9 %all-reduce.4.cloned.1.call-done = (f32[256,256]{1,0:T(8,128)}, f32[256,256]{1,0:T(8,128)}, f32[256,256]{1,0:T(8,128)}, f32[256,601]{0,1:T(8,128)}) async-done(((f32[256,256]{1,0:T(8,128)}, f32[256,256]{1,0:T(8,128)}, f32[256,256]{1,0:T(8,128)}, f32[256,601]{0,1:T(8,128)}), (f32[256,256]{1,0:T(8,128)}, f32[256,256]{1,0:T(8,128)}, f32[256,256]{1,0:T(8,128)}, ...) | async-done | bytes 1401872 | tf_op jit(solution)/shard_map/psum | solution.py:221
  711.0 3.2 multiply_add_fusion.2
  (1021 shorter events, 421.0 us)
Async XLA Ops:
  7.2 702.6 %all-reduce.4.cloned.1.call-start = ((), (), s32[]{:S(2)}) async-start(), calls=%async_computation | async-start | bytes 2818048 | tf_op jit(solution)/shard_map/psum | solution.py:221
  30.2 2.9 collective-permute-start
  45.9 2.4 collective-permute-start
  61.2 2.9 collective-permute-start
  77.0 2.4 collective-permute-start
  92.3 3.0 collective-permute-start
  108.1 2.4 collective-permute-start
  123.3 2.9 collective-permute-start
  139.1 2.4 collective-permute-start
  154.4 3.0 collective-permute-start
  170.2 2.4 collective-permute-start
  185.5 2.6 collective-permute-start
  202.8 7.0 copy-start.33
  209.8 5.3 copy-start
  220.7 6.6 collective-permute-start.1
  239.0 7.0 copy-start.33
  246.0 5.3 copy-start
  256.9 6.5 collective-permute-start.1
  260.4 3.1 copy-start.25
  275.2 7.0 copy-start.33
  282.2 5.3 copy-start
  293.1 6.7 collective-permute-start.1
  296.7 3.1 copy-start.25
  311.5 7.0 copy-start.33
  318.5 5.3 copy-start
  329.4 6.5 collective-permute-start.1
  332.8 3.1 copy-start.25
  347.6 7.0 copy-start.33
  354.6 5.3 copy-start
  365.5 6.7 collective-permute-start.1
  383.9 7.0 copy-start.33
  390.9 5.3 copy-start
  401.8 6.5 collective-permute-start.1
  420.1 7.0 copy-start.33
  427.1 5.3 copy-start
  438.0 6.7 collective-permute-start.1
  456.4 7.0 copy-start.33
  463.4 5.3 copy-start
  474.3 6.5 collective-permute-start.1
  492.5 7.0 copy-start.33
  499.6 5.3 copy-start
  510.4 6.7 collective-permute-start.1
  528.8 7.0 copy-start.33
  535.9 5.3 copy-start
  546.7 6.5 collective-permute-start.1
  565.0 7.0 copy-start.33
  572.0 5.3 copy-start
  582.9 6.7 collective-permute-start.1
  674.5 7.4 %copy-start.32 = (f32[1,2,256]{2,1,0:T(2,128)}, f32[1,2,256]{2,1,0:T(2,128)S(1)}, u32[]{:S(2)}) copy-start(f32[1,2,256]{2,1,0:T(2,128)S(1)} %get-tuple-element.946) | copy-start | bytes 6148
  677.2 4.7 copy-start.29
  678.6 32.4 %copy-start.7 = (f32[1,256,601]{1,0,2:T(1,128)S(1)}, f32[1,256,601]{1,0,2:T(1,128)}, u32[]{:S(2)}) copy-start(f32[1,256,601]{1,0,2:T(1,128)} %param.45) | copy-start | bytes 1846276
  678.6 32.4 %copy-start.15 = (f32[1,256,601]{1,0,2:T(1,128)S(1)}, f32[1,256,601]{1,0,2:T(1,128)}, u32[]{:S(2)}) copy-start(f32[1,256,601]{1,0,2:T(1,128)} %param.47) | copy-start | bytes 1846276
  678.6 32.4 %copy-start.16 = (f32[1,256,601]{1,0,2:T(1,128)S(1)}, f32[1,256,601]{1,0,2:T(1,128)}, u32[]{:S(2)}) copy-start(f32[1,256,601]{1,0,2:T(1,128)} %param.46) | copy-start | bytes 1846276
  711.0 4.1 copy-start.9
  711.0 4.1 copy-start.21
  711.0 4.1 copy-start.28
  711.0 4.9 copy-start.18
  714.2 4.0 copy-start.8
  714.3 3.2 copy-start.19
  714.3 4.0 copy-start.14
  714.3 4.0 copy-start.23
  714.3 4.0 copy-start.26
  715.9 4.0 copy-start.11
  715.9 3.2 copy-start.20
  (145 other events, 305.9 us)
Sparse Core Ops, SparseCore 0:
  590.5 119.2 all-reduce.3
where the time goes:
time: 736 us; the launch traced here: 727 us
  matrix products  289 us (39%)
  local copies, waits for them, and re-layouts  148 us (20%)
  other arithmetic  133 us (18%)
  blocking collectives  79.9 us (11%)
  waiting for transfers between devices  28 us (4%)
  loops' own time  27.4 us (4%)
  between operations  15.6 us (2%)
    psum x1, blocking collectives, on_device(): lax.psum((table_total, in_total, gain_total, up_total, down_total, head_t...  79.9 us
    dot_general x22, matrix products, tower_rear(): jnp.dot(active, down_low, preferred_element_type=jnp.float32)  61 us
    reduce_sum x33, other arithmetic, layer_norm(): return centered * scale * gain  44.5 us
    while x352, local copies, waits for them, and re-layouts  38.9 us
    dot_general x11, matrix products, tower_back(): jnp.dot(pre_low, in_low.T, preferred_element_type=jnp.float32)  30 us
    dot_general x11, matrix products, tower_back(): up_grad = jnp.dot(normed.T, inner_grad, preferred_element_type=jnp.float32)  29.6 us
    psum x1, waiting for transfers between devices, on_device(): lax.psum((table_total, in_total, gain_total, up_total, down_total, head_t...  27.9 us
    dot_general x22, matrix products, tower_front(): jnp.dot(picker, table_low, preferred_element_type=jnp.float32)  22.6 us
  transfers between devices with their start and end apart: 23, of which 1 were waited for; matrix products, arithmetic and copies ran while one was open for 14% of the time, Pallas kernels for 0%

commit v1 on v0

v1 whole, which is shorter than its diff:
```python
import functools

import jax
import jax.numpy as jnp
from jax import lax
from jax.experimental import pallas as pl
from jax.experimental.pallas import tpu as pltpu
from jax.sharding import PartitionSpec as P

EPS = 1e-05
MOMENTUM = 0.5
AVERAGE = 0.9
RATE = 0.2
GRAD_SCALE = 4.0
GELU_LINE = 0.7978845608028654
GELU_CUBE = 0.7978845608028654 * 0.044715

BF16 = jnp.bfloat16
F32 = jnp.float32
LANES = 128
TILE = 16
BITS = 24
VMEM = 60 * 1024 * 1024


def dot(left, right):
    return jnp.dot(left, right, preferred_element_type=F32)


def dot_right_t(left, right):
    return lax.dot_general(left, right, (((1,), (1,)), ((), ())), preferred_element_type=F32)


def dot_left_t(left, right):
    return lax.dot_general(left, right, (((0,), (0,)), ((), ())), preferred_element_type=F32)


def gelu_and_slope(value):
    square = value * value
    half = 0.5 + 0.5 * jnp.tanh(value * (GELU_LINE + GELU_CUBE * square))
    result = value * half
    return result, half + result * (1.0 - half) * (2 * GELU_LINE + (6 * GELU_CUBE) * square)


def normalise(value):
    part = 1.0 / value.shape[-1]
    centered = value - jnp.sum(value, axis=-1, keepdims=True) * part
    scale = lax.rsqrt(jnp.sum(centered * centered, axis=-1, keepdims=True) * part + EPS)
    return centered * scale, scale


def normalise_back(out_grad, product, gain, unit, scale):
    part = 1.0 / unit.shape[-1]
    scaled = out_grad * gain
    first = jnp.sum(scaled, axis=-1, keepdims=True) * part
    second = jnp.sum(product * gain, axis=-1, keepdims=True) * part
    return (scaled - first - unit * second) * scale


class Layout:
    def __init__(self, codes, width, bins):
        self.codes, self.width, self.bins = codes, width, bins
        self.wide = -(-bins // LANES) * LANES
        spots, at = {}, 0
        for name in ("in", "up", "down"):
            spots[name] = (at, at + width)
            at += width
        self.full_heads = self.wide // width
        self.rest = self.wide - self.full_heads * width
        for part in range(self.full_heads):
            spots["head", part] = (at, at + width)
            at += width
        self.folds = 0 if self.rest == 0 else width // self.rest
        if self.rest:
            rows = width // self.folds
            spots["head_rest"] = (at, at + rows)
            at += rows
        codes_up = -(-codes // TILE) * TILE
        spots["table"] = (at, at + codes)
        at += codes_up
        spots["tail"] = (at, at + TILE)
        at += TILE
        self.spots = spots
        self.rows = -(-at // 64) * 64
        self.used = at

    def store_head(self, ref, head):
        width = self.width
        for part in range(self.full_heads):
            low, high = self.spots["head", part]
            ref[low:high, :] = head[:, part * width : (part + 1) * width].astype(ref.dtype)
        if self.rest:
            low, high = self.spots["head_rest"]
            tall = width // self.folds
            rest = head[:, self.full_heads * width :]
            for fold in range(self.folds):
                ref[low:high, fold * self.rest : (fold + 1) * self.rest] = rest[
                    fold * tall : (fold + 1) * tall, :
                ].astype(ref.dtype)

    def load_head(self, ref):
        parts = [ref[low:high, :] for low, high in (self.spots["head", p] for p in range(self.full_heads))]
        if self.rest:
            low, high = self.spots["head_rest"]
            parts.append(
                jnp.concatenate(
                    [ref[low:high, f * self.rest : (f + 1) * self.rest] for f in range(self.folds)],
                    axis=0,
                )
            )
        return jnp.concatenate(parts, axis=1)


def split_three(value):
    high = value.astype(BF16)
    left = value - high.astype(F32)
    middle = left.astype(BF16)
    low = (left - middle.astype(F32)).astype(BF16)
    return high, middle, low


def pack_kernel(lay, table, w_in, w_up, w_down, w_head, gains, out):
    for name, ref in (("in", w_in), ("up", w_up), ("down", w_down), ("table", table)):
        low, high = lay.spots[name]
        out[low:high, :] = ref[0].astype(BF16)
    head = w_head[0]
    head = jnp.concatenate([head, jnp.zeros((lay.width, lay.wide - lay.bins), F32)], axis=1)
    lay.store_head(out, head)
    low, high = lay.spots["tail"]
    pieces = [piece.astype(F32) for piece in split_three(gains[0])]
    pieces.append(jnp.zeros((high - low - 6, lay.width), F32))
    out[low:high, :] = jnp.concatenate(pieces, axis=0).astype(BF16)
    out[high:, :] = jnp.zeros((lay.rows - high, lay.width), BF16)


def towers_kernel(lay, steps, count_rows, which, latent, codes, targets, valid, whole_valid, mine, theirs,
                  keep, send, ends_mine, ends_send,
                  w_in, w_up, w_down, w_head, table, gains,
                  g_in, g_up, g_down, g_head, g_table, g_gain,
                  meta, sent_all, unit_one, slope_one, unit_two, slope_two, active_all,
                  scale_one, scale_two, back, final):
    rows, width = latent.shape
    code_count = lay.codes
    section = which[0]

    @pl.when(pl.program_id(0) == 0)
    def start():
        for ref in (g_in, g_up, g_down, g_head, g_table, g_gain):
            ref[...] = jnp.zeros_like(ref)
        for packed, slot in ((mine, section), (theirs, 1 - section)):
            for name, ref in (("in", w_in), ("up", w_up), ("down", w_down), ("table", table)):
                low, high = lay.spots[name]
                ref[slot] = packed[low:high, :]
            w_head[slot] = lay.load_head(packed)
            low, high = lay.spots["tail"]
            tail = packed[low:high, :].astype(F32)
            gains[slot] = tail[0:2] + tail[2:4] + tail[4:6]

    for step in range(steps):
        line = jnp.concatenate(
            [codes[0, step : step + 1, :], codes[1, step : step + 1, :], targets[0, step : step + 1, :],
             targets[1, step : step + 1, :], valid[step : step + 1, :], jnp.zeros((3, rows), jnp.int32)], axis=0)
        meta[step] = line.T
    sent_all[0] = latent[...]

    def pick_of(step, tower):
        code = meta[step, :, tower : tower + 1]
        return (code == lax.broadcasted_iota(jnp.int32, (rows, code_count), 1)).astype(F32).astype(BF16)

    def forward(step, tower):
        at = 2 * step + tower
        pre = dot(sent_all[at], w_in[tower]) + dot(pick_of(step, tower), table[tower])
        unit, scale = normalise(pre)
        unit_one[at] = unit
        scale_one[at] = scale
        hidden, slope = gelu_and_slope(unit * gains[tower, 0:1, :])
        slope_one[at] = slope
        unit, scale = normalise(hidden)
        unit_two[at] = unit
        scale_two[at] = scale
        normed = (unit * gains[tower, 1:2, :]).astype(BF16)
        active, slope = gelu_and_slope(dot(normed, w_up[tower]))
        slope_two[at] = slope
        active = active.astype(BF16)
        active_all[at] = active
        state = hidden + dot(active, w_down[tower])
        sent_all[at + 1] = state.astype(BF16)
        final[...] = state

    def forward_step(step, carry):
        forward(step, 0)
        forward(step, 1)
        return carry

    lax.fori_loop(0, steps, forward_step, 0)
    back[...] = jnp.zeros_like(back)

    def backward(step, tower):
        at = 2 * step + tower
        sent = sent_all[at + 1]
        logits = dot(sent, w_head[tower])
        column = lax.broadcasted_iota(jnp.int32, (rows, lay.wide), 1)
        goal = meta[step, :, 2 + tower : 3 + tower]
        weight = meta[step, :, 4:5].astype(F32)
        logits = jnp.where(column < lay.bins, logits, -1e30)
        raised = jnp.exp(logits - jnp.max(logits, axis=-1, keepdims=True))
        ratio = weight / jnp.sum(raised, axis=-1, keepdims=True)
        logit_grad = (raised * ratio - jnp.where(column == goal, weight, 0.0)).astype(BF16)
        g_head[tower] += dot_left_t(sent, logit_grad)
        state_grad = dot_right_t(logit_grad, w_head[tower]) + back[...].astype(F32)
        branch_grad = state_grad.astype(BF16)
        g_down[tower] += dot_left_t(active_all[at], branch_grad)
        inner_grad = (dot_right_t(branch_grad, w_down[tower]) * slope_two[at]).astype(BF16)
        unit = unit_two[at]
        gain = gains[tower, 1:2, :]
        g_up[tower] += dot_left_t((unit * gain).astype(BF16), inner_grad)
        out_grad = dot_right_t(inner_grad, w_up[tower])
        product = out_grad * unit
        block_gain_grad = jnp.sum(product, axis=0, keepdims=True)
        hidden_grad = state_grad + normalise_back(out_grad, product, gain, unit, scale_two[at])
        out_grad = hidden_grad * slope_one[at]
        unit = unit_one[at]
        product = out_grad * unit
        in_gain_grad = jnp.sum(product, axis=0, keepdims=True)
        g_gain[tower] += jnp.concatenate([in_gain_grad, block_gain_grad], axis=0)
        pre_grad = normalise_back(out_grad, product, gains[tower, 0:1, :], unit, scale_one[at]).astype(BF16)
        g_table[tower] += dot_left_t(pick_of(step, tower), pre_grad)
        g_in[tower] += dot_left_t(sent_all[at], pre_grad)
        back[...] = dot_right_t(pre_grad, w_in[tower]).astype(BF16)

    def backward_step(turn, carry):
        step = steps - 1 - turn
        backward(step, 1)
        backward(step, 0)
        return carry

    lax.fori_loop(0, steps, backward_step, 0)
    first = back[...].astype(F32)
    last = final[...]
    is_first = section == 0
    ends_mine[...] = jnp.where(is_first, first, last)
    ends_send[...] = jnp.where(is_first, last, first).astype(BF16)

    @pl.when(pl.program_id(0) == pl.num_programs(0) - 1)
    def finish():
        count = jnp.sum(whole_valid[...].astype(F32), axis=(0, 1), keepdims=True).astype(jnp.int32)
        lane = lax.broadcasted_iota(jnp.int32, (1, width), 1)
        bits = jnp.where(lane < BITS, (count >> jnp.minimum(lane, BITS)) & 1, 0).astype(F32)
        for packed, slot in ((keep, section), (send, 1 - section)):
            kind = packed.dtype
            for name, ref in (("in", g_in), ("up", g_up), ("down", g_down), ("table", g_table)):
                low, high = lay.spots[name]
                packed[low:high, :] = ref[slot].astype(kind)
            lay.store_head(packed, g_head[slot])
            low, high = lay.spots["tail"]
            own = bits if packed is keep else jnp.zeros_like(bits)
            tail = jnp.concatenate([g_gain[slot], own, jnp.zeros((high - low - 3, width), F32)], axis=0)
            packed[low:high, :] = tail.astype(kind)
            packed[high:, :] = jnp.zeros((lay.rows - high, width), kind)


def update_kernel(lay, total, *refs):
    ins, outs = refs[:18], refs[18:]
    low, high = lay.spots["tail"]
    tail = total[low:high, :].astype(F32)
    lane = lax.broadcasted_iota(jnp.int32, (1, lay.width), 1)
    place = jnp.where(lane < BITS, (1 << jnp.minimum(lane, BITS)).astype(F32), 0.0)
    count = jnp.sum(tail[2:3] * place, axis=-1, keepdims=True)
    factor = GRAD_SCALE * lax.rsqrt(count)
    head = lay.load_head(total)[:, : lay.bins].astype(F32)
    grads = [None] * 6
    for at, name in ((0, "table"), (1, "in"), (3, "up"), (4, "down")):
        low, high = lay.spots[name]
        grads[at] = total[low:high, :].astype(F32)
    grads[2] = tail[0:2]
    grads[5] = head
    for at, grad in enumerate(grads):
        weight, moment, average = ins[3 * at : 3 * at + 3]
        step_grad = grad * factor
        new_moment = MOMENTUM * moment[0] + step_grad
        new_weight = weight[0] - RATE * (step_grad + MOMENTUM * new_moment)
        out_moment, out_average, out_weight, out_copy = outs[4 * at : 4 * at + 4]
        out_moment[0] = new_moment
        out_average[0] = AVERAGE * average[0] + (1.0 - AVERAGE) * new_weight
        out_weight[0] = new_weight
        out_copy[0] = new_weight.astype(BF16)


def swap(value):
    return lax.ppermute(value, "section", [(0, 1), (1, 0)])


def reduce_all(value, length):
    levels = [1 << bit for bit in range(length.bit_length() - 1)]
    index = lax.axis_index("dp")

    def across(array, mask):
        return lax.ppermute(array, "dp", [(i, i ^ mask) for i in range(length)])

    halving, whole = levels[:2], levels[2:]
    current = value
    for mask in halving:
        half = current.shape[0] // 2
        upper = (index // mask) % 2 == 1
        low, high = current[:half], current[half:]
        sent = jnp.where(upper, low, high)
        kept = jnp.where(upper, high, low)
        current = (kept.astype(F32) + across(sent, mask).astype(F32)).astype(BF16)
    for mask in whole:
        current = (current.astype(F32) + across(current, mask).astype(F32)).astype(BF16)
    for mask in reversed(halving):
        upper = (index // mask) % 2 == 1
        other = across(current, mask)
        current = jnp.where(upper, jnp.concatenate([other, current]), jnp.concatenate([current, other]))
    return current


def on_device(block, length, latent, codes, targets, valid, *weights):
    section = lax.axis_index("section").astype(jnp.int32)
    rows, width = latent.shape
    steps = codes.shape[1]
    own_rows = rows // 2
    block = min(block, own_rows)
    blocks = own_rows // block
    table, w_in, gains, w_up, w_down, w_head = weights[0::3]
    lay = Layout(table.shape[1], width, w_head.shape[2])
    packed_shape = (lay.rows, width)
    roomy = pltpu.CompilerParams(vmem_limit_bytes=VMEM)
    mine = pl.pallas_call(
        functools.partial(pack_kernel, lay),
        out_shape=jax.ShapeDtypeStruct(packed_shape, BF16),
        compiler_params=roomy,
        name="pack",
    )(table, w_in, w_up, w_down, w_head, gains)
    theirs = swap(mine)

    def spec_rows(*shape):
        return pl.BlockSpec(shape, lambda i, which: (which[0] * blocks + i,) + (0,) * (len(shape) - 1))

    def spec_lanes(*shape):
        return pl.BlockSpec(shape, lambda i, which: (0,) * (len(shape) - 1) + (which[0] * blocks + i,))

    def spec_whole(*shape):
        return pl.BlockSpec(shape, lambda i, which: (0,) * len(shape))

    def spec_out(*shape):
        return pl.BlockSpec(shape, lambda i, which: (i, 0))

    ticks = 2 * steps
    square = (2, width, width)
    keep, send, ends_mine, ends_send = pl.pallas_call(
        functools.partial(towers_kernel, lay, steps, rows),
        grid_spec=pltpu.PrefetchScalarGridSpec(
            num_scalar_prefetch=1,
            grid=(blocks,),
            in_specs=[
                spec_rows(block, width),
                spec_lanes(2, steps, block),
                spec_lanes(2, steps, block),
                spec_lanes(steps, block),
                spec_whole(steps, rows),
                spec_whole(*packed_shape),
                spec_whole(*packed_shape),
            ],
            out_specs=[
                spec_whole(*packed_shape),
                spec_whole(*packed_shape),
                spec_out(block, width),
                spec_out(block, width),
            ],
            scratch_shapes=[
                pltpu.VMEM(square, BF16),
                pltpu.VMEM(square, BF16),
                pltpu.VMEM(square, BF16),
                pltpu.VMEM((2, width, lay.wide), BF16),
                pltpu.VMEM((2, lay.codes, width), BF16),
                pltpu.VMEM((2, 2, width), F32),
                pltpu.VMEM(square, F32),
                pltpu.VMEM(square, F32),
                pltpu.VMEM(square, F32),
                pltpu.VMEM((2, width, lay.wide), F32),
                pltpu.VMEM((2, lay.codes, width), F32),
                pltpu.VMEM((2, 2, width), F32),
                pltpu.VMEM((steps, block, 8), jnp.int32),
                pltpu.VMEM((ticks + 1, block, width), BF16),
                pltpu.VMEM((ticks, block, width), F32),
                pltpu.VMEM((ticks, block, width), F32),
                pltpu.VMEM((ticks, block, width), F32),
                pltpu.VMEM((ticks, block, width), F32),
                pltpu.VMEM((ticks, block, width), BF16),
                pltpu.VMEM((ticks, block, 1), F32),
                pltpu.VMEM((ticks, block, 1), F32),
                pltpu.VMEM((block, width), BF16),
                pltpu.VMEM((block, width), F32),
            ],
        ),
        out_shape=[
            jax.ShapeDtypeStruct(packed_shape, F32),
            jax.ShapeDtypeStruct(packed_shape, BF16),
            jax.ShapeDtypeStruct((own_rows, width), F32),
            jax.ShapeDtypeStruct((own_rows, width), BF16),
        ],
        compiler_params=roomy,
        name="towers",
    )(section[None], latent, codes, targets, valid, valid, mine, theirs)

    total = reduce_all((keep + swap(send).astype(F32)).astype(BF16), length)
    other = swap(ends_send).astype(F32)
    ends = jnp.where(
        section == 0,
        jnp.concatenate([ends_mine, other]),
        jnp.concatenate([other, ends_mine]),
    )[None]
    news = [
        jax.ShapeDtypeStruct(weights[3 * at].shape, kind)
        for at in range(6)
        for kind in (F32, F32, F32, BF16)
    ]
    updated = pl.pallas_call(
        functools.partial(update_kernel, lay),
        out_shape=news,
        compiler_params=roomy,
        name="update",
    )(total, *weights)
    table_out, in_out, gain_out, up_out, down_out, head_out = (updated[4 * at : 4 * at + 4] for at in range(6))
    return (ends, *table_out, *in_out, *gain_out, *up_out, *down_out, *head_out)


def solution(mesh):
    by_section = P("section", None, None)
    in_specs = (P("dp", None), P(None, None, "dp"), P(None, None, "dp"), P(None, "dp")) + (by_section,) * 18
    out_specs = (P("section", "dp", None),) + (by_section,) * 24
    return jax.shard_map(
        functools.partial(on_device, 512, mesh.shape["dp"]),
        mesh=mesh,
        in_specs=in_specs,
        out_specs=out_specs,
        check_vma=False,
    )
```

time: 736 us -> 169 us (0.23); the launches traced: 727 us -> 168 us
  matrix products: 289 us -> 0 us
  local copies, waits for them, and re-layouts: 148 us -> 13.6 us
  other arithmetic: 133 us -> 4.86 us
  Pallas kernels: 0 us -> 103 us
  blocking collectives: 79.9 us -> 0 us
  loops' own time: 27.4 us -> 0 us
  between operations: 15.6 us -> 0.78 us
    dot_general x187 -> x0, matrix products: 289 us -> none  [the longest x22 61 us: tower_rear(): jnp.dot(active, down_low, preferred_element_type=jnp.float32)]
    pallas_call x0 -> x3, Pallas kernels: none -> 103 us  [the longest x1 95.8 us: on_device(): pl.pallas_call(functools.partial(towers_kernel, lay, steps, rows), grid_s...]
    dynamic_slice x99 -> x0, local copies, waits for them, and re-layouts: 83.7 us -> none  [the longest x22 20 us: on_device(): lax.scan(forward_tick, start_carry, tick_ids)]
    psum x1 -> x0, blocking collectives: 79.9 us -> none  [on_device(): lax.psum((table_total, in_total, gain_total, up_total, down_total, head_t...]
    reduce_sum x111 -> x0, other arithmetic: 77 us -> none  [the longest x33 44.5 us: layer_norm(): return centered * scale * gain]
    while x352 -> x0, local copies, waits for them, and re-layouts: 38.9 us -> none
    ppermute x22 -> x9, waiting for transfers between devices: 0.06 us -> 33.7 us  [the longest x6 31 us: across(): return lax.ppermute(array, 'dp', [(i, i ^ mask) for i in range(length)])]
    psum x1 -> x0, waiting for transfers between devices: 27.9 us -> none  [on_device(): lax.psum((table_total, in_total, gain_total, up_total, down_total, head_t...]
  transfers between devices with their start and end apart: 23 -> 9, of which waited for: 1 -> 8; matrix products, arithmetic and copies ran while one was open for 14% -> 4% of each run, Pallas kernels for 0% -> 0%
where the time goes in v1:
time: 169 us; the launch traced here: 168 us
  Pallas kernels  103 us (61%)
  waiting for transfers between devices  33.7 us (20%)
  local copies, waits for them, and re-layouts  13.6 us (8%)
  starting transfers between devices  12.2 us (7%)
  other arithmetic  4.86 us (3%)
    pallas_call x1, Pallas kernels, on_device(): pl.pallas_call(functools.partial(towers_kernel, lay, steps, rows), grid_s...  95.8 us
    ppermute x6, waiting for transfers between devices, across(): return lax.ppermute(array, 'dp', [(i, i ^ mask) for i in range(length)])  31 us
    unnamed x27, local copies, waits for them, and re-layouts  13.6 us
    ppermute x6, starting transfers between devices, across(): return lax.ppermute(array, 'dp', [(i, i ^ mask) for i in range(length)])  11.3 us
    pallas_call x1, Pallas kernels, on_device(): pl.pallas_call(functools.partial(update_kernel, lay), out_shape=news, com...  5.09 us
  transfers between devices with their start and end apart: 9, of which 8 were waited for; matrix products, arithmetic and copies ran while one was open for 4% of the time, Pallas kernels for 0%

profile of v1, /device:TPU:0, one launch (start us, length us, event | category | flops | bytes accessed | tf_op | source)
XLA Modules:
  0.0 168.5 jit_solution(2344563185056978463)
XLA Ops:
  0.7 0.0 copy-start.6
  0.7 2.1 %copy.47.w_head.refs_15_ = f32[1,256,601]{2,1,0:T(8,128)} copy(f32[1,256,601]{1,0,2:T(1,128)} %param.41) | data formatting | bytes 1230848 | tf_op args[19]
  2.8 0.0 copy-start.7
  2.8 2.4 %pack.1.mine = bf16[1472,256]{1,0:T(8,128)(2,1)} custom-call(f32[1,32,256]{2,1,0:T(8,128)} %refs_0_.1, f32[1,256,256]{2,1,0:T(8,128)} %refs_3_.1, f32[1,256,256]{2,1,0:T(8,128)} %refs_9_.1, f32[1,256,256]{2,1,0:T(8,128)} %refs_12_.1, f32[1,256,601]{2,1,0:T(8,128)} %copy.47.w_head.refs_15_, f32[1,2,256]{2,1,0:T(2,128)} %refs_6_.1), custom_call_target="tpu_custom_call" | custom-call | tf_op jit(solution)/shard_map/pack/pallas_call | solution.py:329
  5.1 0.5 collective-permute-start
  5.6 0.0 copy-done.6
  5.6 0.7 copy.48.codes
  6.3 0.0 copy-done.7
  6.3 0.7 copy.49.targets
  7.0 0.7 collective-permute-done.theirs
  7.7 0.0 copy-start.1
  7.7 0.9 copy-done.1
  8.5 95.8 %towers.1 = (f32[1472,256]{1,0:T(8,128)}, bf16[1472,256]{1,0:T(8,128)(2,1)}, f32[1024,256]{1,0:T(8,128)}, bf16[1024,256]{1,0:T(8,128)(2,1)}) custom-call(s32[1]{0:T(128)} %bitcast.which, bf16[2048,256]{1,0:T(8,128)(2,1)} %latent.1, s32[2,5,2048]{2,1,0:T(8,128)} %copy.48.codes, s32[2,5,2048]{2,1,0:T(8,128)} %copy.49.targets, s32[5,2048]{1,0:T(8,128)} %whole_valid.1, ...), custom_call_target="tpu_custom_call" | custom-call | tf_op jit(solution)/shard_map/towers/pallas_call | solution.py:351
  104.3 0.4 collective-permute-start.2
  104.7 2.1 %collective-permute-done.2 = bf16[1472,256]{1,0:T(8,128)(2,1)S(1)} collective-permute-done((bf16[1472,256]{1,0:T(8,128)(2,1)}, bf16[1472,256]{1,0:T(8,128)(2,1)S(1)}, u32[]{:S(2)}, u32[]{:S(2)}) %collective-permute-start.2) | collective-permute-done | bytes 753696 | tf_op jit(solution)/shard_map/ppermute | solution.py:290
  106.8 1.5 add_convert_fusion
  108.4 2.9 %collective-permute-start.3 = (bf16[736,256]{1,0:T(8,128)(2,1)S(1)}, bf16[736,256]{1,0:T(8,128)(2,1)S(1)}, u32[]{:S(2)}, u32[]{:S(2)}) collective-permute-start(bf16[736,256]{1,0:T(8,128)(2,1)S(1)} %broadcast_select_fusion), channel_id=1, source_target_pairs={{0,1},{1,0},{2,3},{3,2},{4,5},{5,4},{6,7},{7,6},{8,9},{9,8},{10,11... | collective-permute-start | bytes 1130504 | tf_op jit(solution)/shard_map/ppermute | solution.py:298
  111.3 0.0 copy-start.8
  111.3 9.1 %collective-permute-done.3 = bf16[736,256]{1,0:T(8,128)(2,1)S(1)} collective-permute-done((bf16[736,256]{1,0:T(8,128)(2,1)S(1)}, bf16[736,256]{1,0:T(8,128)(2,1)S(1)}, u32[]{:S(2)}, u32[]{:S(2)}) %collective-permute-start.3) | collective-permute-done | bytes 376864 | tf_op jit(solution)/shard_map/ppermute | solution.py:298
  120.4 0.1 add_convert_fusion.1
  120.5 0.0 copy-start.3
  120.6 0.0 copy-start.4
  120.6 1.8 %collective-permute-start.4 = (bf16[368,256]{1,0:T(8,128)(2,1)S(1)}, bf16[368,256]{1,0:T(8,128)(2,1)S(1)}, u32[]{:S(2)}, u32[]{:S(2)}) collective-permute-start(bf16[368,256]{1,0:T(8,128)(2,1)S(1)} %broadcast_select_fusion.1), channel_id=1, source_target_pairs={{0,2},{1,3},{2,0},{3,1},{4,6},{5,7},{6,4},{7,5},{8,10},{9,11},{10,... | collective-permute-start | bytes 565256 | tf_op jit(solution)/shard_map/ppermute | solution.py:298
  122.4 4.5 %collective-permute-done.4 = bf16[368,256]{1,0:T(8,128)(2,1)S(1)} collective-permute-done((bf16[368,256]{1,0:T(8,128)(2,1)S(1)}, bf16[368,256]{1,0:T(8,128)(2,1)S(1)}, u32[]{:S(2)}, u32[]{:S(2)}) %collective-permute-start.4) | collective-permute-done | bytes 188448 | tf_op jit(solution)/shard_map/ppermute | solution.py:298
  126.9 0.1 add_convert_fusion.4
  127.0 1.6 collective-permute-start.5
  128.6 4.1 %collective-permute-done.5 = bf16[368,256]{1,0:T(8,128)(2,1)S(1)} collective-permute-done((bf16[368,256]{1,0:T(8,128)(2,1)S(1)}, bf16[368,256]{1,0:T(8,128)(2,1)S(1)}, u32[]{:S(2)}, u32[]{:S(2)}) %collective-permute-start.5) | collective-permute-done | bytes 188448 | tf_op jit(solution)/shard_map/ppermute | solution.py:298
  132.6 0.1 add_convert_fusion.3
  132.7 2.7 %collective-permute-start.6 = (bf16[368,256]{1,0:T(8,128)(2,1)S(1)}, bf16[368,256]{1,0:T(8,128)(2,1)S(1)}, u32[]{:S(2)}, u32[]{:S(2)}) collective-permute-start(bf16[368,256]{1,0:T(8,128)(2,1)S(1)} %add_convert_fusion.3), channel_id=1, source_target_pairs={{0,8},{1,9},{2,10},{3,11},{4,12},{5,13},{6,14},{7,15},{8,0},{9,1},... | collective-permute-start | bytes 565256 | tf_op jit(solution)/shard_map/ppermute | solution.py:298
  135.4 0.0 copy-done.8
  135.4 0.0 collective-permute-start.1
  135.4 6.5 %collective-permute-done.6 = bf16[368,256]{1,0:T(8,128)(2,1)S(1)} collective-permute-done((bf16[368,256]{1,0:T(8,128)(2,1)S(1)}, bf16[368,256]{1,0:T(8,128)(2,1)S(1)}, u32[]{:S(2)}, u32[]{:S(2)}) %collective-permute-start.6) | collective-permute-done | bytes 188448 | tf_op jit(solution)/shard_map/ppermute | solution.py:298
  141.9 0.1 add_convert_fusion.2
  142.0 1.2 collective-permute-start.7
  143.1 0.0 copy-done.3
  143.1 1.5 copy.51.refs_16_
  144.7 0.0 copy-done.4
  144.7 0.0 copy-start
  144.7 1.5 copy.52.refs_17_
  146.2 1.4 collective-permute-done.7
  147.6 0.1 maximum_select_fusion.2
  147.8 1.1 collective-permute-start.8
  148.9 0.0 collective-permute-done.1
  148.9 0.1 bitcast_convert_fusion
  149.0 0.0 copy-done
  149.0 1.6 maximum_select_fusion
  150.6 5.4 %collective-permute-done.8 = bf16[736,256]{1,0:T(8,128)(2,1)S(1)} collective-permute-done((bf16[736,256]{1,0:T(8,128)(2,1)S(1)}, bf16[736,256]{1,0:T(8,128)(2,1)S(1)}, u32[]{:S(2)}, u32[]{:S(2)}) %collective-permute-start.8) | collective-permute-done | bytes 376864 | tf_op jit(solution)/shard_map/ppermute | solution.py:298
  156.0 1.1 maximum_select_fusion.1.total
  157.2 5.1 %update.1 = (f32[1,32,256]{2,1,0:T(8,128)}, f32[1,32,256]{2,1,0:T(8,128)}, f32[1,32,256]{2,1,0:T(8,128)}, bf16[1,32,256]{2,1,0:T(8,128)(2,1)}, f32[1,256,256]{2,...) custom-call(bf16[1472,256]{1,0:T(8,128)(2,1)} %maximum_select_fusion, ...), custom_call_target="tpu_custom_call" | custom-call | tf_op jit(solution)/shard_map/update/pallas_call | solution.py:419
  162.3 0.0 copy-start.2
  162.3 2.1 %copy.53 = f32[1,256,601]{1,0,2:T(1,128)} copy(f32[1,256,601]{2,1,0:T(8,128)} %get-tuple-element.102) | data formatting | bytes 1230848
  164.4 0.0 copy-start.5
  164.4 2.1 %copy.54 = f32[1,256,601]{1,0,2:T(1,128)} copy(f32[1,256,601]{2,1,0:T(8,128)} %get-tuple-element.103) | data formatting | bytes 1230848
  166.4 0.0 copy-done.2
  166.4 1.1 copy.55
  167.6 0.0 copy-done.5
  167.6 0.9 copy.56
  (2 shorter events, 0.1 us)
Async XLA Ops:
  0.7 4.9 %copy-start.6 = (s32[2,5,2048]{2,0,1:T(2,128)S(1)}, s32[2,5,2048]{2,0,1:T(2,128)}, u32[]{:S(2)}) copy-start(s32[2,5,2048]{2,0,1:T(2,128)} %param.23) | copy-start | bytes 245764
  2.8 3.5 %copy-start.7 = (s32[2,5,2048]{2,0,1:T(2,128)S(1)}, s32[2,5,2048]{2,0,1:T(2,128)}, u32[]{:S(2)}) copy-start(s32[2,5,2048]{2,0,1:T(2,128)} %param.24) | copy-start | bytes 245764
  5.1 2.5 %collective-permute-start = (bf16[1472,256]{1,0:T(8,128)(2,1)}, bf16[1472,256]{1,0:T(8,128)(2,1)S(1)}, u32[]{:S(2)}, u32[]{:S(2)}) collective-permute-start(bf16[1472,256]{1,0:T(8,128)(2,1)} %pack.1.mine), channel_id=1, source_target_pairs={{0,16},{16,0},{1,17},{17,1},{2,18},{18,2},{3,19},{19,3},{4,20},{20... | collective-permute-start | bytes 2261000 | tf_op jit(solution)/shard_map/ppermute | solution.py:290
  7.7 0.9 copy-start.1
  104.3 2.5 %collective-permute-start.2 = (bf16[1472,256]{1,0:T(8,128)(2,1)}, bf16[1472,256]{1,0:T(8,128)(2,1)S(1)}, u32[]{:S(2)}, u32[]{:S(2)}) collective-permute-start(bf16[1472,256]{1,0:T(8,128)(2,1)} %get-tuple-element.56), channel_id=1, source_target_pairs={{0,16},{16,0},{1,17},{17,1},{2,18},{18,2},{3,19},{19,3},{4,20},{20... | collective-permute-start | bytes 2261000 | tf_op jit(solution)/shard_map/ppermute | solution.py:290
  108.4 12.0 %collective-permute-start.3 = (bf16[736,256]{1,0:T(8,128)(2,1)S(1)}, bf16[736,256]{1,0:T(8,128)(2,1)S(1)}, u32[]{:S(2)}, u32[]{:S(2)}) collective-permute-start(bf16[736,256]{1,0:T(8,128)(2,1)S(1)} %broadcast_select_fusion), channel_id=1, source_target_pairs={{0,1},{1,0},{2,3},{3,2},{4,5},{5,4},{6,7},{7,6},{8,9},{9,8},{10,11... | collective-permute-start | bytes 1130504 | tf_op jit(solution)/shard_map/ppermute | solution.py:298
  111.3 24.0 %copy-start.8 = (bf16[1024,256]{1,0:T(8,128)(2,1)S(1)}, bf16[1024,256]{1,0:T(8,128)(2,1)}, u32[]{:S(2)}) copy-start(bf16[1024,256]{1,0:T(8,128)(2,1)} %get-tuple-element.54) | copy-start | bytes 1572868
  120.5 22.6 %copy-start.3 = (f32[1,256,601]{1,0,2:T(1,128)S(1)}, f32[1,256,601]{1,0,2:T(1,128)}, u32[]{:S(2)}) copy-start(f32[1,256,601]{1,0,2:T(1,128)} %param.42) | copy-start | bytes 1846276
  120.6 24.1 %copy-start.4 = (f32[1,256,601]{1,0,2:T(1,128)S(1)}, f32[1,256,601]{1,0,2:T(1,128)}, u32[]{:S(2)}) copy-start(f32[1,256,601]{1,0,2:T(1,128)} %param.43) | copy-start | bytes 1846276
  120.6 6.3 %collective-permute-start.4 = (bf16[368,256]{1,0:T(8,128)(2,1)S(1)}, bf16[368,256]{1,0:T(8,128)(2,1)S(1)}, u32[]{:S(2)}, u32[]{:S(2)}) collective-permute-start(bf16[368,256]{1,0:T(8,128)(2,1)S(1)} %broadcast_select_fusion.1), channel_id=1, source_target_pairs={{0,2},{1,3},{2,0},{3,1},{4,6},{5,7},{6,4},{7,5},{8,10},{9,11},{10,... | collective-permute-start | bytes 565256 | tf_op jit(solution)/shard_map/ppermute | solution.py:298
  127.0 5.6 %collective-permute-start.5 = (bf16[368,256]{1,0:T(8,128)(2,1)S(1)}, bf16[368,256]{1,0:T(8,128)(2,1)S(1)}, u32[]{:S(2)}, u32[]{:S(2)}) collective-permute-start(bf16[368,256]{1,0:T(8,128)(2,1)S(1)} %add_convert_fusion.4), channel_id=1, source_target_pairs={{0,4},{1,5},{2,6},{3,7},{4,0},{5,1},{6,2},{7,3},{8,12},{9,13},{10,... | collective-permute-start | bytes 565256 | tf_op jit(solution)/shard_map/ppermute | solution.py:298
  132.7 9.2 %collective-permute-start.6 = (bf16[368,256]{1,0:T(8,128)(2,1)S(1)}, bf16[368,256]{1,0:T(8,128)(2,1)S(1)}, u32[]{:S(2)}, u32[]{:S(2)}) collective-permute-start(bf16[368,256]{1,0:T(8,128)(2,1)S(1)} %add_convert_fusion.3), channel_id=1, source_target_pairs={{0,8},{1,9},{2,10},{3,11},{4,12},{5,13},{6,14},{7,15},{8,0},{9,1},... | collective-permute-start | bytes 565256 | tf_op jit(solution)/shard_map/ppermute | solution.py:298
  135.4 13.5 %collective-permute-start.1 = (bf16[1024,256]{1,0:T(8,128)(2,1)S(1)}, bf16[1024,256]{1,0:T(8,128)(2,1)S(1)}, u32[]{:S(2)}, u32[]{:S(2)}) collective-permute-start(bf16[1024,256]{1,0:T(8,128)(2,1)S(1)} %copy-done.8), channel_id=1, source_target_pairs={{0,16},{16,0},{1,17},{17,1},{2,18},{18,2},{3,19},{19,3},{4,20},{20... | collective-permute-start | bytes 1572872 | tf_op jit(solution)/shard_map/ppermute | solution.py:290
  142.0 5.6 %collective-permute-start.7 = (bf16[368,256]{1,0:T(8,128)(2,1)S(1)}, bf16[368,256]{1,0:T(8,128)(2,1)S(1)}, u32[]{:S(2)}, u32[]{:S(2)}) collective-permute-start(bf16[368,256]{1,0:T(8,128)(2,1)S(1)} %add_convert_fusion.2), channel_id=1, source_target_pairs={{0,2},{1,3},{2,0},{3,1},{4,6},{5,7},{6,4},{7,5},{8,10},{9,11},{10,... | collective-permute-start | bytes 565256 | tf_op jit(solution)/shard_map/ppermute | solution.py:298
  144.7 4.3 %copy-start = (f32[1024,256]{1,0:T(8,128)S(1)}, f32[1024,256]{1,0:T(8,128)}, u32[]{:S(2)}) copy-start(f32[1024,256]{1,0:T(8,128)} %get-tuple-element.53) | copy-start | bytes 3145732
  147.8 8.3 %collective-permute-start.8 = (bf16[736,256]{1,0:T(8,128)(2,1)S(1)}, bf16[736,256]{1,0:T(8,128)(2,1)S(1)}, u32[]{:S(2)}, u32[]{:S(2)}) collective-permute-start(bf16[736,256]{1,0:T(8,128)(2,1)S(1)} %maximum_select_fusion.2), channel_id=1, source_target_pairs={{0,1},{1,0},{2,3},{3,2},{4,5},{5,4},{6,7},{7,6},{8,9},{9,8},{10,11... | collective-permute-start | bytes 1130504 | tf_op jit(solution)/shard_map/ppermute | solution.py:298
  162.3 4.2 %copy-start.2 = (f32[1,256,601]{2,1,0:T(8,128)S(1)}, f32[1,256,601]{2,1,0:T(8,128)}, u32[]{:S(2)}) copy-start(f32[1,256,601]{2,1,0:T(8,128)} %get-tuple-element.104) | copy-start | bytes 1846276
  164.4 3.2 %copy-start.5 = (bf16[1,256,601]{2,1,0:T(8,128)(2,1)S(1)}, bf16[1,256,601]{2,1,0:T(8,128)(2,1)}, u32[]{:S(2)}) copy-start(bf16[1,256,601]{2,1,0:T(8,128)(2,1)} %get-tuple-element.105) | copy-start | bytes 923140

commit v2 on v1

v2 whole, which is shorter than its diff:
```python
import functools

import jax
import jax.numpy as jnp
from jax import lax
from jax.experimental import pallas as pl
from jax.experimental.pallas import tpu as pltpu
from jax.sharding import PartitionSpec as P

EPS = 1e-05
MOMENTUM = 0.5
AVERAGE = 0.9
RATE = 0.2
GRAD_SCALE = 4.0
GELU_LINE = 0.7978845608028654
GELU_CUBE = 0.7978845608028654 * 0.044715

BF16 = jnp.bfloat16
F32 = jnp.float32
LANES = 128
TILE = 16
BITS = 24
VMEM = 60 * 1024 * 1024


def dot(left, right):
    return jnp.dot(left, right, preferred_element_type=F32)


def dot_right_t(left, right):
    return lax.dot_general(left, right, (((1,), (1,)), ((), ())), preferred_element_type=F32)


def dot_left_t(left, right):
    return lax.dot_general(left, right, (((0,), (0,)), ((), ())), preferred_element_type=F32)


def gelu_and_slope(value):
    square = value * value
    half = 0.5 + 0.5 * jnp.tanh(value * (GELU_LINE + GELU_CUBE * square))
    result = value * half
    return result, half + result * (1.0 - half) * (2 * GELU_LINE + (6 * GELU_CUBE) * square)


def normalise(value):
    part = 1.0 / value.shape[-1]
    centered = value - jnp.sum(value, axis=-1, keepdims=True) * part
    scale = lax.rsqrt(jnp.sum(centered * centered, axis=-1, keepdims=True) * part + EPS)
    return centered * scale, scale


class Layout:
    def __init__(self, codes, width, bins):
        self.codes, self.width, self.bins = codes, width, bins
        self.wide = -(-bins // LANES) * LANES
        spots, at = {}, 0
        for name, rows in (("in", width), ("up", width), ("down", width), ("head", bins), ("table", codes), ("tail", TILE)):
            spots[name] = (at, at + rows)
            at += -(-rows // TILE) * TILE
        self.spots = spots
        self.used = at
        self.rows = -(-at // (4 * TILE)) * (4 * TILE)


def split_three(value):
    high = value.astype(BF16)
    left = value - high.astype(F32)
    middle = left.astype(BF16)
    low = (left - middle.astype(F32)).astype(BF16)
    return high, middle, low


def pack_kernel(lay, table, w_in, w_up, w_down, w_head, gains, out):
    for name, ref in (("in", w_in), ("up", w_up), ("down", w_down), ("table", table)):
        low, high = lay.spots[name]
        out[low:high, :] = ref[0].astype(BF16)
    low, high = lay.spots["head"]
    above = lay.spots["table"][0]
    head = jnp.concatenate([w_head[:, 0, :], jnp.zeros((above - high, lay.width), F32)], axis=0)
    out[low:above, :] = head.astype(BF16)
    low, high = lay.spots["tail"]
    pieces = [piece.astype(F32) for piece in split_three(gains[0])]
    pieces.append(jnp.zeros((high - low - 6, lay.width), F32))
    out[low:high, :] = jnp.concatenate(pieces, axis=0).astype(BF16)
    if lay.rows > lay.used:
        out[lay.used :, :] = jnp.zeros((lay.rows - lay.used, lay.width), BF16)


def row_sum(value):
    return jnp.sum(value, axis=-1, keepdims=True)


def interleave(streams, matmul_delay=220, vector_delay=60):
    clock = {"M": 0.0, "V": 0.0}
    live = []
    for rank, stream in enumerate(streams):
        live.append([stream, rank, next(stream), 0.0])
    while live:
        best = min(live, key=lambda entry: (max(clock[entry[2][0]], entry[3]), entry[1]))
        unit, cost = best[2]
        begin = max(clock[unit], best[3])
        clock[unit] = begin + cost
        best[3] = begin + cost + (matmul_delay if unit == "M" else vector_delay)
        best[2] = next(best[0], None)
        if best[2] is None:
            live.remove(best)


def in_turn(*streams):
    for stream in streams:
        yield from stream


def towers_kernel(lay, steps, chunk, which, latent, codes, targets, valid, whole_valid, mine, theirs,
                  keep, send, ends_mine, ends_send,
                  w_cat, w_up, w_down, w_head, gains,
                  g_cat, g_up, g_down, g_head, g_gain,
                  meta, inputs, unit_one, slope_one, unit_two, slope_two, active, normed,
                  scale_one, scale_two, head_part, logit_grads, branch_grads, inner_grads, pre_grads,
                  back, final):
    rows, width = latent.shape
    wide = lay.wide
    part = 1.0 / width
    section = which[0]
    chunks = [slice(at, at + chunk) for at in range(0, rows, chunk)]
    weight_of = chunk / 8

    @pl.when(pl.program_id(0) == 0)
    def start():
        for ref in (g_cat, g_up, g_down, g_head, g_gain):
            ref[...] = jnp.zeros_like(ref)
        for packed, slot in ((mine, section), (theirs, 1 - section)):
            for name, ref in (("up", w_up), ("down", w_down)):
                low, high = lay.spots[name]
                ref[slot] = packed[low:high, :]
            low, high = lay.spots["in"]
            w_cat[slot, :width] = packed[low:high, :]
            low, high = lay.spots["table"]
            w_cat[slot, width : width + lay.codes] = packed[low:high, :]
            w_cat[slot, width + lay.codes :] = jnp.zeros((LANES - lay.codes, width), BF16)
            low = lay.spots["head"][0]
            high = lay.spots["table"][0]
            w_head[slot, : high - low] = packed[low:high, :]
            w_head[slot, high - low :] = jnp.zeros((wide - high + low, width), BF16)
            low, high = lay.spots["tail"]
            tail = packed[low:high, :].astype(F32)
            gains[slot] = tail[0:2] + tail[2:4] + tail[4:6]

    lane = lax.broadcasted_iota(jnp.int32, (rows, LANES), 1)
    for step in range(steps):
        alive = valid[step : step + 1, :]
        line = [codes[step, tower : tower + 1, :] for tower in range(2)]
        line += [jnp.where(alive > 0, targets[step, tower : tower + 1, :], -1) for tower in range(2)]
        columns = jnp.concatenate(line + [jnp.zeros((4, rows), jnp.int32)], axis=0).T
        meta[step] = columns
        for tower in range(2):
            inputs[2 * step + tower, :, width:] = (columns[:, tower : tower + 1] == lane).astype(F32).astype(BF16)
    inputs[0, :, :width] = latent[...]

    def forward(step, tower):
        at = 2 * step + tower
        yield "M", rows / 2
        pre = dot(inputs[at], w_cat[tower])
        for where in chunks:
            yield "V", 8 * weight_of
            unit, scale = normalise(pre[where])
            unit_one[at, where, :] = unit
            scale_one[at, where, :] = jnp.broadcast_to(scale, (chunk, LANES))
            hidden, slope = gelu_and_slope(unit * gains[tower, 0:1, :])
            slope_one[at, where, :] = slope
            head_part[at, where, :] = hidden
            unit, scale = normalise(hidden)
            unit_two[at, where, :] = unit
            scale_two[at, where, :] = jnp.broadcast_to(scale, (chunk, LANES))
            normed[at, where, :] = (unit * gains[tower, 1:2, :]).astype(BF16)
        yield "M", rows / 4
        inner = dot(normed[at], w_up[tower])
        for where in chunks:
            yield "V", 4 * weight_of
            result, slope = gelu_and_slope(inner[where])
            slope_two[at, where, :] = slope
            active[at, where, :] = result.astype(BF16)
        yield "M", rows / 4
        branch = dot(active[at], w_down[tower])
        for where in chunks:
            yield "V", weight_of
            state = head_part[at, where, :] + branch[where]
            inputs[at + 1, where, :width] = state.astype(BF16)
            final[where, :] = state

    column = lax.broadcasted_iota(jnp.int32, (1, wide), 1)
    whole_lanes = wide - LANES
    inside = lax.broadcasted_iota(jnp.int32, (1, LANES), 1) < lay.bins - whole_lanes

    def head(step, tower):
        at = 2 * step + tower
        yield "M", 5 * rows / 8
        logits = dot_right_t(inputs[at + 1, :, :width], w_head[tower])
        for where in chunks:
            yield "V", 6 * weight_of
            some = logits[where]
            some = jnp.concatenate(
                [some[:, :whole_lanes], jnp.where(inside, some[:, whole_lanes:], -1e30)], axis=1
            )
            goal = meta[step, where, 2 + tower : 3 + tower]
            raised = jnp.exp(some - jnp.max(some, axis=-1, keepdims=True))
            ratio = jnp.where(goal >= 0, 1.0, 0.0) / row_sum(raised)
            logit_grads[tower, where, :] = (raised * ratio - jnp.where(column == goal, 1.0, 0.0)).astype(BF16)
        yield "M", 5 * rows / 8
        pulled = dot(logit_grads[tower], w_head[tower])
        for where in chunks:
            yield "V", weight_of
            head_part[at, where, :] = pulled[where]
        for low in range(0, wide, width):
            high = min(low + width, wide)
            yield "M", rows / 4 + 20
            some = dot_left_t(inputs[at + 1, :, :width], logit_grads[tower, :, low:high])
            yield "V", 32
            g_head[tower, :, low:high] += some

    def forward_step(step, carry):
        interleave([
            in_turn(forward(step, 0), forward(step, 1)),
            in_turn(head(step - 1, 0), head(step - 1, 1)),
        ])
        return carry

    interleave([in_turn(forward(0, 0), forward(0, 1))])
    lax.fori_loop(1, steps, forward_step, 0)
    interleave([head(steps - 1, 0), head(steps - 1, 1)])

    def both(value):
        return jnp.concatenate([value] * (width // LANES), axis=1)

    def backward(step, tower):
        at = 2 * step + tower
        for where in chunks:
            yield "V", 1.5 * weight_of
            state_grad = head_part[at, where, :] + back[where, :].astype(F32)
            head_part[at, where, :] = state_grad
            branch_grads[tower, where, :] = state_grad.astype(BF16)
        yield "M", rows / 4
        active_grad = dot_right_t(branch_grads[tower], w_down[tower])
        for where in chunks:
            yield "V", 1.5 * weight_of
            inner_grads[tower, where, :] = (active_grad[where] * slope_two[at, where, :]).astype(BF16)
        yield "M", rows / 4
        normed_grad = dot_right_t(inner_grads[tower], w_up[tower])
        for where in chunks:
            yield "V", 6 * weight_of
            unit = unit_two[at, where, :]
            scaled = normed_grad[where] * gains[tower, 1:2, :]
            first = row_sum(scaled) * part
            second = row_sum(scaled * unit) * part
            hidden_grad = head_part[at, where, :] + (scaled - first - unit * second) * both(scale_two[at, where, :])
            out_grad = hidden_grad * slope_one[at, where, :]
            unit = unit_one[at, where, :]
            product = out_grad * unit
            g_gain[tower] += jnp.sum(product.reshape(chunk // 8, 8, width), axis=0)
            gain = gains[tower, 0:1, :]
            scaled = out_grad * gain
            first = row_sum(scaled) * part
            second = row_sum(product * gain) * part
            pre_grads[tower, where, :] = (
                (scaled - first - unit * second) * both(scale_one[at, where, :])
            ).astype(BF16)
        yield "M", rows / 4
        input_grad = dot_right_t(pre_grads[tower], w_cat[tower, :width])
        for where in chunks:
            yield "V", 0.5 * weight_of
            back[where, :] = input_grad[where].astype(BF16)

    def weight_grads(step, tower):
        at = 2 * step + tower
        for left, right, total in (
            (active, branch_grads, g_down),
            (normed, inner_grads, g_up),
            (inputs, pre_grads, g_cat),
        ):
            size = left.shape[2] // LANES
            yield "M", size * (rows + 80) / 8
            some = dot_left_t(left[at], right[tower])
            yield "V", 16 * size
            total[tower] += some

    back[...] = jnp.zeros_like(back)
    for ref in (branch_grads, inner_grads, pre_grads):
        ref[0] = jnp.zeros((rows, width), BF16)

    def backward_step(turn, carry):
        step = steps - 1 - turn
        later = jnp.minimum(step + 1, steps - 1)
        interleave([backward(step, 1), weight_grads(later, 0)])
        interleave([backward(step, 0), weight_grads(step, 1)])
        return carry

    lax.fori_loop(0, steps, backward_step, 0)
    interleave([weight_grads(0, 0)])
    first = back[...].astype(F32)
    last = final[...]
    is_first = section == 0
    ends_mine[...] = jnp.where(is_first, first, last)
    ends_send[...] = jnp.where(is_first, last, first).astype(BF16)

    @pl.when(pl.program_id(0) == pl.num_programs(0) - 1)
    def finish():
        count = jnp.sum(whole_valid[...].astype(F32), axis=(0, 1), keepdims=True).astype(jnp.int32)
        spot = lax.broadcasted_iota(jnp.int32, (1, width), 1)
        bits = jnp.where(spot < BITS, (count >> jnp.minimum(spot, BITS)) & 1, 0).astype(F32)
        for packed, slot in ((keep, section), (send, 1 - section)):
            kind = packed.dtype
            for name, value in (
                ("in", g_cat[slot, :width]),
                ("up", g_up[slot]),
                ("down", g_down[slot]),
                ("table", g_cat[slot, width : width + lay.codes]),
            ):
                low, high = lay.spots[name]
                packed[low:high, :] = value.astype(kind)
            low = lay.spots["head"][0]
            high = lay.spots["table"][0]
            packed[low:high, :] = g_head[slot].T[: high - low].astype(kind)
            in_gain = jnp.sum(g_gain[slot], axis=0, keepdims=True)
            pulled = jnp.sum((w_up[slot].astype(F32) * g_up[slot]).T, axis=0, keepdims=True)
            block_gain = pulled / gains[slot, 1:2, :]
            low, high = lay.spots["tail"]
            own = bits if packed is keep else jnp.zeros_like(bits)
            tail = jnp.concatenate([in_gain, block_gain, own, jnp.zeros((high - low - 3, width), F32)], axis=0)
            packed[low:high, :] = tail.astype(kind)
            if lay.rows > lay.used:
                packed[lay.used :, :] = jnp.zeros((lay.rows - lay.used, width), kind)


def combine_kernel(parts, which, keep, received, *outs):
    rows = outs[0].shape[0]
    for turn, out in enumerate(outs):
        low = pl.multiple_of((which[0] ^ turn) * rows, TILE)
        value = keep[pl.ds(low, rows), :] + received[pl.ds(low, rows), :].astype(F32)
        out[...] = value.astype(out.dtype)


def update_kernel(lay, parts, which, *refs):
    pieces, ins, outs, total = refs[:parts], refs[parts : parts + 18], refs[parts + 18 : parts + 42], refs[-1]
    rows = pieces[0].shape[0]
    for turn, piece in enumerate(pieces):
        low = pl.multiple_of((which[0] ^ turn) * rows, TILE)
        total[pl.ds(low, rows), :] = piece[...]
    low, high = lay.spots["tail"]
    tail = total[low:high, :].astype(F32)
    lane = lax.broadcasted_iota(jnp.int32, (1, lay.width), 1)
    place = jnp.where(lane < BITS, (1 << jnp.minimum(lane, BITS)).astype(F32), 0.0)
    count = jnp.sum(tail[2:3] * place, axis=-1, keepdims=True)
    factor = GRAD_SCALE * lax.rsqrt(count)
    for at, name in enumerate(("table", "in", "gain", "up", "down", "head")):
        if name == "gain":
            grad = tail[0:2]
        else:
            low, high = lay.spots[name]
            grad = total[low:high, :].astype(F32)
        spot = (slice(None), 0) if name == "head" else (0,)
        weight, moment, average = ins[3 * at : 3 * at + 3]
        step_grad = grad * factor
        new_moment = MOMENTUM * moment[spot] + step_grad
        new_weight = weight[spot] - RATE * (step_grad + MOMENTUM * new_moment)
        out_moment, out_average, out_weight, out_copy = outs[4 * at : 4 * at + 4]
        out_moment[spot] = new_moment
        out_average[spot] = AVERAGE * average[spot] + (1.0 - AVERAGE) * new_weight
        out_weight[spot] = new_weight
        out_copy[0] = new_weight.astype(BF16)


def swap(value):
    return lax.ppermute(value, "section", [(0, 1), (1, 0)])


def across(array, mask, length):
    return lax.ppermute(array, "dp", [(i, i ^ mask) for i in range(length)])


def on_device(block, chunk, length, latent, codes, targets, valid, *weights):
    section = lax.axis_index("section").astype(jnp.int32)
    index = lax.axis_index("dp").astype(jnp.int32)
    rows, width = latent.shape
    steps = codes.shape[1]
    own_rows = rows // 2
    block = min(block, own_rows)
    blocks = own_rows // block
    bins = weights[15].shape[2]
    weights = weights[:15] + tuple(jnp.transpose(array, (2, 0, 1)) for array in weights[15:])
    codes, targets = jnp.swapaxes(codes, 0, 1), jnp.swapaxes(targets, 0, 1)
    table, w_in, gains, w_up, w_down, w_head = weights[0::3]
    lay = Layout(table.shape[1], width, bins)
    packed_shape = (lay.rows, width)
    roomy = pltpu.CompilerParams(vmem_limit_bytes=VMEM)
    mine = pl.pallas_call(
        functools.partial(pack_kernel, lay),
        out_shape=jax.ShapeDtypeStruct(packed_shape, BF16),
        compiler_params=roomy,
        name="pack",
    )(table, w_in, w_up, w_down, w_head, gains)
    theirs = swap(mine)

    def spec_rows(*shape):
        return pl.BlockSpec(shape, lambda i, which: (which[0] * blocks + i,) + (0,) * (len(shape) - 1))

    def spec_lanes(*shape):
        return pl.BlockSpec(shape, lambda i, which: (0,) * (len(shape) - 1) + (which[0] * blocks + i,))

    def spec_whole(*shape):
        return pl.BlockSpec(shape, lambda i, which: (0,) * len(shape))

    def spec_out(*shape):
        return pl.BlockSpec(shape, lambda i, which: (i, 0))

    ticks = 2 * steps
    square = (2, width, width)
    per_tick = (ticks, block, width)
    narrow = (ticks, block, LANES)
    pair = (2, block, width)
    keep, send, ends_mine, ends_send = pl.pallas_call(
        functools.partial(towers_kernel, lay, steps, chunk),
        grid_spec=pltpu.PrefetchScalarGridSpec(
            num_scalar_prefetch=1,
            grid=(blocks,),
            in_specs=[
                spec_rows(block, width),
                spec_lanes(steps, 2, block),
                spec_lanes(steps, 2, block),
                spec_lanes(steps, block),
                spec_whole(steps, rows),
                spec_whole(*packed_shape),
                spec_whole(*packed_shape),
            ],
            out_specs=[
                spec_whole(*packed_shape),
                spec_whole(*packed_shape),
                spec_out(block, width),
                spec_out(block, width),
            ],
            scratch_shapes=[
                pltpu.VMEM((2, width + LANES, width), BF16),
                pltpu.VMEM(square, BF16),
                pltpu.VMEM(square, BF16),
                pltpu.VMEM((2, lay.wide, width), BF16),
                pltpu.VMEM((2, 2, width), F32),
                pltpu.VMEM((2, width + LANES, width), F32),
                pltpu.VMEM(square, F32),
                pltpu.VMEM(square, F32),
                pltpu.VMEM((2, width, lay.wide), F32),
                pltpu.VMEM((2, 8, width), F32),
                pltpu.VMEM((steps, block, 8), jnp.int32),
                pltpu.VMEM((ticks + 1, block, width + LANES), BF16),
                pltpu.VMEM(per_tick, F32),
                pltpu.VMEM(per_tick, F32),
                pltpu.VMEM(per_tick, F32),
                pltpu.VMEM(per_tick, F32),
                pltpu.VMEM(per_tick, BF16),
                pltpu.VMEM(per_tick, BF16),
                pltpu.VMEM(narrow, F32),
                pltpu.VMEM(narrow, F32),
                pltpu.VMEM(per_tick, F32),
                pltpu.VMEM((2, block, lay.wide), BF16),
                pltpu.VMEM(pair, BF16),
                pltpu.VMEM(pair, BF16),
                pltpu.VMEM(pair, BF16),
                pltpu.VMEM((block, width), BF16),
                pltpu.VMEM((block, width), F32),
            ],
        ),
        out_shape=[
            jax.ShapeDtypeStruct(packed_shape, F32),
            jax.ShapeDtypeStruct(packed_shape, BF16),
            jax.ShapeDtypeStruct((own_rows, width), F32),
            jax.ShapeDtypeStruct((own_rows, width), BF16),
        ],
        compiler_params=roomy,
        name="towers",
    )(section[None], latent, codes, targets, valid, valid, mine, theirs)

    parts = min(4, length)
    place = (index % parts)[None]
    in_smem = pl.BlockSpec(memory_space=pltpu.SMEM)
    in_vmem = pl.BlockSpec(memory_space=pltpu.VMEM)
    part_shape = (lay.rows // parts, width)
    own, *others = pl.pallas_call(
        functools.partial(combine_kernel, parts),
        in_specs=[in_smem, in_vmem, in_vmem],
        out_shape=[jax.ShapeDtypeStruct(part_shape, F32)]
        + [jax.ShapeDtypeStruct(part_shape, BF16)] * (parts - 1),
        compiler_params=roomy,
        name="combine",
    )(place, keep, swap(send))
    current = own
    for arrived in [across(other, mask, length) for mask, other in enumerate(others, 1)]:
        current = current + arrived.astype(F32)
    current = current.astype(BF16)
    mask = parts
    while mask < length:
        current = (current.astype(F32) + across(current, mask, length).astype(F32)).astype(BF16)
        mask *= 2
    pieces = [current] + [across(current, mask, length) for mask in range(1, parts)]

    other = swap(ends_send).astype(F32)
    ends = jnp.where(
        section == 0,
        jnp.concatenate([ends_mine, other]),
        jnp.concatenate([other, ends_mine]),
    )[None]
    news = []
    for at in range(6):
        shape = weights[3 * at].shape
        news += [jax.ShapeDtypeStruct(shape, F32)] * 3
        news.append(jax.ShapeDtypeStruct((1, shape[0], width) if at == 5 else shape, BF16))
    updated = pl.pallas_call(
        functools.partial(update_kernel, lay, parts),
        in_specs=[in_smem] + [in_vmem] * (parts + 18),
        out_shape=news,
        scratch_shapes=[pltpu.VMEM(packed_shape, BF16)],
        compiler_params=roomy,
        name="update",
    )(place, *pieces, *weights)
    table_out, in_out, gain_out, up_out, down_out, head_out = (updated[4 * at : 4 * at + 4] for at in range(6))
    head_out = [jnp.transpose(array, (1, 2, 0)) for array in head_out[:3]] + [jnp.swapaxes(head_out[3], 1, 2)]
    return (ends, *table_out, *in_out, *gain_out, *up_out, *down_out, *head_out)


def solution(mesh):
    by_section = P("section", None, None)
    in_specs = (P("dp", None), P(None, None, "dp"), P(None, None, "dp"), P(None, "dp")) + (by_section,) * 18
    out_specs = (P("section", "dp", None),) + (by_section,) * 24
    return jax.shard_map(
        functools.partial(on_device, 512, 64, mesh.shape["dp"]),
        mesh=mesh,
        in_specs=in_specs,
        out_specs=out_specs,
        check_vma=False,
    )
```

time: 169 us -> 135 us (0.80)
  Pallas kernels: 103 us -> 85.3 us
  local copies, waits for them, and re-layouts: 13.6 us -> 2.5 us
  waiting for transfers between devices: 33.7 us -> 30 us
  other arithmetic: 4.86 us -> 2.83 us
    pallas_call x2 -> x3, Pallas kernels: 101 us -> 82.8 us  [the longest x1 73.9 us: on_device(): pl.pallas_call(functools.partial(towers_kernel, lay, steps, chunk), grid_...]
    unnamed x27 -> x16, local copies, waits for them, and re-layouts: 13.6 us -> 2.5 us
    ppermute x6 -> x8, waiting for transfers between devices: 31 us -> 25.8 us  [across(): return lax.ppermute(array, 'dp', [(i, i ^ mask) for i in range(length)])]
    ppermute x6 -> x8, starting transfers between devices: 11.3 us -> 12.2 us  [across(): return lax.ppermute(array, 'dp', [(i, i ^ mask) for i in range(length)])]
  transfers between devices with their start and end apart: 9 -> 11, of which waited for: 8 -> 8; matrix products, arithmetic and copies ran while one was open for 4% -> 2% of each run, Pallas kernels for 0% -> 0%
where the time goes in v2:
time: 135 us
  Pallas kernels  85.3 us (63%)
  waiting for transfers between devices  30 us (22%)
  starting transfers between devices  13.1 us (10%)
  other arithmetic  2.83 us (2%)
  local copies, waits for them, and re-layouts  2.5 us (2%)
    pallas_call x1, Pallas kernels, on_device(): pl.pallas_call(functools.partial(towers_kernel, lay, steps, chunk), grid_...  73.9 us
    ppermute x8, waiting for transfers between devices, across(): return lax.ppermute(array, 'dp', [(i, i ^ mask) for i in range(length)])  25.8 us
    ppermute x8, starting transfers between devices, across(): return lax.ppermute(array, 'dp', [(i, i ^ mask) for i in range(length)])  12.2 us
    pallas_call x1, Pallas kernels, on_device(): pl.pallas_call(functools.partial(update_kernel, lay, parts), in_specs=[in...  6.32 us
    ppermute x3, waiting for transfers between devices, swap(): return lax.ppermute(value, 'section', [(0, 1), (1, 0)])  4.15 us
  transfers between devices with their start and end apart: 11, of which 8 were waited for; matrix products, arithmetic and copies ran while one was open for 2% of the time, Pallas kernels for 0%

profile of v2, /device:TPU:0, one launch (start us, length us, event | category | flops | bytes accessed | tf_op | source)
XLA Modules:
  0.0 134.6 jit_solution(6172638870451430559)
XLA Ops:
  0.7 2.5 %pack.1.mine = bf16[1472,256]{1,0:T(8,128)(2,1)} custom-call(f32[1,32,256]{2,1,0:T(8,128)} %refs_4_.1, f32[1,256,256]{2,1,0:T(8,128)} %refs_7_.1, f32[1,256,256]{2,1,0:T(8,128)} %refs_13_.1, f32[1,256,256]{2,1,0:T(8,128)} %refs_16_.1, f32[601,1,256]{2,1,0:T(1,128)} %bitcast.15, f32[1,2,256]{2,1,0:T(2,128)} %refs_10_.1), custom_call_target="tpu_custom_call" | custom-call | tf_op jit(solution)/shard_map/pack/pallas_call | solution.py:395
  3.2 0.5 collective-permute-start
  3.6 2.1 %collective-permute-done.theirs = bf16[1472,256]{1,0:T(8,128)(2,1)S(1)} collective-permute-done((bf16[1472,256]{1,0:T(8,128)(2,1)}, bf16[1472,256]{1,0:T(8,128)(2,1)S(1)}, u32[]{:S(2)}, u32[]{:S(2)}) %collective-permute-start) | collective-permute-done | bytes 753696 | tf_op jit(solution)/shard_map/ppermute | solution.py:373
  5.7 0.0 copy-start.3
  5.7 0.9 copy-done.3
  6.5 73.9 %towers.1 = (f32[1472,256]{1,0:T(8,128)}, bf16[1472,256]{1,0:T(8,128)(2,1)}, f32[1024,256]{1,0:T(8,128)}, bf16[1024,256]{1,0:T(8,128)(2,1)}) custom-call(s32[1]{0:T(128)} %bitcast.which, bf16[2048,256]{1,0:T(8,128)(2,1)} %latent.1, s32[5,2,2048]{2,1,0:T(2,128)} %bitcast.20, s32[5,2,2048]{2,1,0:T(2,128)} %bitcast.21, s32[5,2048]{1,0:T(8,128)} %whole_valid.1, ...), custom_call_target="tpu_custom_call" | custom-call | tf_op jit(solution)/shard_map/towers/pallas_call | solution.py:420
  80.4 0.0 copy-start.7
  80.4 0.4 collective-permute-start.2
  80.9 2.1 %collective-permute-done.2.received = bf16[1472,256]{1,0:T(8,128)(2,1)S(1)} collective-permute-done((bf16[1472,256]{1,0:T(8,128)(2,1)}, bf16[1472,256]{1,0:T(8,128)(2,1)S(1)}, u32[]{:S(2)}, u32[]{:S(2)}) %collective-permute-start.2) | collective-permute-done | bytes 753696 | tf_op jit(solution)/shard_map/ppermute | solution.py:373
  83.0 0.0 copy-start.2
  83.0 0.9 copy-done.2
  83.8 2.6 %combine.1 = (f32[368,256]{1,0:T(8,128)}, bf16[368,256]{1,0:T(8,128)(2,1)}, bf16[368,256]{1,0:T(8,128)(2,1)}, bf16[368,256]{1,0:T(8,128)(2,1)}) custom-call(s32[1]{0:T(128)} %bitcast.7.which, f32[1472,256]{1,0:T(8,128)} %get-tuple-element.59.keep, bf16[1472,256]{1,0:T(8,128)(2,1)} %copy-done.2), custom_call_target="tpu_custom_call" | custom-call | tf_op jit(solution)/shard_map/combine/pallas_call | solution.py:485
  86.5 0.0 copy-start
  86.5 2.8 %collective-permute-start.3 = (bf16[368,256]{1,0:T(8,128)(2,1)}, bf16[368,256]{1,0:T(8,128)(2,1)S(1)}, u32[]{:S(2)}, u32[]{:S(2)}) collective-permute-start(bf16[368,256]{1,0:T(8,128)(2,1)} %get-tuple-element.62), channel_id=1, source_target_pairs={{0,1},{1,0},{2,3},{3,2},{4,5},{5,4},{6,7},{7,6},{8,9},{9,8},{10,11... | collective-permute-start | bytes 565256 | tf_op jit(solution)/shard_map/ppermute | solution.py:377
  89.3 1.5 %collective-permute-start.4 = (bf16[368,256]{1,0:T(8,128)(2,1)}, bf16[368,256]{1,0:T(8,128)(2,1)S(1)}, u32[]{:S(2)}, u32[]{:S(2)}) collective-permute-start(bf16[368,256]{1,0:T(8,128)(2,1)} %get-tuple-element.63), channel_id=1, source_target_pairs={{0,2},{1,3},{2,0},{3,1},{4,6},{5,7},{6,4},{7,5},{8,10},{9,11},{10,... | collective-permute-start | bytes 565256 | tf_op jit(solution)/shard_map/ppermute | solution.py:377
  90.8 0.0 collective-permute-start.5
  90.8 0.0 copy-done.7
  90.8 0.0 collective-permute-start.1
  90.9 4.2 %collective-permute-done.3 = bf16[368,256]{1,0:T(8,128)(2,1)S(1)} collective-permute-done((bf16[368,256]{1,0:T(8,128)(2,1)}, bf16[368,256]{1,0:T(8,128)(2,1)S(1)}, u32[]{:S(2)}, u32[]{:S(2)}) %collective-permute-start.3) | collective-permute-done | bytes 188448 | tf_op jit(solution)/shard_map/ppermute | solution.py:377
  95.0 5.0 %collective-permute-done.4 = bf16[368,256]{1,0:T(8,128)(2,1)S(1)} collective-permute-done((bf16[368,256]{1,0:T(8,128)(2,1)}, bf16[368,256]{1,0:T(8,128)(2,1)S(1)}, u32[]{:S(2)}, u32[]{:S(2)}) %collective-permute-start.4) | collective-permute-done | bytes 188448 | tf_op jit(solution)/shard_map/ppermute | solution.py:377
  100.1 0.0 collective-permute-done.5
  100.1 1.1 add_convert_fusion.2
  101.1 1.6 %collective-permute-start.6 = (bf16[368,256]{1,0:T(8,128)(2,1)S(1)}, bf16[368,256]{1,0:T(8,128)(2,1)S(1)}, u32[]{:S(2)}, u32[]{:S(2)}) collective-permute-start(bf16[368,256]{1,0:T(8,128)(2,1)S(1)} %add_convert_fusion.2), channel_id=1, source_target_pairs={{0,4},{1,5},{2,6},{3,7},{4,0},{5,1},{6,2},{7,3},{8,12},{9,13},{10,... | collective-permute-start | bytes 565256 | tf_op jit(solution)/shard_map/ppermute | solution.py:377
  102.8 4.1 %collective-permute-done.6 = bf16[368,256]{1,0:T(8,128)(2,1)S(1)} collective-permute-done((bf16[368,256]{1,0:T(8,128)(2,1)S(1)}, bf16[368,256]{1,0:T(8,128)(2,1)S(1)}, u32[]{:S(2)}, u32[]{:S(2)}) %collective-permute-start.6) | collective-permute-done | bytes 188448 | tf_op jit(solution)/shard_map/ppermute | solution.py:377
  106.9 0.1 add_convert_fusion.1
  107.0 2.7 %collective-permute-start.7 = (bf16[368,256]{1,0:T(8,128)(2,1)S(1)}, bf16[368,256]{1,0:T(8,128)(2,1)S(1)}, u32[]{:S(2)}, u32[]{:S(2)}) collective-permute-start(bf16[368,256]{1,0:T(8,128)(2,1)S(1)} %add_convert_fusion.1), channel_id=1, source_target_pairs={{0,8},{1,9},{2,10},{3,11},{4,12},{5,13},{6,14},{7,15},{8,0},{9,1},... | collective-permute-start | bytes 565256 | tf_op jit(solution)/shard_map/ppermute | solution.py:377
  109.6 0.0 collective-permute-done.1
  109.6 0.1 bitcast_convert_fusion
  109.7 7.1 %collective-permute-done.7 = bf16[368,256]{1,0:T(8,128)(2,1)S(1)} collective-permute-done((bf16[368,256]{1,0:T(8,128)(2,1)S(1)}, bf16[368,256]{1,0:T(8,128)(2,1)S(1)}, u32[]{:S(2)}, u32[]{:S(2)}) %collective-permute-start.7) | collective-permute-done | bytes 188448 | tf_op jit(solution)/shard_map/ppermute | solution.py:377
  116.8 0.1 add_convert_fusion.refs_0_
  116.8 0.0 copy-start.1
  116.9 1.5 %collective-permute-start.10 = (bf16[368,256]{1,0:T(8,128)(2,1)S(1)}, bf16[368,256]{1,0:T(8,128)(2,1)S(1)}, u32[]{:S(2)}, u32[]{:S(2)}) collective-permute-start(bf16[368,256]{1,0:T(8,128)(2,1)S(1)} %add_convert_fusion.refs_0_), channel_id=1, source_target_pairs={{0,3},{1,2},{2,1},{3,0},{4,7},{5,6},{6,5},{7,4},{8,11},{9,10},{10,... | collective-permute-start | bytes 565256 | tf_op jit(solution)/shard_map/ppermute | solution.py:377
  118.3 1.7 %collective-permute-start.9 = (bf16[368,256]{1,0:T(8,128)(2,1)S(1)}, bf16[368,256]{1,0:T(8,128)(2,1)S(1)}, u32[]{:S(2)}, u32[]{:S(2)}) collective-permute-start(bf16[368,256]{1,0:T(8,128)(2,1)S(1)} %add_convert_fusion.refs_0_), channel_id=1, source_target_pairs={{0,2},{1,3},{2,0},{3,1},{4,6},{5,7},{6,4},{7,5},{8,10},{9,11},{10,... | collective-permute-start | bytes 565256 | tf_op jit(solution)/shard_map/ppermute | solution.py:377
  120.1 0.4 collective-permute-start.8
  120.4 0.0 copy-done
  120.4 1.6 %maximum_select_fusion = f32[1,2048,256]{2,1,0:T(8,128)} fusion(f32[1,1024,256]{2,1,0:T(8,128)S(1)} %bitcast_convert_fusion, f32[1,1024,256]{2,1,0:T(8,128)S(1)} %bitcast.17, pred[]{:T(512)S(6)} %eq.5), kind=kLoop, calls=%fused_computation | loop fusion | flops 1572864 | bytes 4194305 | tf_op jit(solution)/shard_map/jit(_where)/select_n | solution.py:504
  122.0 0.0 copy-done.1
  122.0 3.5 %collective-permute-done.10.refs_3_ = bf16[368,256]{1,0:T(8,128)(2,1)S(1)} collective-permute-done((bf16[368,256]{1,0:T(8,128)(2,1)S(1)}, bf16[368,256]{1,0:T(8,128)(2,1)S(1)}, u32[]{:S(2)}, u32[]{:S(2)}) %collective-permute-start.10) | collective-permute-done | bytes 188448 | tf_op jit(solution)/shard_map/ppermute | solution.py:377
  125.4 0.0 copy-start.4
  125.4 2.0 %collective-permute-done.9.refs_2_ = bf16[368,256]{1,0:T(8,128)(2,1)S(1)} collective-permute-done((bf16[368,256]{1,0:T(8,128)(2,1)S(1)}, bf16[368,256]{1,0:T(8,128)(2,1)S(1)}, u32[]{:S(2)}, u32[]{:S(2)}) %collective-permute-start.9) | collective-permute-done | bytes 188448 | tf_op jit(solution)/shard_map/ppermute | solution.py:377
  127.4 0.0 copy-start.5
  127.4 0.0 collective-permute-done.8.refs_1_
  127.4 0.0 copy-start.6
  127.4 0.0 copy-done.4
  127.4 0.7 copy-done.5
  128.1 0.1 copy-done.6
  128.2 6.3 %update.1 = (f32[1,32,256]{2,1,0:T(8,128)}, f32[1,32,256]{2,1,0:T(8,128)}, f32[1,32,256]{2,1,0:T(8,128)}, bf16[1,32,256]{2,1,0:T(8,128)(2,1)}, f32[1,256,256]{2,...) custom-call(s32[1]{0:T(128)} %bitcast.7.which, ...), custom_call_target="tpu_custom_call" | custom-call | tf_op jit(solution)/shard_map/update/pallas_call | solution.py:514
Async XLA Ops:
  3.2 2.5 %collective-permute-start = (bf16[1472,256]{1,0:T(8,128)(2,1)}, bf16[1472,256]{1,0:T(8,128)(2,1)S(1)}, u32[]{:S(2)}, u32[]{:S(2)}) collective-permute-start(bf16[1472,256]{1,0:T(8,128)(2,1)} %pack.1.mine), channel_id=1, source_target_pairs={{0,16},{16,0},{1,17},{17,1},{2,18},{18,2},{3,19},{19,3},{4,20},{20... | collective-permute-start | bytes 2261000 | tf_op jit(solution)/shard_map/ppermute | solution.py:373
  5.7 0.9 copy-start.3
  80.4 10.4 %copy-start.7 = (bf16[1024,256]{1,0:T(8,128)(2,1)S(1)}, bf16[1024,256]{1,0:T(8,128)(2,1)}, u32[]{:S(2)}) copy-start(bf16[1024,256]{1,0:T(8,128)(2,1)} %get-tuple-element.58) | copy-start | bytes 1572868
  80.4 2.5 %collective-permute-start.2 = (bf16[1472,256]{1,0:T(8,128)(2,1)}, bf16[1472,256]{1,0:T(8,128)(2,1)S(1)}, u32[]{:S(2)}, u32[]{:S(2)}) collective-permute-start(bf16[1472,256]{1,0:T(8,128)(2,1)} %get-tuple-element.60), channel_id=1, source_target_pairs={{0,16},{16,0},{1,17},{17,1},{2,18},{18,2},{3,19},{19,3},{4,20},{20... | collective-permute-start | bytes 2261000 | tf_op jit(solution)/shard_map/ppermute | solution.py:373
  83.0 0.9 copy-start.2
  86.5 34.0 %copy-start = (f32[1024,256]{1,0:T(8,128)S(1)}, f32[1024,256]{1,0:T(8,128)}, u32[]{:S(2)}) copy-start(f32[1024,256]{1,0:T(8,128)} %get-tuple-element.57) | copy-start | bytes 3145732
  86.5 8.6 %collective-permute-start.3 = (bf16[368,256]{1,0:T(8,128)(2,1)}, bf16[368,256]{1,0:T(8,128)(2,1)S(1)}, u32[]{:S(2)}, u32[]{:S(2)}) collective-permute-start(bf16[368,256]{1,0:T(8,128)(2,1)} %get-tuple-element.62), channel_id=1, source_target_pairs={{0,1},{1,0},{2,3},{3,2},{4,5},{5,4},{6,7},{7,6},{8,9},{9,8},{10,11... | collective-permute-start | bytes 565256 | tf_op jit(solution)/shard_map/ppermute | solution.py:377
  89.3 10.7 %collective-permute-start.4 = (bf16[368,256]{1,0:T(8,128)(2,1)}, bf16[368,256]{1,0:T(8,128)(2,1)S(1)}, u32[]{:S(2)}, u32[]{:S(2)}) collective-permute-start(bf16[368,256]{1,0:T(8,128)(2,1)} %get-tuple-element.63), channel_id=1, source_target_pairs={{0,2},{1,3},{2,0},{3,1},{4,6},{5,7},{6,4},{7,5},{8,10},{9,11},{10,... | collective-permute-start | bytes 565256 | tf_op jit(solution)/shard_map/ppermute | solution.py:377
  90.8 9.2 %collective-permute-start.5 = (bf16[368,256]{1,0:T(8,128)(2,1)}, bf16[368,256]{1,0:T(8,128)(2,1)S(1)}, u32[]{:S(2)}, u32[]{:S(2)}) collective-permute-start(bf16[368,256]{1,0:T(8,128)(2,1)} %get-tuple-element.64), channel_id=1, source_target_pairs={{0,3},{1,2},{2,1},{3,0},{4,7},{5,6},{6,5},{7,4},{8,11},{9,10},{10,... | collective-permute-start | bytes 565256 | tf_op jit(solution)/shard_map/ppermute | solution.py:377
  90.8 18.8 %collective-permute-start.1 = (bf16[1024,256]{1,0:T(8,128)(2,1)S(1)}, bf16[1024,256]{1,0:T(8,128)(2,1)S(1)}, u32[]{:S(2)}, u32[]{:S(2)}) collective-permute-start(bf16[1024,256]{1,0:T(8,128)(2,1)S(1)} %copy-done.7), channel_id=1, source_target_pairs={{0,16},{16,0},{1,17},{17,1},{2,18},{18,2},{3,19},{19,3},{4,20},{20... | collective-permute-start | bytes 1572872 | tf_op jit(solution)/shard_map/ppermute | solution.py:373
  101.1 5.8 %collective-permute-start.6 = (bf16[368,256]{1,0:T(8,128)(2,1)S(1)}, bf16[368,256]{1,0:T(8,128)(2,1)S(1)}, u32[]{:S(2)}, u32[]{:S(2)}) collective-permute-start(bf16[368,256]{1,0:T(8,128)(2,1)S(1)} %add_convert_fusion.2), channel_id=1, source_target_pairs={{0,4},{1,5},{2,6},{3,7},{4,0},{5,1},{6,2},{7,3},{8,12},{9,13},{10,... | collective-permute-start | bytes 565256 | tf_op jit(solution)/shard_map/ppermute | solution.py:377
  107.0 9.8 %collective-permute-start.7 = (bf16[368,256]{1,0:T(8,128)(2,1)S(1)}, bf16[368,256]{1,0:T(8,128)(2,1)S(1)}, u32[]{:S(2)}, u32[]{:S(2)}) collective-permute-start(bf16[368,256]{1,0:T(8,128)(2,1)S(1)} %add_convert_fusion.1), channel_id=1, source_target_pairs={{0,8},{1,9},{2,10},{3,11},{4,12},{5,13},{6,14},{7,15},{8,0},{9,1},... | collective-permute-start | bytes 565256 | tf_op jit(solution)/shard_map/ppermute | solution.py:377
  116.8 5.1 %copy-start.1 = (bf16[368,256]{1,0:T(8,128)(2,1)}, bf16[368,256]{1,0:T(8,128)(2,1)S(1)}, u32[]{:S(2)}) copy-start(bf16[368,256]{1,0:T(8,128)(2,1)S(1)} %add_convert_fusion.refs_0_) | copy-start | bytes 565252
  116.9 8.6 %collective-permute-start.10 = (bf16[368,256]{1,0:T(8,128)(2,1)S(1)}, bf16[368,256]{1,0:T(8,128)(2,1)S(1)}, u32[]{:S(2)}, u32[]{:S(2)}) collective-permute-start(bf16[368,256]{1,0:T(8,128)(2,1)S(1)} %add_convert_fusion.refs_0_), channel_id=1, source_target_pairs={{0,3},{1,2},{2,1},{3,0},{4,7},{5,6},{6,5},{7,4},{8,11},{9,10},{10,... | collective-permute-start | bytes 565256 | tf_op jit(solution)/shard_map/ppermute | solution.py:377
  118.3 9.1 %collective-permute-start.9 = (bf16[368,256]{1,0:T(8,128)(2,1)S(1)}, bf16[368,256]{1,0:T(8,128)(2,1)S(1)}, u32[]{:S(2)}, u32[]{:S(2)}) collective-permute-start(bf16[368,256]{1,0:T(8,128)(2,1)S(1)} %add_convert_fusion.refs_0_), channel_id=1, source_target_pairs={{0,2},{1,3},{2,0},{3,1},{4,6},{5,7},{6,4},{7,5},{8,10},{9,11},{10,... | collective-permute-start | bytes 565256 | tf_op jit(solution)/shard_map/ppermute | solution.py:377
  120.1 7.4 %collective-permute-start.8 = (bf16[368,256]{1,0:T(8,128)(2,1)S(1)}, bf16[368,256]{1,0:T(8,128)(2,1)S(1)}, u32[]{:S(2)}, u32[]{:S(2)}) collective-permute-start(bf16[368,256]{1,0:T(8,128)(2,1)S(1)} %add_convert_fusion.refs_0_), channel_id=1, source_target_pairs={{0,1},{1,0},{2,3},{3,2},{4,5},{5,4},{6,7},{7,6},{8,9},{9,8},{10,11... | collective-permute-start | bytes 565256 | tf_op jit(solution)/shard_map/ppermute | solution.py:377
  125.4 2.0 %copy-start.4 = (bf16[368,256]{1,0:T(8,128)(2,1)}, bf16[368,256]{1,0:T(8,128)(2,1)S(1)}, u32[]{:S(2)}) copy-start(bf16[368,256]{1,0:T(8,128)(2,1)S(1)} %collective-permute-done.10.refs_3_) | copy-start | bytes 565252
  127.4 0.7 copy-start.5
  127.4 0.7 copy-start.6

commit v3 on v2

--- a/solution.py
+++ b/solution.py
@@ -20,7 +20,10 @@
 LANES = 128
 TILE = 16
 BITS = 24
-VMEM = 60 * 1024 * 1024
+FIRST, SECOND = 4, 4
+SPARE = 7
+STEPS = 4
+VMEM = 63 * 1024 * 1024
 
 
 def dot(left, right):
@@ -54,12 +57,20 @@
         self.codes, self.width, self.bins = codes, width, bins
         self.wide = -(-bins // LANES) * LANES
         spots, at = {}, 0
-        for name, rows in (("in", width), ("up", width), ("down", width), ("head", bins), ("table", codes), ("tail", TILE)):
-            spots[name] = (at, at + rows)
-            at += -(-rows // TILE) * TILE
+        sizes = (("in", width), ("up", width), ("down", width), ("head", bins + SPARE), ("table", codes))
+        for name, rows in sizes:
+            spots[name] = (at, at + -(-rows // TILE) * TILE)
+            at = spots[name][1]
+        spots["table"] = (spots["table"][0], spots["table"][0] + codes)
+        self.tail = spots["head"][0] + bins
         self.spots = spots
         self.used = at
-        self.rows = -(-at // (4 * TILE)) * (4 * TILE)
+        self.rows = -(-at // (8 * TILE)) * (8 * TILE)
+
+    def with_tail(self, head, *extra):
+        low, high = self.spots["head"]
+        left = high - low - self.bins - sum(rows.shape[0] for rows in extra)
+        return jnp.concatenate([head[: self.bins], *extra, jnp.zeros((left, self.width), F32)], axis=0)
 
 
 def split_three(value):
@@ -75,13 +86,8 @@
         low, high = lay.spots[name]
         out[low:high, :] = ref[0].astype(BF16)
     low, high = lay.spots["head"]
-    above = lay.spots["table"][0]
-    head = jnp.concatenate([w_head[:, 0, :], jnp.zeros((above - high, lay.width), F32)], axis=0)
-    out[low:above, :] = head.astype(BF16)
-    low, high = lay.spots["tail"]
     pieces = [piece.astype(F32) for piece in split_three(gains[0])]
-    pieces.append(jnp.zeros((high - low - 6, lay.width), F32))
-    out[low:high, :] = jnp.concatenate(pieces, axis=0).astype(BF16)
+    out[low:high, :] = lay.with_tail(w_head[:, 0, :], *pieces).astype(BF16)
     if lay.rows > lay.used:
         out[lay.used :, :] = jnp.zeros((lay.rows - lay.used, lay.width), BF16)
 
@@ -115,9 +121,10 @@
                   keep, send, ends_mine, ends_send,
                   w_cat, w_up, w_down, w_head, gains,
                   g_cat, g_up, g_down, g_head, g_gain,
-                  meta, inputs, unit_one, slope_one, unit_two, slope_two, active, normed,
-                  scale_one, scale_two, head_part, logit_grads, branch_grads, inner_grads, pre_grads,
-                  back, final):
+                  meta, picks, low_state, unit_one, slope_one, unit_two, slope_two, active_now, normed_now, active, normed,
+                  scale_one, scale_two, head_part, turned, turned_pick, logits_all, logit_grads, pre_grads, back):
+    branch_grads = tuple(low_state.at[slot, : latent.shape[0]] for slot in range(2))
+    inner_grads = (active_now, normed_now)
     rows, width = latent.shape
     wide = lay.wide
     part = 1.0 / width
@@ -138,15 +145,18 @@
             low, high = lay.spots["table"]
             w_cat[slot, width : width + lay.codes] = packed[low:high, :]
             w_cat[slot, width + lay.codes :] = jnp.zeros((LANES - lay.codes, width), BF16)
-            low = lay.spots["head"][0]
-            high = lay.spots["table"][0]
+            low, high = lay.spots["head"]
+            w_head[slot] = jnp.zeros((wide, width), BF16)
             w_head[slot, : high - low] = packed[low:high, :]
-            w_head[slot, high - low :] = jnp.zeros((wide - high + low, width), BF16)
-            low, high = lay.spots["tail"]
-            tail = packed[low:high, :].astype(F32)
-            gains[slot] = tail[0:2] + tail[2:4] + tail[4:6]
+            start_tail = (lay.tail - low) // TILE * TILE
+            block = packed[low + start_tail : high, :].astype(F32)
+            at = lay.tail - low - start_tail
+            gains[slot] = block[at : at + 2] + block[at + 2 : at + 4] + block[at + 4 : at + 6]
+            row = lax.broadcasted_iota(jnp.int32, block.shape, 0)
+            w_head[slot, start_tail : high - low] = jnp.where(row < at, block, 0.0).astype(BF16)
 
     lane = lax.broadcasted_iota(jnp.int32, (rows, LANES), 1)
+    upright = lax.broadcasted_iota(jnp.int32, (lay.codes, rows), 0)
     for step in range(steps):
         alive = valid[step : step + 1, :]
         line = [codes[step, tower : tower + 1, :] for tower in range(2)]
@@ -154,15 +164,17 @@
         columns = jnp.concatenate(line + [jnp.zeros((4, rows), jnp.int32)], axis=0).T
         meta[step] = columns
         for tower in range(2):
-            inputs[2 * step + tower, :, width:] = (columns[:, tower : tower + 1] == lane).astype(F32).astype(BF16)
-    inputs[0, :, :width] = latent[...]
+            turned_pick[2 * step + tower] = (line[tower] == upright).astype(F32).astype(BF16)
+            picks[2 * step + tower] = (columns[:, tower : tower + 1] == lane).astype(F32).astype(BF16)
+    low_state[0, :rows] = latent[...]
+    turned[0] = latent[...].T
 
     def forward(step, tower):
         at = 2 * step + tower
-        yield "M", rows / 2
-        pre = dot(inputs[at], w_cat[tower])
-        for where in chunks:
-            yield "V", 8 * weight_of
+        yield "m1"
+        pre = dot(jnp.concatenate([low_state[tower, :rows], picks[at]], axis=1), w_cat[tower])
+        for where in chunks:
+            yield "v1"
             unit, scale = normalise(pre[where])
             unit_one[at, where, :] = unit
             scale_one[at, where, :] = jnp.broadcast_to(scale, (chunk, LANES))
@@ -172,33 +184,49 @@
             unit, scale = normalise(hidden)
             unit_two[at, where, :] = unit
             scale_two[at, where, :] = jnp.broadcast_to(scale, (chunk, LANES))
-            normed[at, where, :] = (unit * gains[tower, 1:2, :]).astype(BF16)
-        yield "M", rows / 4
-        inner = dot(normed[at], w_up[tower])
-        for where in chunks:
-            yield "V", 4 * weight_of
+            normed_now[where, :] = (unit * gains[tower, 1:2, :]).astype(BF16)
+        yield "m2"
+        inner = dot(normed_now[...], w_up[tower])
+        normed[at] = normed_now[...].T
+        for where in chunks:
+            yield "v2"
             result, slope = gelu_and_slope(inner[where])
             slope_two[at, where, :] = slope
-            active[at, where, :] = result.astype(BF16)
-        yield "M", rows / 4
-        branch = dot(active[at], w_down[tower])
-        for where in chunks:
-            yield "V", weight_of
+            active_now[where, :] = result.astype(BF16)
+        yield "m3"
+        branch = dot(active_now[...], w_down[tower])
+        active[at] = active_now[...].T
+        for where in chunks:
+            yield "v3"
             state = head_part[at, where, :] + branch[where]
-            inputs[at + 1, where, :width] = state.astype(BF16)
-            final[where, :] = state
+            low_state[1 - tower, where, :] = state.astype(BF16)
+            ends_mine[where, :] = state
+        yield "t"
+        turned[at + 1] = low_state[1 - tower, :rows].T
+
+    def hold_logits(tower, at, row):
+        spot = pl.multiple_of(rows + 8 * section, 8)
+        logits_all[tower, pl.ds(spot, 8), :LANES] = at[row : row + 8, :LANES].astype(F32)
+
+    def hold_low(ref, slot, at, row):
+        spot = pl.multiple_of(rows + TILE * section, TILE)
+        ref[slot, pl.ds(spot, TILE), :LANES] = at[row : row + TILE, :LANES].astype(BF16)
 
     column = lax.broadcasted_iota(jnp.int32, (1, wide), 1)
     whole_lanes = wide - LANES
     inside = lax.broadcasted_iota(jnp.int32, (1, LANES), 1) < lay.bins - whole_lanes
 
-    def head(step, tower):
-        at = 2 * step + tower
+    def head_logits(step, tower):
         yield "M", 5 * rows / 8
-        logits = dot_right_t(inputs[at + 1, :, :width], w_head[tower])
-        for where in chunks:
-            yield "V", 6 * weight_of
-            some = logits[where]
+        logits = dot_right_t(low_state[1 - tower, :rows], w_head[tower])
+        for where in chunks:
+            yield "V", weight_of
+            logits_all[tower, where, :] = logits[where]
+
+    def head_softmax(step, tower):
+        for where in chunks:
+            yield "V", 14 * weight_of
+            some = logits_all[tower, where, :]
             some = jnp.concatenate(
                 [some[:, :whole_lanes], jnp.where(inside, some[:, whole_lanes:], -1e30)], axis=1
             )
@@ -206,28 +234,82 @@
             raised = jnp.exp(some - jnp.max(some, axis=-1, keepdims=True))
             ratio = jnp.where(goal >= 0, 1.0, 0.0) / row_sum(raised)
             logit_grads[tower, where, :] = (raised * ratio - jnp.where(column == goal, 1.0, 0.0)).astype(BF16)
+
+    def head_products(step, tower):
+        at = 2 * step + tower
         yield "M", 5 * rows / 8
-        pulled = dot(logit_grads[tower], w_head[tower])
+        pulled = dot(logit_grads[tower, :rows], w_head[tower])
         for where in chunks:
             yield "V", weight_of
             head_part[at, where, :] = pulled[where]
-        for low in range(0, wide, width):
-            high = min(low + width, wide)
-            yield "M", rows / 4 + 20
-            some = dot_left_t(inputs[at + 1, :, :width], logit_grads[tower, :, low:high])
-            yield "V", 32
-            g_head[tower, :, low:high] += some
+        yield "M", 5 * rows / 8
+        some = dot(turned[at + 1], logit_grads[tower, :rows])
+        yield "V", 80
+        g_head[tower] += some
+
+    def tick(step, tower, stages="flsp"):
+        at = 2 * step + tower
+        count = len(chunks)
+        streams = {}
+        if "f" in stages:
+            streams["f"] = forward(step, tower)
+        if "s" in stages:
+            streams["s"] = head_softmax(step - 1, tower)
+        if "l" in stages:
+            streams["l"] = head_logits(step - 1 + tower, 1 - tower)
+        if "p" in stages:
+            streams["p"] = head_products(step - 2 + tower, 1 - tower)
+        for stream in streams.values():
+            next(stream)
+
+        def go(name, pieces=1):
+            for _ in range(pieces):
+                if name in streams:
+                    next(streams[name], None)
+
+        if "f" not in stages:
+            for name in "spl":
+                go(name, 100)
+            return
+        first, second = FIRST, SECOND
+        go("f")
+        go("s", first)
+        go("f")
+        if "p" in stages:
+            hold_low(logit_grads, 1 - tower, unit_one.at[at], 0)
+        if "l" in stages:
+            hold_low(low_state, tower, unit_one.at[at], 0)
+        for turn in range(1, count):
+            go("f")
+            if turn % 2 == 1:
+                go("p")
+                go("l")
+        go("p", 100)
+        go("l", 100)
+        if "s" in stages:
+            hold_logits(tower, unit_two.at[at], rows - 8)
+        go("f")
+        go("s", second)
+        go("f", count)
+        if "s" in stages:
+            hold_logits(tower, slope_two.at[at], rows - 8)
+        go("f")
+        go("s", 100)
+        go("f", 100)
 
     def forward_step(step, carry):
-        interleave([
-            in_turn(forward(step, 0), forward(step, 1)),
-            in_turn(head(step - 1, 0), head(step - 1, 1)),
-        ])
+        tick(step, 0)
+        tick(step, 1)
         return carry
 
-    interleave([in_turn(forward(0, 0), forward(0, 1))])
-    lax.fori_loop(1, steps, forward_step, 0)
-    interleave([head(steps - 1, 0), head(steps - 1, 1)])
+    tick(0, 0, "f")
+    tick(0, 1, "fl")
+    tick(1, 0, "fls")
+    tick(1, 1)
+    lax.fori_loop(2, steps, forward_step, 0)
+    tick(steps, 0, "lsp")
+    tick(steps, 1, "sp")
+    tick(steps + 1, 0, "p")
 
     def both(value):
         return jnp.concatenate([value] * (width // LANES), axis=1)
@@ -235,19 +317,19 @@
     def backward(step, tower):
         at = 2 * step + tower
         for where in chunks:
-            yield "V", 1.5 * weight_of
+            yield "V", weight_of
             state_grad = head_part[at, where, :] + back[where, :].astype(F32)
             head_part[at, where, :] = state_grad
-            branch_grads[tower, where, :] = state_grad.astype(BF16)
+            branch_grads[tower][where, :] = state_grad.astype(BF16)
         yield "M", rows / 4
-        active_grad = dot_right_t(branch_grads[tower], w_down[tower])
-        for where in chunks:
-            yield "V", 1.5 * weight_of
-            inner_grads[tower, where, :] = (active_grad[where] * slope_two[at, where, :]).astype(BF16)
+        active_grad = dot_right_t(branch_grads[tower][...], w_down[tower])
+        for where in chunks:
+            yield "V", weight_of
+            inner_grads[tower][where, :] = (active_grad[where] * slope_two[at, where, :]).astype(BF16)
         yield "M", rows / 4
-        normed_grad = dot_right_t(inner_grads[tower], w_up[tower])
-        for where in chunks:
-            yield "V", 6 * weight_of
+        normed_grad = dot_right_t(inner_grads[tower][...], w_up[tower])
+        for where in chunks:
+            yield "V", 12.5 * weight_of
             unit = unit_two[at, where, :]
             scaled = normed_grad[where] * gains[tower, 1:2, :]
             first = row_sum(scaled) * part
@@ -272,20 +354,19 @@
 
     def weight_grads(step, tower):
         at = 2 * step + tower
-        for left, right, total in (
-            (active, branch_grads, g_down),
-            (normed, inner_grads, g_up),
-            (inputs, pre_grads, g_cat),
-        ):
-            size = left.shape[2] // LANES
-            yield "M", size * (rows + 80) / 8
-            some = dot_left_t(left[at], right[tower])
-            yield "V", 16 * size
+        for left, right, total in ((active, branch_grads, g_down), (normed, inner_grads, g_up)):
+            yield "M", rows / 4 + 20
+            some = dot(left[at], right[tower][...])
+            yield "V", 32
             total[tower] += some
+        yield "M", rows / 4 + 40
+        some = dot(jnp.concatenate([turned[at], turned_pick[at]], axis=0), pre_grads[tower])
+        yield "V", 36
+        g_cat[tower] += some
 
     back[...] = jnp.zeros_like(back)
-    for ref in (branch_grads, inner_grads, pre_grads):
-        ref[0] = jnp.zeros((rows, width), BF16)
+    for ref in (branch_grads[0], inner_grads[0], pre_grads.at[0]):
+        ref[...] = jnp.zeros((rows, width), BF16)
 
     def backward_step(turn, carry):
         step = steps - 1 - turn
@@ -297,7 +378,7 @@
     lax.fori_loop(0, steps, backward_step, 0)
     interleave([weight_grads(0, 0)])
     first = back[...].astype(F32)
-    last = final[...]
+    last = ends_mine[...]
     is_first = section == 0
     ends_mine[...] = jnp.where(is_first, first, last)
     ends_send[...] = jnp.where(is_first, last, first).astype(BF16)
@@ -317,16 +398,12 @@
             ):
                 low, high = lay.spots[name]
                 packed[low:high, :] = value.astype(kind)
-            low = lay.spots["head"][0]
-            high = lay.spots["table"][0]
-            packed[low:high, :] = g_head[slot].T[: high - low].astype(kind)
             in_gain = jnp.sum(g_gain[slot], axis=0, keepdims=True)
             pulled = jnp.sum((w_up[slot].astype(F32) * g_up[slot]).T, axis=0, keepdims=True)
             block_gain = pulled / gains[slot, 1:2, :]
-            low, high = lay.spots["tail"]
             own = bits if packed is keep else jnp.zeros_like(bits)
-            tail = jnp.concatenate([in_gain, block_gain, own, jnp.zeros((high - low - 3, width), F32)], axis=0)
-            packed[low:high, :] = tail.astype(kind)
+            low, high = lay.spots["head"]
+            packed[low:high, :] = lay.with_tail(g_head[slot].T, in_gain, block_gain, own).astype(kind)
             if lay.rows > lay.used:
                 packed[lay.used :, :] = jnp.zeros((lay.rows - lay.used, width), kind)
 
@@ -335,31 +412,18 @@
     rows = outs[0].shape[0]
     for turn, out in enumerate(outs):
         low = pl.multiple_of((which[0] ^ turn) * rows, TILE)
-        value = keep[pl.ds(low, rows), :] + received[pl.ds(low, rows), :].astype(F32)
+        value = keep[pl.ds(low, rows), :].astype(F32) + received[pl.ds(low, rows), :].astype(F32)
         out[...] = value.astype(out.dtype)
 
 
 def update_kernel(lay, parts, which, *refs):
-    pieces, ins, outs, total = refs[:parts], refs[parts : parts + 18], refs[parts + 18 : parts + 42], refs[-1]
-    rows = pieces[0].shape[0]
-    for turn, piece in enumerate(pieces):
-        low = pl.multiple_of((which[0] ^ turn) * rows, TILE)
-        total[pl.ds(low, rows), :] = piece[...]
-    low, high = lay.spots["tail"]
-    tail = total[low:high, :].astype(F32)
-    lane = lax.broadcasted_iota(jnp.int32, (1, lay.width), 1)
-    place = jnp.where(lane < BITS, (1 << jnp.minimum(lane, BITS)).astype(F32), 0.0)
-    count = jnp.sum(tail[2:3] * place, axis=-1, keepdims=True)
-    factor = GRAD_SCALE * lax.rsqrt(count)
-    for at, name in enumerate(("table", "in", "gain", "up", "down", "head")):
-        if name == "gain":
-            grad = tail[0:2]
-        else:
-            low, high = lay.spots[name]
-            grad = total[low:high, :].astype(F32)
-        spot = (slice(None), 0) if name == "head" else (0,)
+    pieces, ins, outs = refs[:parts], refs[parts : parts + 18], refs[parts + 18 : parts + 42]
+    total, scale = refs[-2:]
+    step = pl.program_id(0)
+
+    def new(at, spot, grad):
         weight, moment, average = ins[3 * at : 3 * at + 3]
-        step_grad = grad * factor
+        step_grad = grad.astype(F32) * scale[0:1, 0:1]
         new_moment = MOMENTUM * moment[spot] + step_grad
         new_weight = weight[spot] - RATE * (step_grad + MOMENTUM * new_moment)
         out_moment, out_average, out_weight, out_copy = outs[4 * at : 4 * at + 4]
@@ -367,6 +431,31 @@
         out_average[spot] = AVERAGE * average[spot] + (1.0 - AVERAGE) * new_weight
         out_weight[spot] = new_weight
         out_copy[0] = new_weight.astype(BF16)
+
+    @pl.when(step == 0)
+    def start():
+        rows = pieces[0].shape[0]
+        for turn, piece in enumerate(pieces):
+            low = pl.multiple_of((which[0] ^ turn) * rows, TILE)
+            total[pl.ds(low, rows), :] = piece[...]
+        low = lay.tail // TILE * TILE
+        high = lay.spots["head"][1]
+        tail = total[low:high, :].astype(F32)[lay.tail - low : lay.tail - low + 3]
+        lane = lax.broadcasted_iota(jnp.int32, (1, lay.width), 1)
+        place = jnp.where(lane < BITS, (1 << jnp.minimum(lane, BITS)).astype(F32), 0.0)
+        count = jnp.sum(tail[2:3] * place, axis=-1, keepdims=True)
+        scale[...] = jnp.broadcast_to(GRAD_SCALE * lax.rsqrt(count), scale.shape)
+        low, high = lay.spots["table"]
+        new(0, (0,), total[low:high, :])
+        new(2, (0,), tail[0:2])
+
+    for at, name in ((1, "in"), (3, "up"), (4, "down")):
+        rows = ins[3 * at].shape[1]
+        low = pl.multiple_of(lay.spots[name][0] + step * rows, TILE)
+        new(at, (0,), total[pl.ds(low, rows), :])
+    rows = ins[15].shape[0]
+    low = pl.multiple_of(lay.spots["head"][0] + step * rows, TILE)
+    new(5, (slice(None), 0), total[pl.ds(low, rows), :])
 
 
 def swap(value):
@@ -409,6 +498,9 @@
     def spec_whole(*shape):
         return pl.BlockSpec(shape, lambda i, which: (0,) * len(shape))
 
+    def spec_once(*shape):
+        return pl.BlockSpec(shape, lambda i, which: (0,) * len(shape), pipeline_mode=pl.Buffered(1))
+
     def spec_out(*shape):
         return pl.BlockSpec(shape, lambda i, which: (i, 0))
 
@@ -428,12 +520,12 @@
                 spec_lanes(steps, 2, block),
                 spec_lanes(steps, block),
                 spec_whole(steps, rows),
-                spec_whole(*packed_shape),
-                spec_whole(*packed_shape),
+                spec_once(*packed_shape),
+                spec_once(*packed_shape),
             ],
             out_specs=[
-                spec_whole(*packed_shape),
-                spec_whole(*packed_shape),
+                spec_once(*packed_shape),
+                spec_once(*packed_shape),
                 spec_out(block, width),
                 spec_out(block, width),
             ],
@@ -443,32 +535,35 @@
                 pltpu.VMEM(square, BF16),
                 pltpu.VMEM((2, lay.wide, width), BF16),
                 pltpu.VMEM((2, 2, width), F32),
-                pltpu.VMEM((2, width + LANES, width), F32),
+                pltpu.VMEM((2, width + lay.codes, width), F32),
                 pltpu.VMEM(square, F32),
                 pltpu.VMEM(square, F32),
                 pltpu.VMEM((2, width, lay.wide), F32),
                 pltpu.VMEM((2, 8, width), F32),
                 pltpu.VMEM((steps, block, 8), jnp.int32),
-                pltpu.VMEM((ticks + 1, block, width + LANES), BF16),
+                pltpu.VMEM((ticks, block, LANES), BF16),
+                pltpu.VMEM((2, block + 2 * TILE, width), BF16),
                 pltpu.VMEM(per_tick, F32),
                 pltpu.VMEM(per_tick, F32),
                 pltpu.VMEM(per_tick, F32),
                 pltpu.VMEM(per_tick, F32),
-                pltpu.VMEM(per_tick, BF16),
-                pltpu.VMEM(per_tick, BF16),
+                pltpu.VMEM((block, width), BF16),
+                pltpu.VMEM((block, width), BF16),
+                pltpu.VMEM((ticks, width, block), BF16),
+                pltpu.VMEM((ticks, width, block), BF16),
                 pltpu.VMEM(narrow, F32),
                 pltpu.VMEM(narrow, F32),
                 pltpu.VMEM(per_tick, F32),
-                pltpu.VMEM((2, block, lay.wide), BF16),
-                pltpu.VMEM(pair, BF16),
-                pltpu.VMEM(pair, BF16),
+                pltpu.VMEM((ticks + 1, width, block), BF16),
+                pltpu.VMEM((ticks, lay.codes, block), BF16),
+                pltpu.VMEM((2, block + TILE, lay.wide), F32),
+                pltpu.VMEM((2, block + 2 * TILE, lay.wide), BF16),
                 pltpu.VMEM(pair, BF16),
                 pltpu.VMEM((block, width), BF16),
-                pltpu.VMEM((block, width), F32),
             ],
         ),
         out_shape=[
-            jax.ShapeDtypeStruct(packed_shape, F32),
+            jax.ShapeDtypeStruct(packed_shape, BF16),
             jax.ShapeDtypeStruct(packed_shape, BF16),
             jax.ShapeDtypeStruct((own_rows, width), F32),
             jax.ShapeDtypeStruct((own_rows, width), BF16),
@@ -480,11 +575,14 @@
     parts = min(4, length)
     place = (index % parts)[None]
     in_smem = pl.BlockSpec(memory_space=pltpu.SMEM)
-    in_vmem = pl.BlockSpec(memory_space=pltpu.VMEM)
+
+    def spec_all(*shape):
+        return pl.BlockSpec(shape, lambda *_: (0,) * len(shape))
+
     part_shape = (lay.rows // parts, width)
     own, *others = pl.pallas_call(
         functools.partial(combine_kernel, parts),
-        in_specs=[in_smem, in_vmem, in_vmem],
+        in_specs=[in_smem, spec_all(*packed_shape), spec_all(*packed_shape)],
         out_shape=[jax.ShapeDtypeStruct(part_shape, F32)]
         + [jax.ShapeDtypeStruct(part_shape, BF16)] * (parts - 1),
         compiler_params=roomy,
@@ -494,10 +592,20 @@
     for arrived in [across(other, mask, length) for mask, other in enumerate(others, 1)]:
         current = current + arrived.astype(F32)
     current = current.astype(BF16)
-    mask = parts
-    while mask < length:
+    masks = [1 << bit for bit in range(length.bit_length() - 1)][parts.bit_length() - 1 :]
+    halved = masks[:1] if len(masks) > 1 else []
+    for mask in halved:
+        half = current.shape[0] // 2
+        upper = (index // mask) % 2 == 1
+        sent = jnp.where(upper, current[:half], current[half:])
+        kept = jnp.where(upper, current[half:], current[:half])
+        current = (kept.astype(F32) + across(sent, mask, length).astype(F32)).astype(BF16)
+    for mask in masks[len(halved) :]:
         current = (current.astype(F32) + across(current, mask, length).astype(F32)).astype(BF16)
-        mask *= 2
+    for mask in halved:
+        upper = (index // mask) % 2 == 1
+        found = across(current, mask, length)
+        current = jnp.where(upper, jnp.concatenate([found, current]), jnp.concatenate([current, found]))
     pieces = [current] + [across(current, mask, length) for mask in range(1, parts)]
 
     other = swap(ends_send).astype(F32)
@@ -506,16 +614,29 @@
         jnp.concatenate([ends_mine, other]),
         jnp.concatenate([other, ends_mine]),
     )[None]
-    news = []
+    head_rows = -(-bins // (STEPS * TILE)) * TILE
+    news, in_specs, out_specs = [], [], []
     for at in range(6):
         shape = weights[3 * at].shape
         news += [jax.ShapeDtypeStruct(shape, F32)] * 3
         news.append(jax.ShapeDtypeStruct((1, shape[0], width) if at == 5 else shape, BF16))
+        if at in (0, 2):
+            spec = copy_spec = spec_all(*shape)
+        elif at == 5:
+            spec = pl.BlockSpec((head_rows, 1, width), lambda i: (i, 0, 0))
+            copy_spec = pl.BlockSpec((1, head_rows, width), lambda i: (0, i, 0))
+        else:
+            spec = copy_spec = pl.BlockSpec((1, width // STEPS, width), lambda i: (0, i, 0))
+        in_specs += [spec] * 3
+        out_specs += [spec] * 3 + [copy_spec]
+    total_rows = max(lay.rows, lay.spots["head"][0] + STEPS * head_rows)
     updated = pl.pallas_call(
         functools.partial(update_kernel, lay, parts),
-        in_specs=[in_smem] + [in_vmem] * (parts + 18),
+        grid=(STEPS,),
+        in_specs=[in_smem] + [spec_all(*part_shape)] * parts + in_specs,
+        out_specs=out_specs,
         out_shape=news,
-        scratch_shapes=[pltpu.VMEM(packed_shape, BF16)],
+        scratch_shapes=[pltpu.VMEM((total_rows, width), BF16), pltpu.VMEM((8, LANES), F32)],
         compiler_params=roomy,
         name="update",
     )(place, *pieces, *weights)

time: 135 us -> 126 us (0.933)
  Pallas kernels: 85.3 us -> 79.9 us
  waiting for transfers between devices: 30 us -> 24.9 us
  starting transfers between devices: 13.1 us -> 14.8 us
    pallas_call x1, Pallas kernels: 73.9 us -> 68.7 us  [on_device(): pl.pallas_call(functools.partial(towers_kernel, lay, steps, chunk), grid_...]
    ppermute x8 -> x9, waiting for transfers between devices: 25.8 us -> 20.9 us  [across(): return lax.ppermute(array, 'dp', [(i, i ^ mask) for i in range(length)])]
    ppermute x8 -> x9, starting transfers between devices: 12.2 us -> 13.9 us  [across(): return lax.ppermute(array, 'dp', [(i, i ^ mask) for i in range(length)])]
  transfers between devices with their start and end apart: 11 -> 12, of which waited for: 8 -> 10; matrix products, arithmetic and copies ran while one was open for 2% -> 1% of each run, Pallas kernels for 0% -> 0%
where the time goes in v3:
time: 126 us
  Pallas kernels  79.9 us (63%)
  waiting for transfers between devices  24.9 us (20%)
  starting transfers between devices  14.8 us (12%)
  other arithmetic  2.84 us (2%)
  local copies, waits for them, and re-layouts  2.46 us (2%)
    pallas_call x1, Pallas kernels, on_device(): pl.pallas_call(functools.partial(towers_kernel, lay, steps, chunk), grid_...  68.7 us
    ppermute x9, waiting for transfers between devices, across(): return lax.ppermute(array, 'dp', [(i, i ^ mask) for i in range(length)])  20.9 us
    ppermute x9, starting transfers between devices, across(): return lax.ppermute(array, 'dp', [(i, i ^ mask) for i in range(length)])  13.9 us
    pallas_call x1, Pallas kernels, on_device(): pl.pallas_call(functools.partial(update_kernel, lay, parts), grid=(STEPS,...  6.44 us
    ppermute x3, waiting for transfers between devices, swap(): return lax.ppermute(value, 'section', [(0, 1), (1, 0)])  4.06 us
  transfers between devices with their start and end apart: 12, of which 10 were waited for; matrix products, arithmetic and copies ran while one was open for 1% of the time, Pallas kernels for 0%

profile of v3, /device:TPU:0, one launch (start us, length us, event | category | flops | bytes accessed | tf_op | source)
XLA Modules:
  0.0 125.8 jit_solution(15021051453156720343)
XLA Ops:
  0.7 2.4 %pack.1.mine = bf16[1408,256]{1,0:T(8,128)(2,1)} custom-call(f32[1,32,256]{2,1,0:T(8,128)} %refs_4_.1, f32[1,256,256]{2,1,0:T(8,128)} %refs_7_.1, f32[1,256,256]{2,1,0:T(8,128)} %refs_13_.1, f32[1,256,256]{2,1,0:T(8,128)} %refs_16_.1, f32[601,1,256]{2,1,0:T(1,128)} %bitcast.15, f32[1,2,256]{2,1,0:T(2,128)} %refs_10_.1), custom_call_target="tpu_custom_call" | custom-call | tf_op jit(solution)/shard_map/pack/pallas_call | solution.py:484
  3.1 0.5 collective-permute-start
  3.6 2.0 %collective-permute-done.theirs = bf16[1408,256]{1,0:T(8,128)(2,1)S(1)} collective-permute-done((bf16[1408,256]{1,0:T(8,128)(2,1)}, bf16[1408,256]{1,0:T(8,128)(2,1)S(1)}, u32[]{:S(2)}, u32[]{:S(2)}) %collective-permute-start) | collective-permute-done | bytes 720928 | tf_op jit(solution)/shard_map/ppermute | solution.py:462
  5.6 0.0 copy-start.3
  5.6 0.9 copy-done.3
  6.5 68.7 %towers.1 = (bf16[1408,256]{1,0:T(8,128)(2,1)}, bf16[1408,256]{1,0:T(8,128)(2,1)}, f32[1024,256]{1,0:T(8,128)}, bf16[1024,256]{1,0:T(8,128)(2,1)}) custom-call(s32[1]{0:T(128)} %bitcast.which, bf16[2048,256]{1,0:T(8,128)(2,1)} %latent.1, s32[5,2,2048]{2,1,0:T(2,128)} %bitcast.20, s32[5,2,2048]{2,1,0:T(2,128)} %bitcast.21, s32[5,2048]{1,0:T(8,128)} %whole_valid.1, ...), custom_call_target="tpu_custom_call" | custom-call | tf_op jit(solution)/shard_map/towers/pallas_call | solution.py:512
  75.2 0.4 collective-permute-start.2
  75.6 2.0 %collective-permute-done.2.received = bf16[1408,256]{1,0:T(8,128)(2,1)S(1)} collective-permute-done((bf16[1408,256]{1,0:T(8,128)(2,1)}, bf16[1408,256]{1,0:T(8,128)(2,1)S(1)}, u32[]{:S(2)}, u32[]{:S(2)}) %collective-permute-start.2) | collective-permute-done | bytes 720928 | tf_op jit(solution)/shard_map/ppermute | solution.py:462
  77.6 0.0 copy-start.2
  77.6 0.9 copy-done.2
  78.5 2.3 %combine.1 = (f32[352,256]{1,0:T(8,128)}, bf16[352,256]{1,0:T(8,128)(2,1)}, bf16[352,256]{1,0:T(8,128)(2,1)}, bf16[352,256]{1,0:T(8,128)(2,1)}) custom-call(s32[1]{0:T(128)} %bitcast.7.which, bf16[1408,256]{1,0:T(8,128)(2,1)} %get-tuple-element.59.keep, bf16[1408,256]{1,0:T(8,128)(2,1)} %copy-done.2), custom_call_target="tpu_custom_call" | custom-call | tf_op jit(solution)/shard_map/combine/pallas_call | solution.py:583
  80.9 0.0 copy-start
  80.9 2.8 %collective-permute-start.3 = (bf16[352,256]{1,0:T(8,128)(2,1)}, bf16[352,256]{1,0:T(8,128)(2,1)S(1)}, u32[]{:S(2)}, u32[]{:S(2)}) collective-permute-start(bf16[352,256]{1,0:T(8,128)(2,1)} %get-tuple-element.62), channel_id=1, source_target_pairs={{0,1},{1,0},{2,3},{3,2},{4,5},{5,4},{6,7},{7,6},{8,9},{9,8},{10,11... | collective-permute-start | bytes 540680 | tf_op jit(solution)/shard_map/ppermute | solution.py:466
  83.7 1.5 %collective-permute-start.4 = (bf16[352,256]{1,0:T(8,128)(2,1)}, bf16[352,256]{1,0:T(8,128)(2,1)S(1)}, u32[]{:S(2)}, u32[]{:S(2)}) collective-permute-start(bf16[352,256]{1,0:T(8,128)(2,1)} %get-tuple-element.63), channel_id=1, source_target_pairs={{0,2},{1,3},{2,0},{3,1},{4,6},{5,7},{6,4},{7,5},{8,10},{9,11},{10,... | collective-permute-start | bytes 540680 | tf_op jit(solution)/shard_map/ppermute | solution.py:466
  85.2 0.0 collective-permute-start.5
  85.2 4.0 %collective-permute-done.3 = bf16[352,256]{1,0:T(8,128)(2,1)S(1)} collective-permute-done((bf16[352,256]{1,0:T(8,128)(2,1)}, bf16[352,256]{1,0:T(8,128)(2,1)S(1)}, u32[]{:S(2)}, u32[]{:S(2)}) %collective-permute-start.3) | collective-permute-done | bytes 180256 | tf_op jit(solution)/shard_map/ppermute | solution.py:466
  89.3 4.9 %collective-permute-done.4 = bf16[352,256]{1,0:T(8,128)(2,1)S(1)} collective-permute-done((bf16[352,256]{1,0:T(8,128)(2,1)}, bf16[352,256]{1,0:T(8,128)(2,1)S(1)}, u32[]{:S(2)}, u32[]{:S(2)}) %collective-permute-start.4) | collective-permute-done | bytes 180256 | tf_op jit(solution)/shard_map/ppermute | solution.py:466
  94.1 0.0 collective-permute-done.5
  94.1 1.1 add_convert_fusion
  95.2 1.6 %collective-permute-start.6 = (bf16[176,256]{1,0:T(8,128)(2,1)S(1)}, bf16[176,256]{1,0:T(8,128)(2,1)S(1)}, u32[]{:S(2)}, u32[]{:S(2)}) collective-permute-start(bf16[176,256]{1,0:T(8,128)(2,1)S(1)} %broadcast_select_fusion), channel_id=1, source_target_pairs={{0,4},{1,5},{2,6},{3,7},{4,0},{5,1},{6,2},{7,3},{8,12},{9,13},{10,... | collective-permute-start | bytes 270344 | tf_op jit(solution)/shard_map/ppermute | solution.py:466
  96.8 0.0 collective-permute-start.1
  96.8 3.0 %collective-permute-done.6 = bf16[176,256]{1,0:T(8,128)(2,1)S(1)} collective-permute-done((bf16[176,256]{1,0:T(8,128)(2,1)S(1)}, bf16[176,256]{1,0:T(8,128)(2,1)S(1)}, u32[]{:S(2)}, u32[]{:S(2)}) %collective-permute-start.6) | collective-permute-done | bytes 90144 | tf_op jit(solution)/shard_map/ppermute | solution.py:466
  99.8 2.7 %collective-permute-start.7 = (bf16[176,256]{1,0:T(8,128)(2,1)S(1)}, bf16[176,256]{1,0:T(8,128)(2,1)S(1)}, u32[]{:S(2)}, u32[]{:S(2)}) collective-permute-start(bf16[176,256]{1,0:T(8,128)(2,1)S(1)} %add_convert_fusion.2), channel_id=1, source_target_pairs={{0,8},{1,9},{2,10},{3,11},{4,12},{5,13},{6,14},{7,15},{8,0},{9,1},... | collective-permute-start | bytes 270344 | tf_op jit(solution)/shard_map/ppermute | solution.py:466
  102.5 2.9 %collective-permute-done.7 = bf16[176,256]{1,0:T(8,128)(2,1)S(1)} collective-permute-done((bf16[176,256]{1,0:T(8,128)(2,1)S(1)}, bf16[176,256]{1,0:T(8,128)(2,1)S(1)}, u32[]{:S(2)}, u32[]{:S(2)}) %collective-permute-start.7) | collective-permute-done | bytes 90144 | tf_op jit(solution)/shard_map/ppermute | solution.py:466
  105.4 1.7 %collective-permute-start.8 = (bf16[176,256]{1,0:T(8,128)(2,1)S(1)}, bf16[176,256]{1,0:T(8,128)(2,1)S(1)}, u32[]{:S(2)}, u32[]{:S(2)}) collective-permute-start(bf16[176,256]{1,0:T(8,128)(2,1)S(1)} %add_convert_fusion.1), channel_id=1, source_target_pairs={{0,4},{1,5},{2,6},{3,7},{4,0},{5,1},{6,2},{7,3},{8,12},{9,13},{10,... | collective-permute-start | bytes 270344 | tf_op jit(solution)/shard_map/ppermute | solution.py:466
  107.1 0.0 collective-permute-done.1
  107.1 0.1 bitcast_convert_fusion
  107.2 2.8 %collective-permute-done.8 = bf16[176,256]{1,0:T(8,128)(2,1)S(1)} collective-permute-done((bf16[176,256]{1,0:T(8,128)(2,1)S(1)}, bf16[176,256]{1,0:T(8,128)(2,1)S(1)}, u32[]{:S(2)}, u32[]{:S(2)}) %collective-permute-start.8) | collective-permute-done | bytes 90144 | tf_op jit(solution)/shard_map/ppermute | solution.py:466
  110.0 0.1 maximum_select_fusion.1.refs_0_
  110.0 0.0 copy-start.1
  110.1 1.5 %collective-permute-start.11 = (bf16[352,256]{1,0:T(8,128)(2,1)S(1)}, bf16[352,256]{1,0:T(8,128)(2,1)S(1)}, u32[]{:S(2)}, u32[]{:S(2)}) collective-permute-start(bf16[352,256]{1,0:T(8,128)(2,1)S(1)} %maximum_select_fusion.1.refs_0_), channel_id=1, source_target_pairs={{0,3},{1,2},{2,1},{3,0},{4,7},{5,6},{6,5},{7,4},{8,11},{9,10},{10,... | collective-permute-start | bytes 540680 | tf_op jit(solution)/shard_map/ppermute | solution.py:466
  111.6 1.2 collective-permute-start.10
  112.8 0.8 collective-permute-start.9
  113.6 0.0 copy-done
  113.6 1.6 %maximum_select_fusion = f32[1,2048,256]{2,1,0:T(8,128)} fusion(f32[1,1024,256]{2,1,0:T(8,128)S(1)} %bitcast_convert_fusion, f32[1,1024,256]{2,1,0:T(8,128)S(1)} %bitcast.17, pred[]{:T(512)S(6)} %eq.11), kind=kLoop, calls=%fused_computation | loop fusion | flops 1572864 | bytes 4194305 | tf_op jit(solution)/shard_map/jit(_where)/select_n | solution.py:612
  115.2 0.0 copy-done.1
  115.2 1.4 %collective-permute-done.11.refs_3_ = bf16[352,256]{1,0:T(8,128)(2,1)S(1)} collective-permute-done((bf16[352,256]{1,0:T(8,128)(2,1)S(1)}, bf16[352,256]{1,0:T(8,128)(2,1)S(1)}, u32[]{:S(2)}, u32[]{:S(2)}) %collective-permute-start.11) | collective-permute-done | bytes 180256 | tf_op jit(solution)/shard_map/ppermute | solution.py:466
  116.6 0.0 copy-start.4
  116.6 1.8 %collective-permute-done.10.refs_2_ = bf16[352,256]{1,0:T(8,128)(2,1)S(1)} collective-permute-done((bf16[352,256]{1,0:T(8,128)(2,1)S(1)}, bf16[352,256]{1,0:T(8,128)(2,1)S(1)}, u32[]{:S(2)}, u32[]{:S(2)}) %collective-permute-start.10) | collective-permute-done | bytes 180256 | tf_op jit(solution)/shard_map/ppermute | solution.py:466
  118.4 0.0 copy-start.5
  118.5 0.1 collective-permute-done.9.refs_1_
  118.5 0.0 copy-start.6
  118.5 0.0 copy-done.4
  118.5 0.6 copy-done.5
  119.1 0.1 copy-done.6
  119.2 6.4 %update.1 = (f32[1,32,256]{2,1,0:T(8,128)}, f32[1,32,256]{2,1,0:T(8,128)}, f32[1,32,256]{2,1,0:T(8,128)}, bf16[1,32,256]{2,1,0:T(8,128)(2,1)}, f32[1,256,256]{2,...) custom-call(s32[1]{0:T(128)} %bitcast.7.which, ...), custom_call_target="tpu_custom_call" | custom-call | tf_op jit(solution)/shard_map/update/pallas_call | solution.py:633
  (3 shorter events, 0.1 us)
Async XLA Ops:
  3.1 2.5 %collective-permute-start = (bf16[1408,256]{1,0:T(8,128)(2,1)}, bf16[1408,256]{1,0:T(8,128)(2,1)S(1)}, u32[]{:S(2)}, u32[]{:S(2)}) collective-permute-start(bf16[1408,256]{1,0:T(8,128)(2,1)} %pack.1.mine), channel_id=1, source_target_pairs={{0,16},{16,0},{1,17},{17,1},{2,18},{18,2},{3,19},{19,3},{4,20},{20... | collective-permute-start | bytes 2162696 | tf_op jit(solution)/shard_map/ppermute | solution.py:462
  5.6 0.9 copy-start.3
  75.2 2.5 %collective-permute-start.2 = (bf16[1408,256]{1,0:T(8,128)(2,1)}, bf16[1408,256]{1,0:T(8,128)(2,1)S(1)}, u32[]{:S(2)}, u32[]{:S(2)}) collective-permute-start(bf16[1408,256]{1,0:T(8,128)(2,1)} %get-tuple-element.60), channel_id=1, source_target_pairs={{0,16},{16,0},{1,17},{17,1},{2,18},{18,2},{3,19},{19,3},{4,20},{20... | collective-permute-start | bytes 2162696 | tf_op jit(solution)/shard_map/ppermute | solution.py:462
  77.6 0.9 copy-start.2
  80.9 32.8 %copy-start = (f32[1024,256]{1,0:T(8,128)S(1)}, f32[1024,256]{1,0:T(8,128)}, u32[]{:S(2)}) copy-start(f32[1024,256]{1,0:T(8,128)} %get-tuple-element.57) | copy-start | bytes 3145732
  80.9 8.4 %collective-permute-start.3 = (bf16[352,256]{1,0:T(8,128)(2,1)}, bf16[352,256]{1,0:T(8,128)(2,1)S(1)}, u32[]{:S(2)}, u32[]{:S(2)}) collective-permute-start(bf16[352,256]{1,0:T(8,128)(2,1)} %get-tuple-element.62), channel_id=1, source_target_pairs={{0,1},{1,0},{2,3},{3,2},{4,5},{5,4},{6,7},{7,6},{8,9},{9,8},{10,11... | collective-permute-start | bytes 540680 | tf_op jit(solution)/shard_map/ppermute | solution.py:466
  83.7 10.4 %collective-permute-start.4 = (bf16[352,256]{1,0:T(8,128)(2,1)}, bf16[352,256]{1,0:T(8,128)(2,1)S(1)}, u32[]{:S(2)}, u32[]{:S(2)}) collective-permute-start(bf16[352,256]{1,0:T(8,128)(2,1)} %get-tuple-element.63), channel_id=1, source_target_pairs={{0,2},{1,3},{2,0},{3,1},{4,6},{5,7},{6,4},{7,5},{8,10},{9,11},{10,... | collective-permute-start | bytes 540680 | tf_op jit(solution)/shard_map/ppermute | solution.py:466
  85.2 8.9 %collective-permute-start.5 = (bf16[352,256]{1,0:T(8,128)(2,1)}, bf16[352,256]{1,0:T(8,128)(2,1)S(1)}, u32[]{:S(2)}, u32[]{:S(2)}) collective-permute-start(bf16[352,256]{1,0:T(8,128)(2,1)} %get-tuple-element.64), channel_id=1, source_target_pairs={{0,3},{1,2},{2,1},{3,0},{4,7},{5,6},{6,5},{7,4},{8,11},{9,10},{10,... | collective-permute-start | bytes 540680 | tf_op jit(solution)/shard_map/ppermute | solution.py:466
  95.2 4.6 %collective-permute-start.6 = (bf16[176,256]{1,0:T(8,128)(2,1)S(1)}, bf16[176,256]{1,0:T(8,128)(2,1)S(1)}, u32[]{:S(2)}, u32[]{:S(2)}) collective-permute-start(bf16[176,256]{1,0:T(8,128)(2,1)S(1)} %broadcast_select_fusion), channel_id=1, source_target_pairs={{0,4},{1,5},{2,6},{3,7},{4,0},{5,1},{6,2},{7,3},{8,12},{9,13},{10,... | collective-permute-start | bytes 270344 | tf_op jit(solution)/shard_map/ppermute | solution.py:466
  96.8 10.2 %collective-permute-start.1 = (bf16[1024,256]{1,0:T(8,128)(2,1)}, bf16[1024,256]{1,0:T(8,128)(2,1)S(1)}, u32[]{:S(2)}, u32[]{:S(2)}) collective-permute-start(bf16[1024,256]{1,0:T(8,128)(2,1)} %get-tuple-element.58), channel_id=1, source_target_pairs={{0,16},{16,0},{1,17},{17,1},{2,18},{18,2},{3,19},{19,3},{4,20},{20... | collective-permute-start | bytes 1572872 | tf_op jit(solution)/shard_map/ppermute | solution.py:462
  99.8 5.5 %collective-permute-start.7 = (bf16[176,256]{1,0:T(8,128)(2,1)S(1)}, bf16[176,256]{1,0:T(8,128)(2,1)S(1)}, u32[]{:S(2)}, u32[]{:S(2)}) collective-permute-start(bf16[176,256]{1,0:T(8,128)(2,1)S(1)} %add_convert_fusion.2), channel_id=1, source_target_pairs={{0,8},{1,9},{2,10},{3,11},{4,12},{5,13},{6,14},{7,15},{8,0},{9,1},... | collective-permute-start | bytes 270344 | tf_op jit(solution)/shard_map/ppermute | solution.py:466
  105.4 4.6 %collective-permute-start.8 = (bf16[176,256]{1,0:T(8,128)(2,1)S(1)}, bf16[176,256]{1,0:T(8,128)(2,1)S(1)}, u32[]{:S(2)}, u32[]{:S(2)}) collective-permute-start(bf16[176,256]{1,0:T(8,128)(2,1)S(1)} %add_convert_fusion.1), channel_id=1, source_target_pairs={{0,4},{1,5},{2,6},{3,7},{4,0},{5,1},{6,2},{7,3},{8,12},{9,13},{10,... | collective-permute-start | bytes 270344 | tf_op jit(solution)/shard_map/ppermute | solution.py:466
  110.0 5.1 %copy-start.1 = (bf16[352,256]{1,0:T(8,128)(2,1)}, bf16[352,256]{1,0:T(8,128)(2,1)S(1)}, u32[]{:S(2)}) copy-start(bf16[352,256]{1,0:T(8,128)(2,1)S(1)} %maximum_select_fusion.1.refs_0_) | copy-start | bytes 540676
  110.1 6.6 %collective-permute-start.11 = (bf16[352,256]{1,0:T(8,128)(2,1)S(1)}, bf16[352,256]{1,0:T(8,128)(2,1)S(1)}, u32[]{:S(2)}, u32[]{:S(2)}) collective-permute-start(bf16[352,256]{1,0:T(8,128)(2,1)S(1)} %maximum_select_fusion.1.refs_0_), channel_id=1, source_target_pairs={{0,3},{1,2},{2,1},{3,0},{4,7},{5,6},{6,5},{7,4},{8,11},{9,10},{10,... | collective-permute-start | bytes 540680 | tf_op jit(solution)/shard_map/ppermute | solution.py:466
  111.6 6.8 %collective-permute-start.10 = (bf16[352,256]{1,0:T(8,128)(2,1)S(1)}, bf16[352,256]{1,0:T(8,128)(2,1)S(1)}, u32[]{:S(2)}, u32[]{:S(2)}) collective-permute-start(bf16[352,256]{1,0:T(8,128)(2,1)S(1)} %maximum_select_fusion.1.refs_0_), channel_id=1, source_target_pairs={{0,2},{1,3},{2,0},{3,1},{4,6},{5,7},{6,4},{7,5},{8,10},{9,11},{10,... | collective-permute-start | bytes 540680 | tf_op jit(solution)/shard_map/ppermute | solution.py:466
  112.8 5.7 %collective-permute-start.9 = (bf16[352,256]{1,0:T(8,128)(2,1)S(1)}, bf16[352,256]{1,0:T(8,128)(2,1)S(1)}, u32[]{:S(2)}, u32[]{:S(2)}) collective-permute-start(bf16[352,256]{1,0:T(8,128)(2,1)S(1)} %maximum_select_fusion.1.refs_0_), channel_id=1, source_target_pairs={{0,1},{1,0},{2,3},{3,2},{4,5},{5,4},{6,7},{7,6},{8,9},{9,8},{10,11... | collective-permute-start | bytes 540680 | tf_op jit(solution)/shard_map/ppermute | solution.py:466
  116.6 1.9 %copy-start.4 = (bf16[352,256]{1,0:T(8,128)(2,1)}, bf16[352,256]{1,0:T(8,128)(2,1)S(1)}, u32[]{:S(2)}) copy-start(bf16[352,256]{1,0:T(8,128)(2,1)S(1)} %collective-permute-done.11.refs_3_) | copy-start | bytes 540676
  118.4 0.7 copy-start.5
  118.5 0.7 copy-start.6

commit v4 on v3

--- a/solution.py
+++ b/solution.py
@@ -23,6 +23,7 @@
 FIRST, SECOND = 4, 4
 SPARE = 7
 STEPS = 4
+SMALL = 16 * 1024 * 1024
 VMEM = 63 * 1024 * 1024
 
 
@@ -408,54 +409,50 @@
                 packed[lay.used :, :] = jnp.zeros((lay.rows - lay.used, width), kind)
 
 
-def combine_kernel(parts, which, keep, received, *outs):
-    rows = outs[0].shape[0]
-    for turn, out in enumerate(outs):
-        low = pl.multiple_of((which[0] ^ turn) * rows, TILE)
-        value = keep[pl.ds(low, rows), :].astype(F32) + received[pl.ds(low, rows), :].astype(F32)
-        out[...] = value.astype(out.dtype)
-
-
 def update_kernel(lay, parts, which, *refs):
     pieces, ins, outs = refs[:parts], refs[parts : parts + 18], refs[parts + 18 : parts + 42]
-    total, scale = refs[-2:]
-    step = pl.program_id(0)
-
-    def new(at, spot, grad):
+    stages, total, done = refs[parts + 42 : parts + 66], refs[-2], refs[-1]
+    rows = pieces[0].shape[0]
+    for turn, piece in enumerate(pieces):
+        low = pl.multiple_of((which[0] ^ turn) * rows, TILE)
+        total[pl.ds(low, rows), :] = piece[...]
+    low = lay.tail // TILE * TILE
+    tail = total[low : lay.spots["head"][1], :].astype(F32)[lay.tail - low : lay.tail - low + 3]
+    lane = lax.broadcasted_iota(jnp.int32, (1, lay.width), 1)
+    place = jnp.where(lane < BITS, (1 << jnp.minimum(lane, BITS)).astype(F32), 0.0)
+    count = jnp.sum(tail[2:3] * place, axis=-1, keepdims=True)
+    scale = GRAD_SCALE * lax.rsqrt(count)
+    copies = []
+
+    def new(at, spot, copy_spot, parts_of, grad):
         weight, moment, average = ins[3 * at : 3 * at + 3]
-        step_grad = grad.astype(F32) * scale[0:1, 0:1]
+        step_grad = grad.astype(F32) * scale
         new_moment = MOMENTUM * moment[spot] + step_grad
         new_weight = weight[spot] - RATE * (step_grad + MOMENTUM * new_moment)
-        out_moment, out_average, out_weight, out_copy = outs[4 * at : 4 * at + 4]
-        out_moment[spot] = new_moment
-        out_average[spot] = AVERAGE * average[spot] + (1.0 - AVERAGE) * new_weight
-        out_weight[spot] = new_weight
-        out_copy[0] = new_weight.astype(BF16)
-
-    @pl.when(step == 0)
-    def start():
-        rows = pieces[0].shape[0]
-        for turn, piece in enumerate(pieces):
-            low = pl.multiple_of((which[0] ^ turn) * rows, TILE)
-            total[pl.ds(low, rows), :] = piece[...]
-        low = lay.tail // TILE * TILE
-        high = lay.spots["head"][1]
-        tail = total[low:high, :].astype(F32)[lay.tail - low : lay.tail - low + 3]
-        lane = lax.broadcasted_iota(jnp.int32, (1, lay.width), 1)
-        place = jnp.where(lane < BITS, (1 << jnp.minimum(lane, BITS)).astype(F32), 0.0)
-        count = jnp.sum(tail[2:3] * place, axis=-1, keepdims=True)
-        scale[...] = jnp.broadcast_to(GRAD_SCALE * lax.rsqrt(count), scale.shape)
-        low, high = lay.spots["table"]
-        new(0, (0,), total[low:high, :])
-        new(2, (0,), tail[0:2])
-
-    for at, name in ((1, "in"), (3, "up"), (4, "down")):
-        rows = ins[3 * at].shape[1]
-        low = pl.multiple_of(lay.spots[name][0] + step * rows, TILE)
-        new(at, (0,), total[pl.ds(low, rows), :])
-    rows = ins[15].shape[0]
-    low = pl.multiple_of(lay.spots["head"][0] + step * rows, TILE)
-    new(5, (slice(None), 0), total[pl.ds(low, rows), :])
+        new_average = AVERAGE * average[spot] + (1.0 - AVERAGE) * new_weight
+        news = (new_moment, new_average, new_weight, new_weight.astype(BF16))
+        for kind, value in enumerate(news):
+            stage, out = stages[4 * at + kind], outs[4 * at + kind]
+            stage[copy_spot if kind == 3 else spot] = value
+            piece = parts_of[1 if kind == 3 else 0]
+            copies.append(pltpu.make_async_copy(stage.at[piece], out.at[piece], done.at[len(copies)]))
+            copies[-1].start()
+
+    everything = (slice(None),)
+    low, high = lay.spots["head"]
+    step = -(-lay.bins // (STEPS * TILE)) * TILE
+    for begin in range(0, lay.bins, step):
+        end = min(begin + step, lay.bins)
+        cover = min(-(-end // TILE) * TILE, high - low)
+        grad = total[low + begin : low + cover, :].astype(F32)[: end - begin]
+        new(5, (slice(begin, end), 0), (0, slice(begin, end)),
+            ((slice(begin, end),), (slice(None), slice(begin, end))), grad)
+    for at, name in ((1, "in"), (3, "up"), (4, "down"), (0, "table")):
+        low, high = lay.spots[name]
+        new(at, (0,), (0,), (everything, everything), total[low:high, :])
+    new(2, (0,), (0,), (everything, everything), tail[0:2])
+    for copy in copies:
+        copy.wait()
 
 
 def swap(value):
@@ -576,18 +573,15 @@
     place = (index % parts)[None]
     in_smem = pl.BlockSpec(memory_space=pltpu.SMEM)
 
-    def spec_all(*shape):
-        return pl.BlockSpec(shape, lambda *_: (0,) * len(shape))
-
     part_shape = (lay.rows // parts, width)
-    own, *others = pl.pallas_call(
-        functools.partial(combine_kernel, parts),
-        in_specs=[in_smem, spec_all(*packed_shape), spec_all(*packed_shape)],
-        out_shape=[jax.ShapeDtypeStruct(part_shape, F32)]
-        + [jax.ShapeDtypeStruct(part_shape, BF16)] * (parts - 1),
-        compiler_params=roomy,
-        name="combine",
-    )(place, keep, swap(send))
+    both = keep.astype(F32) + swap(send).astype(F32)
+    both = lax.optimization_barrier(both.reshape(parts, *part_shape))
+
+    def part_for(mask):
+        return lax.dynamic_index_in_dim(both, place[0] ^ mask, 0, keepdims=False)
+
+    own = part_for(0)
+    others = [part_for(mask).astype(BF16) for mask in range(1, parts)]
     current = own
     for arrived in [across(other, mask, length) for mask, other in enumerate(others, 1)]:
         current = current + arrived.astype(F32)
@@ -614,30 +608,20 @@
         jnp.concatenate([ends_mine, other]),
         jnp.concatenate([other, ends_mine]),
     )[None]
-    head_rows = -(-bins // (STEPS * TILE)) * TILE
-    news, in_specs, out_specs = [], [], []
+    news = []
     for at in range(6):
         shape = weights[3 * at].shape
         news += [jax.ShapeDtypeStruct(shape, F32)] * 3
         news.append(jax.ShapeDtypeStruct((1, shape[0], width) if at == 5 else shape, BF16))
-        if at in (0, 2):
-            spec = copy_spec = spec_all(*shape)
-        elif at == 5:
-            spec = pl.BlockSpec((head_rows, 1, width), lambda i: (i, 0, 0))
-            copy_spec = pl.BlockSpec((1, head_rows, width), lambda i: (0, i, 0))
-        else:
-            spec = copy_spec = pl.BlockSpec((1, width // STEPS, width), lambda i: (0, i, 0))
-        in_specs += [spec] * 3
-        out_specs += [spec] * 3 + [copy_spec]
-    total_rows = max(lay.rows, lay.spots["head"][0] + STEPS * head_rows)
+    copy_count = 4 * (5 + -(-bins // (-(-bins // (STEPS * TILE)) * TILE)))
     updated = pl.pallas_call(
         functools.partial(update_kernel, lay, parts),
-        grid=(STEPS,),
-        in_specs=[in_smem] + [spec_all(*part_shape)] * parts + in_specs,
-        out_specs=out_specs,
+        in_specs=[in_smem] + [pl.BlockSpec(memory_space=pltpu.VMEM)] * (parts + 18),
+        out_specs=[pl.BlockSpec(memory_space=pl.ANY)] * 24,
         out_shape=news,
-        scratch_shapes=[pltpu.VMEM((total_rows, width), BF16), pltpu.VMEM((8, LANES), F32)],
-        compiler_params=roomy,
+        scratch_shapes=[pltpu.VMEM(new.shape, new.dtype) for new in news]
+        + [pltpu.VMEM(packed_shape, BF16), pltpu.SemaphoreType.DMA((copy_count,))],
+        compiler_params=pltpu.CompilerParams(vmem_limit_bytes=SMALL),
         name="update",
     )(place, *pieces, *weights)
     table_out, in_out, gain_out, up_out, down_out, head_out = (updated[4 * at : 4 * at + 4] for at in range(6))

time: 126 us -> 124 us (0.984)
  Pallas kernels: 79.9 us -> 75 us
  waiting for transfers between devices: 24.9 us -> 27.7 us
  local copies, waits for them, and re-layouts: 2.46 us -> 1.03 us
    pallas_call x2 -> x1, Pallas kernels: 8.76 us -> 3.82 us  [on_device(): pl.pallas_call(functools.partial(update_kernel, lay, parts), in_specs=[in...]
    ppermute x9, waiting for transfers between devices: 20.9 us -> 23.7 us  [across(): return lax.ppermute(array, 'dp', [(i, i ^ mask) for i in range(length)])]
    unnamed x14 -> x40, local copies, waits for them, and re-layouts: 2.46 us -> 0.97 us
  transfers between devices with their start and end apart: 12 -> 12, of which waited for: 10 -> 11; matrix products, arithmetic and copies ran while one was open for 1% -> 1% of each run, Pallas kernels for 0% -> 0%
where the time goes in v4:
time: 124 us; the launch traced here: 123 us
  Pallas kernels  75 us (60%)
  waiting for transfers between devices  27.7 us (22%)
  starting transfers between devices  14.4 us (12%)
  other arithmetic  4.03 us (3%)
    pallas_call x1, Pallas kernels, on_device(): pl.pallas_call(functools.partial(towers_kernel, lay, steps, chunk), grid_...  68.7 us
    ppermute x9, waiting for transfers between devices, across(): return lax.ppermute(array, 'dp', [(i, i ^ mask) for i in range(length)])  23.7 us
    ppermute x9, starting transfers between devices, across(): return lax.ppermute(array, 'dp', [(i, i ^ mask) for i in range(length)])  13.5 us
    ppermute x3, waiting for transfers between devices, swap(): return lax.ppermute(value, 'section', [(0, 1), (1, 0)])  4.06 us
    pallas_call x1, Pallas kernels, on_device(): pl.pallas_call(functools.partial(update_kernel, lay, parts), in_specs=[in...  3.82 us
  transfers between devices with their start and end apart: 12, of which 11 were waited for; matrix products, arithmetic and copies ran while one was open for 1% of the time, Pallas kernels for 0%

profile of v4, /device:TPU:0, one launch (start us, length us, event | category | flops | bytes accessed | tf_op | source)
XLA Modules:
  0.0 123.3 jit_solution(12512542952800786301)
XLA Ops:
  0.7 2.5 %pack.1.mine = bf16[1408,256]{1,0:T(8,128)(2,1)} custom-call(f32[1,32,256]{2,1,0:T(8,128)} %refs_4_.1, f32[1,256,256]{2,1,0:T(8,128)} %refs_7_.1, f32[1,256,256]{2,1,0:T(8,128)} %refs_13_.1, f32[1,256,256]{2,1,0:T(8,128)} %refs_16_.1, f32[601,1,256]{2,1,0:T(1,128)} %bitcast.30, f32[1,2,256]{2,1,0:T(2,128)} %refs_10_.1), custom_call_target="tpu_custom_call" | custom-call | tf_op jit(solution)/shard_map/pack/pallas_call | solution.py:481
  3.1 0.5 collective-permute-start
  3.6 2.0 %collective-permute-done.theirs = bf16[1408,256]{1,0:T(8,128)(2,1)S(1)} collective-permute-done((bf16[1408,256]{1,0:T(8,128)(2,1)}, bf16[1408,256]{1,0:T(8,128)(2,1)S(1)}, u32[]{:S(2)}, u32[]{:S(2)}) %collective-permute-start) | collective-permute-done | bytes 720928 | tf_op jit(solution)/shard_map/ppermute | solution.py:459
  5.6 0.9 copy-done.19
  6.5 68.7 %towers.1 = (bf16[1408,256]{1,0:T(8,128)(2,1)}, bf16[1408,256]{1,0:T(8,128)(2,1)}, f32[1024,256]{1,0:T(8,128)}, bf16[1024,256]{1,0:T(8,128)(2,1)}) custom-call(s32[1]{0:T(128)} %bitcast.which, bf16[2048,256]{1,0:T(8,128)(2,1)} %latent.1, s32[5,2,2048]{2,1,0:T(2,128)} %bitcast.37, s32[5,2,2048]{2,1,0:T(2,128)} %bitcast.38, s32[5,2048]{1,0:T(8,128)} %whole_valid.1, ...), custom_call_target="tpu_custom_call" | custom-call | tf_op jit(solution)/shard_map/towers/pallas_call | solution.py:509
  75.2 0.4 collective-permute-start.2
  75.6 2.0 %collective-permute-done.2 = bf16[1408,256]{1,0:T(8,128)(2,1)S(1)} collective-permute-done((bf16[1408,256]{1,0:T(8,128)(2,1)}, bf16[1408,256]{1,0:T(8,128)(2,1)S(1)}, u32[]{:S(2)}, u32[]{:S(2)}) %collective-permute-start.2) | collective-permute-done | bytes 720928 | tf_op jit(solution)/shard_map/ppermute | solution.py:459
  77.6 1.3 %convert_add_fusion = f32[1408,256]{1,0:T(8,128)S(1)} fusion(bf16[1408,256]{1,0:T(8,128)(2,1)S(1)} %collective-permute-done.2, bf16[1408,256]{1,0:T(8,128)(2,1)} %get-tuple-element.55), kind=kLoop, calls=%fused_computation.1 | loop fusion | flops 1081344 | bytes 2883584 | tf_op jit(solution)/shard_map/add | solution.py:577
  78.9 0.1 fusion.3
  79.0 0.0 copy-start.18
  79.0 2.9 %collective-permute-start.3 = (bf16[352,256]{1,0:T(8,128)(2,1)S(1)}, bf16[352,256]{1,0:T(8,128)(2,1)S(1)}, u32[]{:S(2)}, u32[]{:S(2)}) collective-permute-start(bf16[352,256]{1,0:T(8,128)(2,1)S(1)} %get-tuple-element.81), channel_id=1, source_target_pairs={{0,1},{1,0},{2,3},{3,2},{4,5},{5,4},{6,7},{7,6},{8,9},{9,8},{10,11... | collective-permute-start | bytes 540680 | tf_op jit(solution)/shard_map/ppermute | solution.py:463
  81.9 1.5 %collective-permute-start.5 = (bf16[352,256]{1,0:T(8,128)(2,1)S(1)}, bf16[352,256]{1,0:T(8,128)(2,1)S(1)}, u32[]{:S(2)}, u32[]{:S(2)}) collective-permute-start(bf16[352,256]{1,0:T(8,128)(2,1)S(1)} %get-tuple-element.82), channel_id=1, source_target_pairs={{0,3},{1,2},{2,1},{3,0},{4,7},{5,6},{6,5},{7,4},{8,11},{9,10},{10,... | collective-permute-start | bytes 540680 | tf_op jit(solution)/shard_map/ppermute | solution.py:463
  83.4 0.0 collective-permute-start.4
  83.4 3.8 %collective-permute-done.3 = bf16[352,256]{1,0:T(8,128)(2,1)S(1)} collective-permute-done((bf16[352,256]{1,0:T(8,128)(2,1)S(1)}, bf16[352,256]{1,0:T(8,128)(2,1)S(1)}, u32[]{:S(2)}, u32[]{:S(2)}) %collective-permute-start.3) | collective-permute-done | bytes 180256 | tf_op jit(solution)/shard_map/ppermute | solution.py:463
  87.2 4.7 %collective-permute-done.5 = bf16[352,256]{1,0:T(8,128)(2,1)S(1)} collective-permute-done((bf16[352,256]{1,0:T(8,128)(2,1)S(1)}, bf16[352,256]{1,0:T(8,128)(2,1)S(1)}, u32[]{:S(2)}, u32[]{:S(2)}) %collective-permute-start.5) | collective-permute-done | bytes 180256 | tf_op jit(solution)/shard_map/ppermute | solution.py:463
  91.9 1.5 %collective-permute-done.4 = bf16[352,256]{1,0:T(8,128)(2,1)} collective-permute-done((bf16[352,256]{1,0:T(8,128)(2,1)S(1)}, bf16[352,256]{1,0:T(8,128)(2,1)}, u32[]{:S(2)}, u32[]{:S(2)}) %collective-permute-start.4) | collective-permute-done | bytes 180256 | tf_op jit(solution)/shard_map/ppermute | solution.py:463
  93.4 1.0 fusion.2
  94.4 1.6 %collective-permute-start.6 = (bf16[176,256]{1,0:T(8,128)(2,1)S(1)}, bf16[176,256]{1,0:T(8,128)(2,1)S(1)}, u32[]{:S(2)}, u32[]{:S(2)}) collective-permute-start(bf16[176,256]{1,0:T(8,128)(2,1)S(1)} %broadcast_select_fusion), channel_id=1, source_target_pairs={{0,4},{1,5},{2,6},{3,7},{4,0},{5,1},{6,2},{7,3},{8,12},{9,13},{10,... | collective-permute-start | bytes 270344 | tf_op jit(solution)/shard_map/ppermute | solution.py:463
  96.1 0.0 collective-permute-start.1
  96.1 2.9 %collective-permute-done.6 = bf16[176,256]{1,0:T(8,128)(2,1)S(1)} collective-permute-done((bf16[176,256]{1,0:T(8,128)(2,1)S(1)}, bf16[176,256]{1,0:T(8,128)(2,1)S(1)}, u32[]{:S(2)}, u32[]{:S(2)}) %collective-permute-start.6) | collective-permute-done | bytes 90144 | tf_op jit(solution)/shard_map/ppermute | solution.py:463
  99.1 3.4 %collective-permute-start.7 = (bf16[176,256]{1,0:T(8,128)(2,1)S(1)}, bf16[176,256]{1,0:T(8,128)(2,1)S(1)}, u32[]{:S(2)}, u32[]{:S(2)}) collective-permute-start(bf16[176,256]{1,0:T(8,128)(2,1)S(1)} %add_convert_fusion.1), channel_id=1, source_target_pairs={{0,8},{1,9},{2,10},{3,11},{4,12},{5,13},{6,14},{7,15},{8,0},{9,1},... | collective-permute-start | bytes 270344 | tf_op jit(solution)/shard_map/ppermute | solution.py:463
  102.5 3.5 %collective-permute-done.7 = bf16[176,256]{1,0:T(8,128)(2,1)S(1)} collective-permute-done((bf16[176,256]{1,0:T(8,128)(2,1)S(1)}, bf16[176,256]{1,0:T(8,128)(2,1)S(1)}, u32[]{:S(2)}, u32[]{:S(2)}) %collective-permute-start.7) | collective-permute-done | bytes 90144 | tf_op jit(solution)/shard_map/ppermute | solution.py:463
  106.0 0.5 collective-permute-start.8
  106.4 0.0 collective-permute-done.1
  106.4 0.1 bitcast_convert_fusion
  106.5 4.1 %collective-permute-done.8 = bf16[176,256]{1,0:T(8,128)(2,1)S(1)} collective-permute-done((bf16[176,256]{1,0:T(8,128)(2,1)S(1)}, bf16[176,256]{1,0:T(8,128)(2,1)S(1)}, u32[]{:S(2)}, u32[]{:S(2)}) %collective-permute-start.8) | collective-permute-done | bytes 90144 | tf_op jit(solution)/shard_map/ppermute | solution.py:463
  110.6 0.1 maximum_select_fusion.1.refs_0_
  110.6 1.5 %collective-permute-start.11 = (bf16[352,256]{1,0:T(8,128)(2,1)S(1)}, bf16[352,256]{1,0:T(8,128)(2,1)S(1)}, u32[]{:S(2)}, u32[]{:S(2)}) collective-permute-start(bf16[352,256]{1,0:T(8,128)(2,1)S(1)} %maximum_select_fusion.1.refs_0_), channel_id=1, source_target_pairs={{0,3},{1,2},{2,1},{3,0},{4,7},{5,6},{6,5},{7,4},{8,11},{9,10},{10,... | collective-permute-start | bytes 540680 | tf_op jit(solution)/shard_map/ppermute | solution.py:463
  112.1 1.5 %collective-permute-start.10 = (bf16[352,256]{1,0:T(8,128)(2,1)S(1)}, bf16[352,256]{1,0:T(8,128)(2,1)S(1)}, u32[]{:S(2)}, u32[]{:S(2)}) collective-permute-start(bf16[352,256]{1,0:T(8,128)(2,1)S(1)} %maximum_select_fusion.1.refs_0_), channel_id=1, source_target_pairs={{0,2},{1,3},{2,0},{3,1},{4,6},{5,7},{6,4},{7,5},{8,10},{9,11},{10,... | collective-permute-start | bytes 540680 | tf_op jit(solution)/shard_map/ppermute | solution.py:463
  113.7 0.5 collective-permute-start.9
  114.2 0.0 copy-done.18
  114.2 0.0 copy-start.3
  114.2 0.0 copy-start.4
  114.2 0.0 copy-start.5
  114.2 0.0 copy-start.6
  114.2 0.0 copy-start.7
  114.3 0.0 copy-start.8
  114.3 0.0 copy-start.9
  114.3 0.0 copy-start.10
  114.3 0.0 copy-start.12
  114.3 0.0 copy-start.13
  114.3 0.0 copy-start.14
  114.3 0.0 copy-start.15
  114.3 0.0 copy-start.16
  114.4 0.0 copy-start.17
  114.4 1.6 %maximum_select_fusion = f32[1,2048,256]{2,1,0:T(8,128)} fusion(f32[1,1024,256]{2,1,0:T(8,128)S(1)} %bitcast_convert_fusion, f32[1,1024,256]{2,1,0:T(8,128)S(1)} %bitcast.36, pred[]{:T(512)S(6)} %eq.11), kind=kLoop, calls=%fused_computation | loop fusion | flops 1572864 | bytes 4194305 | tf_op jit(solution)/shard_map/jit(_where)/select_n | solution.py:606
  115.9 1.3 %collective-permute-done.11.refs_3_ = bf16[352,256]{1,0:T(8,128)(2,1)S(1)} collective-permute-done((bf16[352,256]{1,0:T(8,128)(2,1)S(1)}, bf16[352,256]{1,0:T(8,128)(2,1)S(1)}, u32[]{:S(2)}, u32[]{:S(2)}) %collective-permute-start.11) | collective-permute-done | bytes 180256 | tf_op jit(solution)/shard_map/ppermute | solution.py:463
  117.2 1.8 %collective-permute-done.10.refs_2_ = bf16[352,256]{1,0:T(8,128)(2,1)S(1)} collective-permute-done((bf16[352,256]{1,0:T(8,128)(2,1)S(1)}, bf16[352,256]{1,0:T(8,128)(2,1)S(1)}, u32[]{:S(2)}, u32[]{:S(2)}) %collective-permute-start.10) | collective-permute-done | bytes 180256 | tf_op jit(solution)/shard_map/ppermute | solution.py:463
  119.0 0.1 collective-permute-done.9.refs_1_
  119.1 0.0 copy-done.11
  119.2 0.0 copy-done
  119.2 0.0 copy-done.1
  119.2 0.0 copy-done.2
  119.2 0.0 copy-done.3
  119.2 0.0 copy-done.4
  119.2 0.0 copy-done.5
  119.2 0.0 copy-done.6
  119.2 0.0 copy-done.7
  119.2 0.0 copy-done.8
  119.2 0.0 copy-done.9
  119.2 0.0 copy-done.10
  119.2 0.0 copy-done.12
  119.3 0.0 copy-done.13
  119.3 3.8 %update.1 = (f32[1,32,256]{2,1,0:T(8,128)}, f32[1,32,256]{2,1,0:T(8,128)}, f32[1,32,256]{2,1,0:T(8,128)}, bf16[1,32,256]{2,1,0:T(8,128)(2,1)}, f32[1,256,256]{2,...) custom-call(s32[1]{0:T(128)} %bitcast.7.which, ...), custom_call_target="tpu_custom_call" | custom-call | tf_op jit(solution)/shard_map/update/pallas_call | solution.py:617
  (12 shorter events, 0.1 us)
Async XLA Ops:
  3.1 2.5 %collective-permute-start = (bf16[1408,256]{1,0:T(8,128)(2,1)}, bf16[1408,256]{1,0:T(8,128)(2,1)S(1)}, u32[]{:S(2)}, u32[]{:S(2)}) collective-permute-start(bf16[1408,256]{1,0:T(8,128)(2,1)} %pack.1.mine), channel_id=1, source_target_pairs={{0,16},{16,0},{1,17},{17,1},{2,18},{18,2},{3,19},{19,3},{4,20},{20... | collective-permute-start | bytes 2162696 | tf_op jit(solution)/shard_map/ppermute | solution.py:459
  5.6 0.9 copy-start.19
  75.2 2.5 %collective-permute-start.2 = (bf16[1408,256]{1,0:T(8,128)(2,1)}, bf16[1408,256]{1,0:T(8,128)(2,1)S(1)}, u32[]{:S(2)}, u32[]{:S(2)}) collective-permute-start(bf16[1408,256]{1,0:T(8,128)(2,1)} %get-tuple-element.56), channel_id=1, source_target_pairs={{0,16},{16,0},{1,17},{17,1},{2,18},{18,2},{3,19},{19,3},{4,20},{20... | collective-permute-start | bytes 2162696 | tf_op jit(solution)/shard_map/ppermute | solution.py:459
  79.0 35.2 %copy-start.18 = (f32[1024,256]{1,0:T(8,128)S(1)}, f32[1024,256]{1,0:T(8,128)}, u32[]{:S(2)}) copy-start(f32[1024,256]{1,0:T(8,128)} %get-tuple-element.53) | copy-start | bytes 3145732
  79.0 8.2 %collective-permute-start.3 = (bf16[352,256]{1,0:T(8,128)(2,1)S(1)}, bf16[352,256]{1,0:T(8,128)(2,1)S(1)}, u32[]{:S(2)}, u32[]{:S(2)}) collective-permute-start(bf16[352,256]{1,0:T(8,128)(2,1)S(1)} %get-tuple-element.81), channel_id=1, source_target_pairs={{0,1},{1,0},{2,3},{3,2},{4,5},{5,4},{6,7},{7,6},{8,9},{9,8},{10,11... | collective-permute-start | bytes 540680 | tf_op jit(solution)/shard_map/ppermute | solution.py:463
  81.9 10.0 %collective-permute-start.5 = (bf16[352,256]{1,0:T(8,128)(2,1)S(1)}, bf16[352,256]{1,0:T(8,128)(2,1)S(1)}, u32[]{:S(2)}, u32[]{:S(2)}) collective-permute-start(bf16[352,256]{1,0:T(8,128)(2,1)S(1)} %get-tuple-element.82), channel_id=1, source_target_pairs={{0,3},{1,2},{2,1},{3,0},{4,7},{5,6},{6,5},{7,4},{8,11},{9,10},{10,... | collective-permute-start | bytes 540680 | tf_op jit(solution)/shard_map/ppermute | solution.py:463
  83.4 10.0 %collective-permute-start.4 = (bf16[352,256]{1,0:T(8,128)(2,1)S(1)}, bf16[352,256]{1,0:T(8,128)(2,1)}, u32[]{:S(2)}, u32[]{:S(2)}) collective-permute-start(bf16[352,256]{1,0:T(8,128)(2,1)S(1)} %get-tuple-element.83), channel_id=1, source_target_pairs={{0,2},{1,3},{2,0},{3,1},{4,6},{5,7},{6,4},{7,5},{8,10},{9,11},{10,... | collective-permute-start | bytes 540680 | tf_op jit(solution)/shard_map/ppermute | solution.py:463
  94.4 4.6 %collective-permute-start.6 = (bf16[176,256]{1,0:T(8,128)(2,1)S(1)}, bf16[176,256]{1,0:T(8,128)(2,1)S(1)}, u32[]{:S(2)}, u32[]{:S(2)}) collective-permute-start(bf16[176,256]{1,0:T(8,128)(2,1)S(1)} %broadcast_select_fusion), channel_id=1, source_target_pairs={{0,4},{1,5},{2,6},{3,7},{4,0},{5,1},{6,2},{7,3},{8,12},{9,13},{10,... | collective-permute-start | bytes 270344 | tf_op jit(solution)/shard_map/ppermute | solution.py:463
  96.1 10.4 %collective-permute-start.1 = (bf16[1024,256]{1,0:T(8,128)(2,1)}, bf16[1024,256]{1,0:T(8,128)(2,1)S(1)}, u32[]{:S(2)}, u32[]{:S(2)}) collective-permute-start(bf16[1024,256]{1,0:T(8,128)(2,1)} %get-tuple-element.54), channel_id=1, source_target_pairs={{0,16},{16,0},{1,17},{17,1},{2,18},{18,2},{3,19},{19,3},{4,20},{20... | collective-permute-start | bytes 1572872 | tf_op jit(solution)/shard_map/ppermute | solution.py:459
  99.1 6.9 %collective-permute-start.7 = (bf16[176,256]{1,0:T(8,128)(2,1)S(1)}, bf16[176,256]{1,0:T(8,128)(2,1)S(1)}, u32[]{:S(2)}, u32[]{:S(2)}) collective-permute-start(bf16[176,256]{1,0:T(8,128)(2,1)S(1)} %add_convert_fusion.1), channel_id=1, source_target_pairs={{0,8},{1,9},{2,10},{3,11},{4,12},{5,13},{6,14},{7,15},{8,0},{9,1},... | collective-permute-start | bytes 270344 | tf_op jit(solution)/shard_map/ppermute | solution.py:463
  106.0 4.6 %collective-permute-start.8 = (bf16[176,256]{1,0:T(8,128)(2,1)S(1)}, bf16[176,256]{1,0:T(8,128)(2,1)S(1)}, u32[]{:S(2)}, u32[]{:S(2)}) collective-permute-start(bf16[176,256]{1,0:T(8,128)(2,1)S(1)} %add_convert_fusion), channel_id=1, source_target_pairs={{0,4},{1,5},{2,6},{3,7},{4,0},{5,1},{6,2},{7,3},{8,12},{9,13},{10,... | collective-permute-start | bytes 270344 | tf_op jit(solution)/shard_map/ppermute | solution.py:463
  110.6 8.6 %copy-start.11 = (f32[1,256,256]{2,1,0:T(8,128)S(1)}, f32[1,256,256]{2,1,0:T(8,128)}, u32[]{:S(2)}) copy-start(f32[1,256,256]{2,1,0:T(8,128)} %refs_18_.1) | copy-start | bytes 786436
  110.6 6.6 %collective-permute-start.11 = (bf16[352,256]{1,0:T(8,128)(2,1)S(1)}, bf16[352,256]{1,0:T(8,128)(2,1)S(1)}, u32[]{:S(2)}, u32[]{:S(2)}) collective-permute-start(bf16[352,256]{1,0:T(8,128)(2,1)S(1)} %maximum_select_fusion.1.refs_0_), channel_id=1, source_target_pairs={{0,3},{1,2},{2,1},{3,0},{4,7},{5,6},{6,5},{7,4},{8,11},{9,10},{10,... | collective-permute-start | bytes 540680 | tf_op jit(solution)/shard_map/ppermute | solution.py:463
  112.1 6.9 %collective-permute-start.10 = (bf16[352,256]{1,0:T(8,128)(2,1)S(1)}, bf16[352,256]{1,0:T(8,128)(2,1)S(1)}, u32[]{:S(2)}, u32[]{:S(2)}) collective-permute-start(bf16[352,256]{1,0:T(8,128)(2,1)S(1)} %maximum_select_fusion.1.refs_0_), channel_id=1, source_target_pairs={{0,2},{1,3},{2,0},{3,1},{4,6},{5,7},{6,4},{7,5},{8,10},{9,11},{10,... | collective-permute-start | bytes 540680 | tf_op jit(solution)/shard_map/ppermute | solution.py:463
  113.7 5.5 %collective-permute-start.9 = (bf16[352,256]{1,0:T(8,128)(2,1)S(1)}, bf16[352,256]{1,0:T(8,128)(2,1)S(1)}, u32[]{:S(2)}, u32[]{:S(2)}) collective-permute-start(bf16[352,256]{1,0:T(8,128)(2,1)S(1)} %maximum_select_fusion.1.refs_0_), channel_id=1, source_target_pairs={{0,1},{1,0},{2,3},{3,2},{4,5},{5,4},{6,7},{7,6},{8,9},{9,8},{10,11... | collective-permute-start | bytes 540680 | tf_op jit(solution)/shard_map/ppermute | solution.py:463
  114.2 5.0 %copy-start = (f32[1,256,601]{1,0,2:T(1,128)S(1)}, f32[1,256,601]{1,0,2:T(1,128)}, u32[]{:S(2)}) copy-start(f32[1,256,601]{1,0,2:T(1,128)} %param.41) | copy-start | bytes 1846276
  114.2 5.0 %copy-start.1 = (f32[1,256,256]{2,1,0:T(8,128)S(1)}, f32[1,256,256]{2,1,0:T(8,128)}, u32[]{:S(2)}) copy-start(f32[1,256,256]{2,1,0:T(8,128)} %refs_7_.1) | copy-start | bytes 786436
  114.2 5.0 %copy-start.2 = (f32[1,256,256]{2,1,0:T(8,128)S(1)}, f32[1,256,256]{2,1,0:T(8,128)}, u32[]{:S(2)}) copy-start(f32[1,256,256]{2,1,0:T(8,128)} %refs_13_.1) | copy-start | bytes 786436
  114.2 5.0 %copy-start.3 = (f32[1,256,256]{2,1,0:T(8,128)S(1)}, f32[1,256,256]{2,1,0:T(8,128)}, u32[]{:S(2)}) copy-start(f32[1,256,256]{2,1,0:T(8,128)} %refs_16_.1) | copy-start | bytes 786436
  114.2 5.0 %copy-start.4 = (f32[1,256,601]{1,0,2:T(1,128)S(1)}, f32[1,256,601]{1,0,2:T(1,128)}, u32[]{:S(2)}) copy-start(f32[1,256,601]{1,0,2:T(1,128)} %param.42) | copy-start | bytes 1846276
  114.2 5.0 %copy-start.5 = (f32[1,256,601]{1,0,2:T(1,128)S(1)}, f32[1,256,601]{1,0,2:T(1,128)}, u32[]{:S(2)}) copy-start(f32[1,256,601]{1,0,2:T(1,128)} %param.43) | copy-start | bytes 1846276
  114.2 5.0 %copy-start.6 = (f32[1,256,256]{2,1,0:T(8,128)S(1)}, f32[1,256,256]{2,1,0:T(8,128)}, u32[]{:S(2)}) copy-start(f32[1,256,256]{2,1,0:T(8,128)} %refs_8_.1) | copy-start | bytes 786436
  114.2 5.0 %copy-start.7 = (f32[1,256,256]{2,1,0:T(8,128)S(1)}, f32[1,256,256]{2,1,0:T(8,128)}, u32[]{:S(2)}) copy-start(f32[1,256,256]{2,1,0:T(8,128)} %refs_9_.1) | copy-start | bytes 786436
  114.3 5.0 %copy-start.8 = (f32[1,256,256]{2,1,0:T(8,128)S(1)}, f32[1,256,256]{2,1,0:T(8,128)}, u32[]{:S(2)}) copy-start(f32[1,256,256]{2,1,0:T(8,128)} %refs_14_.1) | copy-start | bytes 786436
  114.3 5.0 %copy-start.9 = (f32[1,256,256]{2,1,0:T(8,128)S(1)}, f32[1,256,256]{2,1,0:T(8,128)}, u32[]{:S(2)}) copy-start(f32[1,256,256]{2,1,0:T(8,128)} %refs_15_.1) | copy-start | bytes 786436
  114.3 5.0 %copy-start.10 = (f32[1,256,256]{2,1,0:T(8,128)S(1)}, f32[1,256,256]{2,1,0:T(8,128)}, u32[]{:S(2)}) copy-start(f32[1,256,256]{2,1,0:T(8,128)} %refs_17_.1) | copy-start | bytes 786436
  114.3 5.0 %copy-start.12 = (f32[1,32,256]{2,1,0:T(8,128)S(1)}, f32[1,32,256]{2,1,0:T(8,128)}, u32[]{:S(2)}) copy-start(f32[1,32,256]{2,1,0:T(8,128)} %refs_4_.1) | copy-start | bytes 98308
  114.3 5.0 %copy-start.13 = (f32[1,32,256]{2,1,0:T(8,128)S(1)}, f32[1,32,256]{2,1,0:T(8,128)}, u32[]{:S(2)}) copy-start(f32[1,32,256]{2,1,0:T(8,128)} %refs_5_.1) | copy-start | bytes 98308
  114.3 5.0 %copy-start.14 = (f32[1,32,256]{2,1,0:T(8,128)S(1)}, f32[1,32,256]{2,1,0:T(8,128)}, u32[]{:S(2)}) copy-start(f32[1,32,256]{2,1,0:T(8,128)} %refs_6_.1) | copy-start | bytes 98308
  114.3 5.0 %copy-start.15 = (f32[1,2,256]{2,1,0:T(2,128)S(1)}, f32[1,2,256]{2,1,0:T(2,128)}, u32[]{:S(2)}) copy-start(f32[1,2,256]{2,1,0:T(2,128)} %refs_10_.1) | copy-start | bytes 6148
  114.3 5.0 %copy-start.16 = (f32[1,2,256]{2,1,0:T(2,128)S(1)}, f32[1,2,256]{2,1,0:T(2,128)}, u32[]{:S(2)}) copy-start(f32[1,2,256]{2,1,0:T(2,128)} %refs_11_.1) | copy-start | bytes 6148
  114.4 5.0 %copy-start.17 = (f32[1,2,256]{2,1,0:T(2,128)S(1)}, f32[1,2,256]{2,1,0:T(2,128)}, u32[]{:S(2)}) copy-start(f32[1,2,256]{2,1,0:T(2,128)} %refs_12_.1) | copy-start | bytes 6148

commit v5 on v4

--- a/solution.py
+++ b/solution.py
@@ -20,7 +20,9 @@
 LANES = 128
 TILE = 16
 BITS = 24
-FIRST, SECOND = 4, 4
+FIRST, SECOND, HOLD_AT, BACK_FIRST = 4, 4, 1, 0
+CHUNK_ONE, CHUNK_TWO, CHUNK_HEAD, CHUNK_BACK, CHUNK_COPY = 64, 64, 64, 64, 64
+LOGITS_FIRST = False
 SPARE = 7
 STEPS = 4
 SMALL = 16 * 1024 * 1024
@@ -123,15 +125,20 @@
                   w_cat, w_up, w_down, w_head, gains,
                   g_cat, g_up, g_down, g_head, g_gain,
                   meta, picks, low_state, unit_one, slope_one, unit_two, slope_two, active_now, normed_now, active, normed,
-                  scale_one, scale_two, head_part, turned, turned_pick, logits_all, logit_grads, pre_grads, back):
-    branch_grads = tuple(low_state.at[slot, : latent.shape[0]] for slot in range(2))
+                  scale_one, scale_two, head_part, turned, turned_pick, logits_all, logit_grads, pre_pair, back):
+    branch_grads = (low_state.at[0], low_state.at[1])
     inner_grads = (active_now, normed_now)
+    pre_grads = (pre_pair.at[0], pre_pair.at[1])
     rows, width = latent.shape
     wide = lay.wide
     part = 1.0 / width
     section = which[0]
-    chunks = [slice(at, at + chunk) for at in range(0, rows, chunk)]
-    weight_of = chunk / 8
+    def cut(size):
+        return [slice(at, at + size) for at in range(0, rows, size)]
+
+    chunks_one, chunks_two, chunks_head, chunks_back, chunks_copy = (
+        cut(size) for size in (CHUNK_ONE, CHUNK_TWO, CHUNK_HEAD, CHUNK_BACK, CHUNK_COPY)
+    )
 
     @pl.when(pl.program_id(0) == 0)
     def start():
@@ -173,31 +180,31 @@
     def forward(step, tower):
         at = 2 * step + tower
         yield "m1"
-        pre = dot(jnp.concatenate([low_state[tower, :rows], picks[at]], axis=1), w_cat[tower])
-        for where in chunks:
+        pre = dot(picks[at], w_cat[tower, width:]) + dot(low_state[tower, :rows], w_cat[tower, :width])
+        for where in chunks_one:
             yield "v1"
             unit, scale = normalise(pre[where])
             unit_one[at, where, :] = unit
-            scale_one[at, where, :] = jnp.broadcast_to(scale, (chunk, LANES))
+            scale_one[at, where, :] = jnp.broadcast_to(scale, (CHUNK_ONE, LANES))
             hidden, slope = gelu_and_slope(unit * gains[tower, 0:1, :])
             slope_one[at, where, :] = slope
             head_part[at, where, :] = hidden
             unit, scale = normalise(hidden)
             unit_two[at, where, :] = unit
-            scale_two[at, where, :] = jnp.broadcast_to(scale, (chunk, LANES))
+            scale_two[at, where, :] = jnp.broadcast_to(scale, (CHUNK_ONE, LANES))
             normed_now[where, :] = (unit * gains[tower, 1:2, :]).astype(BF16)
         yield "m2"
-        inner = dot(normed_now[...], w_up[tower])
-        normed[at] = normed_now[...].T
-        for where in chunks:
+        inner = dot(normed_now[:rows, :], w_up[tower])
+        normed[at] = normed_now[:rows, :].T
+        for where in chunks_two:
             yield "v2"
             result, slope = gelu_and_slope(inner[where])
             slope_two[at, where, :] = slope
             active_now[where, :] = result.astype(BF16)
         yield "m3"
-        branch = dot(active_now[...], w_down[tower])
-        active[at] = active_now[...].T
-        for where in chunks:
+        branch = dot(active_now[:rows, :], w_down[tower])
+        active[at] = active_now[:rows, :].T
+        for where in chunks_two:
             yield "v3"
             state = head_part[at, where, :] + branch[where]
             low_state[1 - tower, where, :] = state.astype(BF16)
@@ -220,13 +227,13 @@
     def head_logits(step, tower):
         yield "M", 5 * rows / 8
         logits = dot_right_t(low_state[1 - tower, :rows], w_head[tower])
-        for where in chunks:
-            yield "V", weight_of
+        for where in chunks_copy:
+            yield "V", 1
             logits_all[tower, where, :] = logits[where]
 
     def head_softmax(step, tower):
-        for where in chunks:
-            yield "V", 14 * weight_of
+        for where in chunks_head:
+            yield "V", 14 * 1
             some = logits_all[tower, where, :]
             some = jnp.concatenate(
                 [some[:, :whole_lanes], jnp.where(inside, some[:, whole_lanes:], -1e30)], axis=1
@@ -240,8 +247,8 @@
         at = 2 * step + tower
         yield "M", 5 * rows / 8
         pulled = dot(logit_grads[tower, :rows], w_head[tower])
-        for where in chunks:
-            yield "V", weight_of
+        for where in chunks_copy:
+            yield "V", 1
             head_part[at, where, :] = pulled[where]
         yield "M", 5 * rows / 8
         some = dot(turned[at + 1], logit_grads[tower, :rows])
@@ -250,7 +257,7 @@
 
     def tick(step, tower, stages="flsp"):
         at = 2 * step + tower
-        count = len(chunks)
+        count, later = len(chunks_one), len(chunks_two)
         streams = {}
         if "f" in stages:
             streams["f"] = forward(step, tower)
@@ -275,12 +282,14 @@
         first, second = FIRST, SECOND
         go("f")
         go("s", first)
-        go("f")
+        go("f", HOLD_AT)
         if "p" in stages:
             hold_low(logit_grads, 1 - tower, unit_one.at[at], 0)
         if "l" in stages:
             hold_low(low_state, tower, unit_one.at[at], 0)
-        for turn in range(1, count):
+        if LOGITS_FIRST:
+            go("l", 100)
+        for turn in range(HOLD_AT, count):
             go("f")
             if turn % 2 == 1:
                 go("p")
@@ -291,7 +300,7 @@
             hold_logits(tower, unit_two.at[at], rows - 8)
         go("f")
         go("s", second)
-        go("f", count)
+        go("f", later)
         if "s" in stages:
             hold_logits(tower, slope_two.at[at], rows - 8)
         go("f")
@@ -317,20 +326,20 @@
 
     def backward(step, tower):
         at = 2 * step + tower
-        for where in chunks:
-            yield "V", weight_of
+        for where in chunks_back:
+            yield "V", 1
             state_grad = head_part[at, where, :] + back[where, :].astype(F32)
             head_part[at, where, :] = state_grad
             branch_grads[tower][where, :] = state_grad.astype(BF16)
         yield "M", rows / 4
-        active_grad = dot_right_t(branch_grads[tower][...], w_down[tower])
-        for where in chunks:
-            yield "V", weight_of
+        active_grad = dot_right_t(branch_grads[tower][:rows, :], w_down[tower])
+        for where in chunks_back:
+            yield "V", 1
             inner_grads[tower][where, :] = (active_grad[where] * slope_two[at, where, :]).astype(BF16)
         yield "M", rows / 4
-        normed_grad = dot_right_t(inner_grads[tower][...], w_up[tower])
-        for where in chunks:
-            yield "V", 12.5 * weight_of
+        normed_grad = dot_right_t(inner_grads[tower][:rows, :], w_up[tower])
+        for where in chunks_back:
+            yield "V", 12.5 * 1
             unit = unit_two[at, where, :]
             scaled = normed_grad[where] * gains[tower, 1:2, :]
             first = row_sum(scaled) * part
@@ -339,41 +348,56 @@
             out_grad = hidden_grad * slope_one[at, where, :]
             unit = unit_one[at, where, :]
             product = out_grad * unit
-            g_gain[tower] += jnp.sum(product.reshape(chunk // 8, 8, width), axis=0)
+            g_gain[tower] += jnp.sum(product.reshape(CHUNK_BACK // 8, 8, width), axis=0)
             gain = gains[tower, 0:1, :]
             scaled = out_grad * gain
             first = row_sum(scaled) * part
             second = row_sum(product * gain) * part
-            pre_grads[tower, where, :] = (
+            pre_grads[tower][where, :] = (
                 (scaled - first - unit * second) * both(scale_one[at, where, :])
             ).astype(BF16)
         yield "M", rows / 4
-        input_grad = dot_right_t(pre_grads[tower], w_cat[tower, :width])
-        for where in chunks:
-            yield "V", 0.5 * weight_of
+        input_grad = dot_right_t(pre_grads[tower][:rows, :], w_cat[tower, :width])
+        for where in chunks_back:
+            yield "V", 0.5 * 1
             back[where, :] = input_grad[where].astype(BF16)
 
     def weight_grads(step, tower):
         at = 2 * step + tower
         for left, right, total in ((active, branch_grads, g_down), (normed, inner_grads, g_up)):
             yield "M", rows / 4 + 20
-            some = dot(left[at], right[tower][...])
+            some = dot(left[at], right[tower][:rows, :])
             yield "V", 32
             total[tower] += some
         yield "M", rows / 4 + 40
-        some = dot(jnp.concatenate([turned[at], turned_pick[at]], axis=0), pre_grads[tower])
+        some = dot(jnp.concatenate([turned[at], turned_pick[at]], axis=0), pre_grads[tower][:rows, :])
         yield "V", 36
         g_cat[tower] += some
 
     back[...] = jnp.zeros_like(back)
-    for ref in (branch_grads[0], inner_grads[0], pre_grads.at[0]):
-        ref[...] = jnp.zeros((rows, width), BF16)
+    for ref in (branch_grads[0], inner_grads[0], pre_grads[0]):
+        ref[:rows, :] = jnp.zeros((rows, width), BF16)
+
+    def back_tick(step, tower, before):
+        at = 2 * step + tower
+        chain = backward(step, tower)
+        next(chain)
+        products = weight_grads(before, 1 - tower)
+        next(products)
+        for _ in range(2 * len(chunks_back) + 2 + BACK_FIRST):
+            next(chain)
+        spot = pl.multiple_of(rows + TILE * section, TILE)
+        for ref in (branch_grads, inner_grads, pre_grads):
+            ref[1 - tower][pl.ds(spot, TILE), :LANES] = unit_two[at, :TILE, :LANES].astype(BF16)
+        for _ in products:
+            next(chain, None)
+        for _ in chain:
+            pass
 
     def backward_step(turn, carry):
         step = steps - 1 - turn
-        later = jnp.minimum(step + 1, steps - 1)
-        interleave([backward(step, 1), weight_grads(later, 0)])
-        interleave([backward(step, 0), weight_grads(step, 1)])
+        back_tick(step, 1, jnp.minimum(step + 1, steps - 1))
+        back_tick(step, 0, step)
         return carry
 
     lax.fori_loop(0, steps, backward_step, 0)
@@ -505,7 +529,6 @@
     square = (2, width, width)
     per_tick = (ticks, block, width)
     narrow = (ticks, block, LANES)
-    pair = (2, block, width)
     keep, send, ends_mine, ends_send = pl.pallas_call(
         functools.partial(towers_kernel, lay, steps, chunk),
         grid_spec=pltpu.PrefetchScalarGridSpec(
@@ -544,8 +567,8 @@
                 pltpu.VMEM(per_tick, F32),
                 pltpu.VMEM(per_tick, F32),
                 pltpu.VMEM(per_tick, F32),
-                pltpu.VMEM((block, width), BF16),
-                pltpu.VMEM((block, width), BF16),
+                pltpu.VMEM((block + 2 * TILE, width), BF16),
+                pltpu.VMEM((block + 2 * TILE, width), BF16),
                 pltpu.VMEM((ticks, width, block), BF16),
                 pltpu.VMEM((ticks, width, block), BF16),
                 pltpu.VMEM(narrow, F32),
@@ -555,7 +578,7 @@
                 pltpu.VMEM((ticks, lay.codes, block), BF16),
                 pltpu.VMEM((2, block + TILE, lay.wide), F32),
                 pltpu.VMEM((2, block + 2 * TILE, lay.wide), BF16),
-                pltpu.VMEM(pair, BF16),
+                pltpu.VMEM((2, block + 2 * TILE, width), BF16),
                 pltpu.VMEM((block, width), BF16),
             ],
         ),
@@ -574,13 +597,13 @@
     in_smem = pl.BlockSpec(memory_space=pltpu.SMEM)
 
     part_shape = (lay.rows // parts, width)
-    both = keep.astype(F32) + swap(send).astype(F32)
+    both = lax.optimization_barrier(keep.astype(F32)) + swap(send).astype(F32)
     both = lax.optimization_barrier(both.reshape(parts, *part_shape))
 
     def part_for(mask):
         return lax.dynamic_index_in_dim(both, place[0] ^ mask, 0, keepdims=False)
 
-    own = part_for(0)
+    own = lax.optimization_barrier(part_for(0))
     others = [part_for(mask).astype(BF16) for mask in range(1, parts)]
     current = own
     for arrived in [across(other, mask, length) for mask, other in enumerate(others, 1)]:

time: 124 us -> 121 us (0.976)
  waiting for transfers between devices: 27.7 us -> 26.3 us
  transfers between devices with their start and end apart: 12 -> 12, of which waited for: 11 -> 11; matrix products, arithmetic and copies ran while one was open for 1% -> 2% of each run, Pallas kernels for 0% -> 0%
where the time goes in v5:
time: 121 us; the launch traced here: 120 us
  Pallas kernels  74.2 us (61%)
  waiting for transfers between devices  26.3 us (22%)
  starting transfers between devices  14.4 us (12%)
  other arithmetic  3.27 us (3%)
    pallas_call x1, Pallas kernels, on_device(): pl.pallas_call(functools.partial(towers_kernel, lay, steps, chunk), grid_...  68 us
    ppermute x9, waiting for transfers between devices, across(): return lax.ppermute(array, 'dp', [(i, i ^ mask) for i in range(length)])  23.4 us
    ppermute x9, starting transfers between devices, across(): return lax.ppermute(array, 'dp', [(i, i ^ mask) for i in range(length)])  13.5 us
    pallas_call x1, Pallas kernels, on_device(): pl.pallas_call(functools.partial(update_kernel, lay, parts), in_specs=[in...  3.82 us
    ppermute x3, waiting for transfers between devices, swap(): return lax.ppermute(value, 'section', [(0, 1), (1, 0)])  2.84 us
    pallas_call x1, Pallas kernels, on_device(): pl.pallas_call(functools.partial(pack_kernel, lay), out_shape=jax.ShapeDt...  2.45 us
  transfers between devices with their start and end apart: 12, of which 11 were waited for; matrix products, arithmetic and copies ran while one was open for 2% of the time, Pallas kernels for 0%

profile of v5, /device:TPU:0, one launch (start us, length us, event | category | flops | bytes accessed | tf_op | source)
XLA Modules:
  0.0 120.4 jit_solution(14424487697275225846)
XLA Ops:
  0.7 2.5 %pack.1.mine = bf16[1408,256]{1,0:T(8,128)(2,1)} custom-call(f32[1,32,256]{2,1,0:T(8,128)} %refs_4_.1, f32[1,256,256]{2,1,0:T(8,128)} %refs_7_.1, f32[1,256,256]{2,1,0:T(8,128)} %refs_13_.1, f32[1,256,256]{2,1,0:T(8,128)} %refs_16_.1, f32[601,1,256]{2,1,0:T(1,128)} %bitcast.24, f32[1,2,256]{2,1,0:T(2,128)} %refs_10_.1), custom_call_target="tpu_custom_call" | custom-call | tf_op jit(solution)/shard_map/pack/pallas_call | solution.py:505
  3.1 0.5 collective-permute-start
  3.6 2.0 %collective-permute-done.theirs = bf16[1408,256]{1,0:T(8,128)(2,1)S(1)} collective-permute-done((bf16[1408,256]{1,0:T(8,128)(2,1)}, bf16[1408,256]{1,0:T(8,128)(2,1)S(1)}, u32[]{:S(2)}, u32[]{:S(2)}) %collective-permute-start) | collective-permute-done | bytes 720928 | tf_op jit(solution)/shard_map/ppermute | solution.py:483
  5.6 0.9 copy-done.19
  6.5 68.0 %towers.1 = (bf16[1408,256]{1,0:T(8,128)(2,1)}, bf16[1408,256]{1,0:T(8,128)(2,1)}, f32[1024,256]{1,0:T(8,128)}, bf16[1024,256]{1,0:T(8,128)(2,1)}) custom-call(s32[1]{0:T(128)} %bitcast.which, bf16[2048,256]{1,0:T(8,128)(2,1)} %latent.1, s32[5,2,2048]{2,1,0:T(2,128)} %bitcast.31, s32[5,2,2048]{2,1,0:T(2,128)} %bitcast.32, s32[5,2048]{1,0:T(8,128)} %whole_valid.1, ...), custom_call_target="tpu_custom_call" | custom-call | tf_op jit(solution)/shard_map/towers/pallas_call | solution.py:532
  74.4 0.4 collective-permute-start.2
  74.8 1.2 %convert_element_type.55 = f32[1408,256]{1,0:T(8,128)S(1)} convert(bf16[1408,256]{1,0:T(8,128)(2,1)} %get-tuple-element.55) | non-fusion elementwise | flops 360448 | bytes 2162688 | tf_op jit(solution)/shard_map/convert_element_type | solution.py:600
  76.1 0.8 collective-permute-done.2
  76.9 0.2 convert_add_fusion
  77.1 0.0 copy-start.20
  77.1 0.1 fusion
  77.2 2.9 %collective-permute-start.3 = (bf16[352,256]{1,0:T(8,128)(2,1)S(1)}, bf16[352,256]{1,0:T(8,128)(2,1)S(1)}, u32[]{:S(2)}, u32[]{:S(2)}) collective-permute-start(bf16[352,256]{1,0:T(8,128)(2,1)S(1)} %get-tuple-element.81), channel_id=1, source_target_pairs={{0,1},{1,0},{2,3},{3,2},{4,5},{5,4},{6,7},{7,6},{8,9},{9,8},{10,11... | collective-permute-start | bytes 540680 | tf_op jit(solution)/shard_map/ppermute | solution.py:487
  80.1 1.5 %collective-permute-start.5 = (bf16[352,256]{1,0:T(8,128)(2,1)S(1)}, bf16[352,256]{1,0:T(8,128)(2,1)S(1)}, u32[]{:S(2)}, u32[]{:S(2)}) collective-permute-start(bf16[352,256]{1,0:T(8,128)(2,1)S(1)} %get-tuple-element.82), channel_id=1, source_target_pairs={{0,3},{1,2},{2,1},{3,0},{4,7},{5,6},{6,5},{7,4},{8,11},{9,10},{10,... | collective-permute-start | bytes 540680 | tf_op jit(solution)/shard_map/ppermute | solution.py:487
  81.6 0.0 collective-permute-start.4
  81.6 0.0 copy-start.18
  81.7 3.8 %collective-permute-done.3 = bf16[352,256]{1,0:T(8,128)(2,1)S(1)} collective-permute-done((bf16[352,256]{1,0:T(8,128)(2,1)S(1)}, bf16[352,256]{1,0:T(8,128)(2,1)S(1)}, u32[]{:S(2)}, u32[]{:S(2)}) %collective-permute-start.3) | collective-permute-done | bytes 180256 | tf_op jit(solution)/shard_map/ppermute | solution.py:487
  85.4 4.7 %collective-permute-done.5 = bf16[352,256]{1,0:T(8,128)(2,1)S(1)} collective-permute-done((bf16[352,256]{1,0:T(8,128)(2,1)S(1)}, bf16[352,256]{1,0:T(8,128)(2,1)S(1)}, u32[]{:S(2)}, u32[]{:S(2)}) %collective-permute-start.5) | collective-permute-done | bytes 180256 | tf_op jit(solution)/shard_map/ppermute | solution.py:487
  90.1 1.4 %collective-permute-done.4 = bf16[352,256]{1,0:T(8,128)(2,1)S(1)} collective-permute-done((bf16[352,256]{1,0:T(8,128)(2,1)S(1)}, bf16[352,256]{1,0:T(8,128)(2,1)S(1)}, u32[]{:S(2)}, u32[]{:S(2)}) %collective-permute-start.4) | collective-permute-done | bytes 180256 | tf_op jit(solution)/shard_map/ppermute | solution.py:487
  91.5 0.1 add_convert_fusion
  91.6 1.6 %collective-permute-start.6 = (bf16[176,256]{1,0:T(8,128)(2,1)S(1)}, bf16[176,256]{1,0:T(8,128)(2,1)S(1)}, u32[]{:S(2)}, u32[]{:S(2)}) collective-permute-start(bf16[176,256]{1,0:T(8,128)(2,1)S(1)} %broadcast_select_fusion), channel_id=1, source_target_pairs={{0,4},{1,5},{2,6},{3,7},{4,0},{5,1},{6,2},{7,3},{8,12},{9,13},{10,... | collective-permute-start | bytes 270344 | tf_op jit(solution)/shard_map/ppermute | solution.py:487
  93.2 0.0 copy-done.20
  93.2 0.0 collective-permute-start.1
  93.2 3.0 %collective-permute-done.6 = bf16[176,256]{1,0:T(8,128)(2,1)S(1)} collective-permute-done((bf16[176,256]{1,0:T(8,128)(2,1)S(1)}, bf16[176,256]{1,0:T(8,128)(2,1)S(1)}, u32[]{:S(2)}, u32[]{:S(2)}) %collective-permute-start.6) | collective-permute-done | bytes 90144 | tf_op jit(solution)/shard_map/ppermute | solution.py:487
  96.2 3.3 %collective-permute-start.7 = (bf16[176,256]{1,0:T(8,128)(2,1)S(1)}, bf16[176,256]{1,0:T(8,128)(2,1)S(1)}, u32[]{:S(2)}, u32[]{:S(2)}) collective-permute-start(bf16[176,256]{1,0:T(8,128)(2,1)S(1)} %add_convert_fusion.2), channel_id=1, source_target_pairs={{0,8},{1,9},{2,10},{3,11},{4,12},{5,13},{6,14},{7,15},{8,0},{9,1},... | collective-permute-start | bytes 270344 | tf_op jit(solution)/shard_map/ppermute | solution.py:487
  99.5 3.5 %collective-permute-done.7 = bf16[176,256]{1,0:T(8,128)(2,1)S(1)} collective-permute-done((bf16[176,256]{1,0:T(8,128)(2,1)S(1)}, bf16[176,256]{1,0:T(8,128)(2,1)S(1)}, u32[]{:S(2)}, u32[]{:S(2)}) %collective-permute-start.7) | collective-permute-done | bytes 90144 | tf_op jit(solution)/shard_map/ppermute | solution.py:487
  103.0 0.5 collective-permute-start.8
  103.6 0.0 collective-permute-done.1
  103.6 0.1 bitcast_convert_fusion
  103.7 4.0 %collective-permute-done.8 = bf16[176,256]{1,0:T(8,128)(2,1)S(1)} collective-permute-done((bf16[176,256]{1,0:T(8,128)(2,1)S(1)}, bf16[176,256]{1,0:T(8,128)(2,1)S(1)}, u32[]{:S(2)}, u32[]{:S(2)}) %collective-permute-start.8) | collective-permute-done | bytes 90144 | tf_op jit(solution)/shard_map/ppermute | solution.py:487
  107.6 0.1 maximum_select_fusion.1.refs_0_
  107.7 1.5 %collective-permute-start.11 = (bf16[352,256]{1,0:T(8,128)(2,1)S(1)}, bf16[352,256]{1,0:T(8,128)(2,1)S(1)}, u32[]{:S(2)}, u32[]{:S(2)}) collective-permute-start(bf16[352,256]{1,0:T(8,128)(2,1)S(1)} %maximum_select_fusion.1.refs_0_), channel_id=1, source_target_pairs={{0,3},{1,2},{2,1},{3,0},{4,7},{5,6},{6,5},{7,4},{8,11},{9,10},{10,... | collective-permute-start | bytes 540680 | tf_op jit(solution)/shard_map/ppermute | solution.py:487
  109.2 1.5 %collective-permute-start.10 = (bf16[352,256]{1,0:T(8,128)(2,1)S(1)}, bf16[352,256]{1,0:T(8,128)(2,1)S(1)}, u32[]{:S(2)}, u32[]{:S(2)}) collective-permute-start(bf16[352,256]{1,0:T(8,128)(2,1)S(1)} %maximum_select_fusion.1.refs_0_), channel_id=1, source_target_pairs={{0,2},{1,3},{2,0},{3,1},{4,6},{5,7},{6,4},{7,5},{8,10},{9,11},{10,... | collective-permute-start | bytes 540680 | tf_op jit(solution)/shard_map/ppermute | solution.py:487
  110.7 0.5 collective-permute-start.9
  111.3 0.0 copy-done.18
  111.3 0.0 copy-start.3
  111.3 0.0 copy-start.4
  111.3 0.0 copy-start.5
  111.3 0.0 copy-start.6
  111.3 0.0 copy-start.7
  111.3 0.0 copy-start.8
  111.3 0.0 copy-start.9
  111.4 0.0 copy-start.10
  111.4 0.0 copy-start.12
  111.4 0.0 copy-start.13
  111.4 0.0 copy-start.14
  111.4 0.0 copy-start.15
  111.4 0.0 copy-start.16
  111.4 0.0 copy-start.17
  111.4 1.6 %maximum_select_fusion = f32[1,2048,256]{2,1,0:T(8,128)} fusion(f32[1,1024,256]{2,1,0:T(8,128)S(1)} %bitcast_convert_fusion, f32[1,1024,256]{2,1,0:T(8,128)S(1)} %bitcast.30, pred[]{:T(512)S(6)} %eq.11), kind=kLoop, calls=%fused_computation | loop fusion | flops 1572864 | bytes 4194305 | tf_op jit(solution)/shard_map/jit(_where)/select_n | solution.py:629
  113.0 1.3 %collective-permute-done.11.refs_3_ = bf16[352,256]{1,0:T(8,128)(2,1)S(1)} collective-permute-done((bf16[352,256]{1,0:T(8,128)(2,1)S(1)}, bf16[352,256]{1,0:T(8,128)(2,1)S(1)}, u32[]{:S(2)}, u32[]{:S(2)}) %collective-permute-start.11) | collective-permute-done | bytes 180256 | tf_op jit(solution)/shard_map/ppermute | solution.py:487
  114.3 1.8 %collective-permute-done.10.refs_2_ = bf16[352,256]{1,0:T(8,128)(2,1)S(1)} collective-permute-done((bf16[352,256]{1,0:T(8,128)(2,1)S(1)}, bf16[352,256]{1,0:T(8,128)(2,1)S(1)}, u32[]{:S(2)}, u32[]{:S(2)}) %collective-permute-start.10) | collective-permute-done | bytes 180256 | tf_op jit(solution)/shard_map/ppermute | solution.py:487
  116.1 0.1 collective-permute-done.9.refs_1_
  116.2 0.0 copy-done.11
  116.2 0.0 copy-done
  116.2 0.0 copy-done.1
  116.2 0.0 copy-done.2
  116.2 0.0 copy-done.3
  116.3 0.0 copy-done.4
  116.3 0.0 copy-done.5
  116.3 0.0 copy-done.6
  116.3 0.0 copy-done.7
  116.3 0.0 copy-done.8
  116.3 0.0 copy-done.9
  116.4 3.8 %update.1 = (f32[1,32,256]{2,1,0:T(8,128)}, f32[1,32,256]{2,1,0:T(8,128)}, f32[1,32,256]{2,1,0:T(8,128)}, bf16[1,32,256]{2,1,0:T(8,128)(2,1)}, f32[1,256,256]{2,...) custom-call(s32[1]{0:T(128)} %bitcast.7.which, ...), custom_call_target="tpu_custom_call" | custom-call | tf_op jit(solution)/shard_map/update/pallas_call | solution.py:640
  (16 shorter events, 0.1 us)
Async XLA Ops:
  3.1 2.5 %collective-permute-start = (bf16[1408,256]{1,0:T(8,128)(2,1)}, bf16[1408,256]{1,0:T(8,128)(2,1)S(1)}, u32[]{:S(2)}, u32[]{:S(2)}) collective-permute-start(bf16[1408,256]{1,0:T(8,128)(2,1)} %pack.1.mine), channel_id=1, source_target_pairs={{0,16},{16,0},{1,17},{17,1},{2,18},{18,2},{3,19},{19,3},{4,20},{20... | collective-permute-start | bytes 2162696 | tf_op jit(solution)/shard_map/ppermute | solution.py:483
  5.6 0.9 copy-start.19
  74.4 2.5 %collective-permute-start.2 = (bf16[1408,256]{1,0:T(8,128)(2,1)}, bf16[1408,256]{1,0:T(8,128)(2,1)S(1)}, u32[]{:S(2)}, u32[]{:S(2)}) collective-permute-start(bf16[1408,256]{1,0:T(8,128)(2,1)} %get-tuple-element.56), channel_id=1, source_target_pairs={{0,16},{16,0},{1,17},{17,1},{2,18},{18,2},{3,19},{19,3},{4,20},{20... | collective-permute-start | bytes 2162696 | tf_op jit(solution)/shard_map/ppermute | solution.py:483
  77.1 16.2 %copy-start.20 = (bf16[1024,256]{1,0:T(8,128)(2,1)S(1)}, bf16[1024,256]{1,0:T(8,128)(2,1)}, u32[]{:S(2)}) copy-start(bf16[1024,256]{1,0:T(8,128)(2,1)} %get-tuple-element.54) | copy-start | bytes 1572868
  77.2 8.3 %collective-permute-start.3 = (bf16[352,256]{1,0:T(8,128)(2,1)S(1)}, bf16[352,256]{1,0:T(8,128)(2,1)S(1)}, u32[]{:S(2)}, u32[]{:S(2)}) collective-permute-start(bf16[352,256]{1,0:T(8,128)(2,1)S(1)} %get-tuple-element.81), channel_id=1, source_target_pairs={{0,1},{1,0},{2,3},{3,2},{4,5},{5,4},{6,7},{7,6},{8,9},{9,8},{10,11... | collective-permute-start | bytes 540680 | tf_op jit(solution)/shard_map/ppermute | solution.py:487
  80.1 10.0 %collective-permute-start.5 = (bf16[352,256]{1,0:T(8,128)(2,1)S(1)}, bf16[352,256]{1,0:T(8,128)(2,1)S(1)}, u32[]{:S(2)}, u32[]{:S(2)}) collective-permute-start(bf16[352,256]{1,0:T(8,128)(2,1)S(1)} %get-tuple-element.82), channel_id=1, source_target_pairs={{0,3},{1,2},{2,1},{3,0},{4,7},{5,6},{6,5},{7,4},{8,11},{9,10},{10,... | collective-permute-start | bytes 540680 | tf_op jit(solution)/shard_map/ppermute | solution.py:487
  81.6 9.9 %collective-permute-start.4 = (bf16[352,256]{1,0:T(8,128)(2,1)S(1)}, bf16[352,256]{1,0:T(8,128)(2,1)S(1)}, u32[]{:S(2)}, u32[]{:S(2)}) collective-permute-start(bf16[352,256]{1,0:T(8,128)(2,1)S(1)} %get-tuple-element.83), channel_id=1, source_target_pairs={{0,2},{1,3},{2,0},{3,1},{4,6},{5,7},{6,4},{7,5},{8,10},{9,11},{10,... | collective-permute-start | bytes 540680 | tf_op jit(solution)/shard_map/ppermute | solution.py:487
  81.6 29.6 %copy-start.18 = (f32[1024,256]{1,0:T(8,128)S(1)}, f32[1024,256]{1,0:T(8,128)}, u32[]{:S(2)}) copy-start(f32[1024,256]{1,0:T(8,128)} %get-tuple-element.53) | copy-start | bytes 3145732
  91.6 4.6 %collective-permute-start.6 = (bf16[176,256]{1,0:T(8,128)(2,1)S(1)}, bf16[176,256]{1,0:T(8,128)(2,1)S(1)}, u32[]{:S(2)}, u32[]{:S(2)}) collective-permute-start(bf16[176,256]{1,0:T(8,128)(2,1)S(1)} %broadcast_select_fusion), channel_id=1, source_target_pairs={{0,4},{1,5},{2,6},{3,7},{4,0},{5,1},{6,2},{7,3},{8,12},{9,13},{10,... | collective-permute-start | bytes 270344 | tf_op jit(solution)/shard_map/ppermute | solution.py:487
  93.2 10.4 %collective-permute-start.1 = (bf16[1024,256]{1,0:T(8,128)(2,1)S(1)}, bf16[1024,256]{1,0:T(8,128)(2,1)S(1)}, u32[]{:S(2)}, u32[]{:S(2)}) collective-permute-start(bf16[1024,256]{1,0:T(8,128)(2,1)S(1)} %copy-done.20), channel_id=1, source_target_pairs={{0,16},{16,0},{1,17},{17,1},{2,18},{18,2},{3,19},{19,3},{4,20},{20... | collective-permute-start | bytes 1572872 | tf_op jit(solution)/shard_map/ppermute | solution.py:483
  96.2 6.8 %collective-permute-start.7 = (bf16[176,256]{1,0:T(8,128)(2,1)S(1)}, bf16[176,256]{1,0:T(8,128)(2,1)S(1)}, u32[]{:S(2)}, u32[]{:S(2)}) collective-permute-start(bf16[176,256]{1,0:T(8,128)(2,1)S(1)} %add_convert_fusion.2), channel_id=1, source_target_pairs={{0,8},{1,9},{2,10},{3,11},{4,12},{5,13},{6,14},{7,15},{8,0},{9,1},... | collective-permute-start | bytes 270344 | tf_op jit(solution)/shard_map/ppermute | solution.py:487
  103.0 4.6 %collective-permute-start.8 = (bf16[176,256]{1,0:T(8,128)(2,1)S(1)}, bf16[176,256]{1,0:T(8,128)(2,1)S(1)}, u32[]{:S(2)}, u32[]{:S(2)}) collective-permute-start(bf16[176,256]{1,0:T(8,128)(2,1)S(1)} %add_convert_fusion.1), channel_id=1, source_target_pairs={{0,4},{1,5},{2,6},{3,7},{4,0},{5,1},{6,2},{7,3},{8,12},{9,13},{10,... | collective-permute-start | bytes 270344 | tf_op jit(solution)/shard_map/ppermute | solution.py:487
  107.6 8.6 %copy-start.11 = (f32[1,256,256]{2,1,0:T(8,128)S(1)}, f32[1,256,256]{2,1,0:T(8,128)}, u32[]{:S(2)}) copy-start(f32[1,256,256]{2,1,0:T(8,128)} %refs_18_.1) | copy-start | bytes 786436
  107.7 6.6 %collective-permute-start.11 = (bf16[352,256]{1,0:T(8,128)(2,1)S(1)}, bf16[352,256]{1,0:T(8,128)(2,1)S(1)}, u32[]{:S(2)}, u32[]{:S(2)}) collective-permute-start(bf16[352,256]{1,0:T(8,128)(2,1)S(1)} %maximum_select_fusion.1.refs_0_), channel_id=1, source_target_pairs={{0,3},{1,2},{2,1},{3,0},{4,7},{5,6},{6,5},{7,4},{8,11},{9,10},{10,... | collective-permute-start | bytes 540680 | tf_op jit(solution)/shard_map/ppermute | solution.py:487
  109.2 6.9 %collective-permute-start.10 = (bf16[352,256]{1,0:T(8,128)(2,1)S(1)}, bf16[352,256]{1,0:T(8,128)(2,1)S(1)}, u32[]{:S(2)}, u32[]{:S(2)}) collective-permute-start(bf16[352,256]{1,0:T(8,128)(2,1)S(1)} %maximum_select_fusion.1.refs_0_), channel_id=1, source_target_pairs={{0,2},{1,3},{2,0},{3,1},{4,6},{5,7},{6,4},{7,5},{8,10},{9,11},{10,... | collective-permute-start | bytes 540680 | tf_op jit(solution)/shard_map/ppermute | solution.py:487
  110.7 5.5 %collective-permute-start.9 = (bf16[352,256]{1,0:T(8,128)(2,1)S(1)}, bf16[352,256]{1,0:T(8,128)(2,1)S(1)}, u32[]{:S(2)}, u32[]{:S(2)}) collective-permute-start(bf16[352,256]{1,0:T(8,128)(2,1)S(1)} %maximum_select_fusion.1.refs_0_), channel_id=1, source_target_pairs={{0,1},{1,0},{2,3},{3,2},{4,5},{5,4},{6,7},{7,6},{8,9},{9,8},{10,11... | collective-permute-start | bytes 540680 | tf_op jit(solution)/shard_map/ppermute | solution.py:487
  111.3 5.0 %copy-start = (f32[1,256,601]{1,0,2:T(1,128)S(1)}, f32[1,256,601]{1,0,2:T(1,128)}, u32[]{:S(2)}) copy-start(f32[1,256,601]{1,0,2:T(1,128)} %param.41) | copy-start | bytes 1846276
  111.3 5.0 %copy-start.1 = (f32[1,256,256]{2,1,0:T(8,128)S(1)}, f32[1,256,256]{2,1,0:T(8,128)}, u32[]{:S(2)}) copy-start(f32[1,256,256]{2,1,0:T(8,128)} %refs_7_.1) | copy-start | bytes 786436
  111.3 5.0 %copy-start.2 = (f32[1,256,256]{2,1,0:T(8,128)S(1)}, f32[1,256,256]{2,1,0:T(8,128)}, u32[]{:S(2)}) copy-start(f32[1,256,256]{2,1,0:T(8,128)} %refs_13_.1) | copy-start | bytes 786436
  111.3 5.0 %copy-start.3 = (f32[1,256,256]{2,1,0:T(8,128)S(1)}, f32[1,256,256]{2,1,0:T(8,128)}, u32[]{:S(2)}) copy-start(f32[1,256,256]{2,1,0:T(8,128)} %refs_16_.1) | copy-start | bytes 786436
  111.3 5.0 %copy-start.4 = (f32[1,256,601]{1,0,2:T(1,128)S(1)}, f32[1,256,601]{1,0,2:T(1,128)}, u32[]{:S(2)}) copy-start(f32[1,256,601]{1,0,2:T(1,128)} %param.42) | copy-start | bytes 1846276
  111.3 5.0 %copy-start.5 = (f32[1,256,601]{1,0,2:T(1,128)S(1)}, f32[1,256,601]{1,0,2:T(1,128)}, u32[]{:S(2)}) copy-start(f32[1,256,601]{1,0,2:T(1,128)} %param.43) | copy-start | bytes 1846276
  111.3 5.0 %copy-start.6 = (f32[1,256,256]{2,1,0:T(8,128)S(1)}, f32[1,256,256]{2,1,0:T(8,128)}, u32[]{:S(2)}) copy-start(f32[1,256,256]{2,1,0:T(8,128)} %refs_8_.1) | copy-start | bytes 786436
  111.3 5.0 %copy-start.7 = (f32[1,256,256]{2,1,0:T(8,128)S(1)}, f32[1,256,256]{2,1,0:T(8,128)}, u32[]{:S(2)}) copy-start(f32[1,256,256]{2,1,0:T(8,128)} %refs_9_.1) | copy-start | bytes 786436
  111.3 5.0 %copy-start.8 = (f32[1,256,256]{2,1,0:T(8,128)S(1)}, f32[1,256,256]{2,1,0:T(8,128)}, u32[]{:S(2)}) copy-start(f32[1,256,256]{2,1,0:T(8,128)} %refs_14_.1) | copy-start | bytes 786436
  111.3 5.0 %copy-start.9 = (f32[1,256,256]{2,1,0:T(8,128)S(1)}, f32[1,256,256]{2,1,0:T(8,128)}, u32[]{:S(2)}) copy-start(f32[1,256,256]{2,1,0:T(8,128)} %refs_15_.1) | copy-start | bytes 786436
  111.4 5.0 %copy-start.10 = (f32[1,256,256]{2,1,0:T(8,128)S(1)}, f32[1,256,256]{2,1,0:T(8,128)}, u32[]{:S(2)}) copy-start(f32[1,256,256]{2,1,0:T(8,128)} %refs_17_.1) | copy-start | bytes 786436
  111.4 5.0 %copy-start.12 = (f32[1,32,256]{2,1,0:T(8,128)S(1)}, f32[1,32,256]{2,1,0:T(8,128)}, u32[]{:S(2)}) copy-start(f32[1,32,256]{2,1,0:T(8,128)} %refs_4_.1) | copy-start | bytes 98308
  111.4 5.0 %copy-start.13 = (f32[1,32,256]{2,1,0:T(8,128)S(1)}, f32[1,32,256]{2,1,0:T(8,128)}, u32[]{:S(2)}) copy-start(f32[1,32,256]{2,1,0:T(8,128)} %refs_5_.1) | copy-start | bytes 98308
  111.4 5.0 %copy-start.14 = (f32[1,32,256]{2,1,0:T(8,128)S(1)}, f32[1,32,256]{2,1,0:T(8,128)}, u32[]{:S(2)}) copy-start(f32[1,32,256]{2,1,0:T(8,128)} %refs_6_.1) | copy-start | bytes 98308
  111.4 5.0 %copy-start.15 = (f32[1,2,256]{2,1,0:T(2,128)S(1)}, f32[1,2,256]{2,1,0:T(2,128)}, u32[]{:S(2)}) copy-start(f32[1,2,256]{2,1,0:T(2,128)} %refs_10_.1) | copy-start | bytes 6148
  111.4 5.0 %copy-start.16 = (f32[1,2,256]{2,1,0:T(2,128)S(1)}, f32[1,2,256]{2,1,0:T(2,128)}, u32[]{:S(2)}) copy-start(f32[1,2,256]{2,1,0:T(2,128)} %refs_11_.1) | copy-start | bytes 6148
  111.4 5.0 %copy-start.17 = (f32[1,2,256]{2,1,0:T(2,128)S(1)}, f32[1,2,256]{2,1,0:T(2,128)}, u32[]{:S(2)}) copy-start(f32[1,2,256]{2,1,0:T(2,128)} %refs_12_.1) | copy-start | bytes 6148

commit v6 on v5

--- a/solution.py
+++ b/solution.py
@@ -1,4 +1,5 @@
 import functools
+import math
 
 import jax
 import jax.numpy as jnp
@@ -41,17 +42,18 @@
     return lax.dot_general(left, right, (((0,), (0,)), ((), ())), preferred_element_type=F32)
 
 
-def gelu_and_slope(value):
-    square = value * value
-    half = 0.5 + 0.5 * jnp.tanh(value * (GELU_LINE + GELU_CUBE * square))
-    result = value * half
-    return result, half + result * (1.0 - half) * (2 * GELU_LINE + (6 * GELU_CUBE) * square)
+def gelu_and_slope(half):
+    square = half * half
+    bend = jnp.tanh(half * (2 * GELU_LINE + (8 * GELU_CUBE) * square))
+    raised = 1.0 + bend
+    result = half * raised
+    return result, raised + result * (1.0 - bend) * (2 * GELU_LINE + (24 * GELU_CUBE) * square)
 
 
 def normalise(value):
-    part = 1.0 / value.shape[-1]
-    centered = value - jnp.sum(value, axis=-1, keepdims=True) * part
-    scale = lax.rsqrt(jnp.sum(centered * centered, axis=-1, keepdims=True) * part + EPS)
+    width = value.shape[-1]
+    centered = value - jnp.sum(value, axis=-1, keepdims=True) * (1.0 / width)
+    scale = lax.rsqrt(jnp.sum(centered * centered, axis=-1, keepdims=True) + EPS * width)
     return centered * scale, scale
 
 
@@ -132,6 +134,7 @@
     rows, width = latent.shape
     wide = lay.wide
     part = 1.0 / width
+    root = math.sqrt(width)
     section = which[0]
     def cut(size):
         return [slice(at, at + size) for at in range(0, rows, size)]
@@ -147,7 +150,7 @@
         for packed, slot in ((mine, section), (theirs, 1 - section)):
             for name, ref in (("up", w_up), ("down", w_down)):
                 low, high = lay.spots[name]
-                ref[slot] = packed[low:high, :]
+                ref[slot] = (packed[low:high, :].astype(F32) * (0.5 if name == "up" else 1.0)).astype(BF16)
             low, high = lay.spots["in"]
             w_cat[slot, :width] = packed[low:high, :]
             low, high = lay.spots["table"]
@@ -159,7 +162,8 @@
             start_tail = (lay.tail - low) // TILE * TILE
             block = packed[low + start_tail : high, :].astype(F32)
             at = lay.tail - low - start_tail
-            gains[slot] = block[at : at + 2] + block[at + 2 : at + 4] + block[at + 4 : at + 6]
+            pair = block[at : at + 2] + block[at + 2 : at + 4] + block[at + 4 : at + 6]
+            gains[slot] = pair * jnp.where(lax.broadcasted_iota(jnp.int32, pair.shape, 0) == 0, root / 2, root)
             row = lax.broadcasted_iota(jnp.int32, block.shape, 0)
             w_head[slot, start_tail : high - low] = jnp.where(row < at, block, 0.0).astype(BF16)
 
@@ -343,7 +347,7 @@
             unit = unit_two[at, where, :]
             scaled = normed_grad[where] * gains[tower, 1:2, :]
             first = row_sum(scaled) * part
-            second = row_sum(scaled * unit) * part
+            second = row_sum(scaled * unit)
             hidden_grad = head_part[at, where, :] + (scaled - first - unit * second) * both(scale_two[at, where, :])
             out_grad = hidden_grad * slope_one[at, where, :]
             unit = unit_one[at, where, :]
@@ -352,7 +356,7 @@
             gain = gains[tower, 0:1, :]
             scaled = out_grad * gain
             first = row_sum(scaled) * part
-            second = row_sum(product * gain) * part
+            second = row_sum(product * gain)
             pre_grads[tower][where, :] = (
                 (scaled - first - unit * second) * both(scale_one[at, where, :])
             ).astype(BF16)
@@ -417,15 +421,15 @@
             kind = packed.dtype
             for name, value in (
                 ("in", g_cat[slot, :width]),
-                ("up", g_up[slot]),
+                ("up", g_up[slot] * 0.5),
                 ("down", g_down[slot]),
                 ("table", g_cat[slot, width : width + lay.codes]),
             ):
                 low, high = lay.spots[name]
                 packed[low:high, :] = value.astype(kind)
-            in_gain = jnp.sum(g_gain[slot], axis=0, keepdims=True)
+            in_gain = jnp.sum(g_gain[slot], axis=0, keepdims=True) * (root / 2)
             pulled = jnp.sum((w_up[slot].astype(F32) * g_up[slot]).T, axis=0, keepdims=True)
-            block_gain = pulled / gains[slot, 1:2, :]
+            block_gain = pulled * root / gains[slot, 1:2, :]
             own = bits if packed is keep else jnp.zeros_like(bits)
             low, high = lay.spots["head"]
             packed[low:high, :] = lay.with_tail(g_head[slot].T, in_gain, block_gain, own).astype(kind)

time: 121 us -> 119 us (0.983)
    pallas_call x1, Pallas kernels: 68 us -> 66.7 us  [on_device(): pl.pallas_call(functools.partial(towers_kernel, lay, steps, chunk), grid_...]
where the time goes in v6:
time: 119 us
  Pallas kernels  73 us (61%)
  waiting for transfers between devices  26.2 us (22%)
  starting transfers between devices  14.4 us (12%)
  other arithmetic  3.27 us (3%)
    pallas_call x1, Pallas kernels, on_device(): pl.pallas_call(functools.partial(towers_kernel, lay, steps, chunk), grid_...  66.7 us
    ppermute x9, waiting for transfers between devices, across(): return lax.ppermute(array, 'dp', [(i, i ^ mask) for i in range(length)])  23.4 us
    ppermute x9, starting transfers between devices, across(): return lax.ppermute(array, 'dp', [(i, i ^ mask) for i in range(length)])  13.5 us
    pallas_call x1, Pallas kernels, on_device(): pl.pallas_call(functools.partial(update_kernel, lay, parts), in_specs=[in...  3.82 us
    ppermute x3, waiting for transfers between devices, swap(): return lax.ppermute(value, 'section', [(0, 1), (1, 0)])  2.84 us
    pallas_call x1, Pallas kernels, on_device(): pl.pallas_call(functools.partial(pack_kernel, lay), out_shape=jax.ShapeDt...  2.45 us
  transfers between devices with their start and end apart: 12, of which 11 were waited for; matrix products, arithmetic and copies ran while one was open for 2% of the time, Pallas kernels for 0%

profile of v6, /device:TPU:0, one launch (start us, length us, event | category | flops | bytes accessed | tf_op | source)
XLA Modules:
  0.0 119.1 jit_solution(1184768958024302188)
XLA Ops:
  0.7 2.5 %pack.1.mine = bf16[1408,256]{1,0:T(8,128)(2,1)} custom-call(f32[1,32,256]{2,1,0:T(8,128)} %refs_4_.1, f32[1,256,256]{2,1,0:T(8,128)} %refs_7_.1, f32[1,256,256]{2,1,0:T(8,128)} %refs_13_.1, f32[1,256,256]{2,1,0:T(8,128)} %refs_16_.1, f32[601,1,256]{2,1,0:T(1,128)} %bitcast.24, f32[1,2,256]{2,1,0:T(2,128)} %refs_10_.1), custom_call_target="tpu_custom_call" | custom-call | tf_op jit(solution)/shard_map/pack/pallas_call | solution.py:509
  3.1 0.5 collective-permute-start
  3.6 2.0 %collective-permute-done.theirs = bf16[1408,256]{1,0:T(8,128)(2,1)S(1)} collective-permute-done((bf16[1408,256]{1,0:T(8,128)(2,1)}, bf16[1408,256]{1,0:T(8,128)(2,1)S(1)}, u32[]{:S(2)}, u32[]{:S(2)}) %collective-permute-start) | collective-permute-done | bytes 720928 | tf_op jit(solution)/shard_map/ppermute | solution.py:487
  5.6 0.9 copy-done.19
  6.5 66.7 %towers.1 = (bf16[1408,256]{1,0:T(8,128)(2,1)}, bf16[1408,256]{1,0:T(8,128)(2,1)}, f32[1024,256]{1,0:T(8,128)}, bf16[1024,256]{1,0:T(8,128)(2,1)}) custom-call(s32[1]{0:T(128)} %bitcast.which, bf16[2048,256]{1,0:T(8,128)(2,1)} %latent.1, s32[5,2,2048]{2,1,0:T(2,128)} %bitcast.31, s32[5,2,2048]{2,1,0:T(2,128)} %bitcast.32, s32[5,2048]{1,0:T(8,128)} %whole_valid.1, ...), custom_call_target="tpu_custom_call" | custom-call | tf_op jit(solution)/shard_map/towers/pallas_call | solution.py:536
  73.2 0.4 collective-permute-start.2
  73.6 1.2 %convert_element_type.55 = f32[1408,256]{1,0:T(8,128)S(1)} convert(bf16[1408,256]{1,0:T(8,128)(2,1)} %get-tuple-element.55) | non-fusion elementwise | flops 360448 | bytes 2162688 | tf_op jit(solution)/shard_map/convert_element_type | solution.py:604
  74.8 0.8 collective-permute-done.2
  75.6 0.2 convert_add_fusion
  75.8 0.0 copy-start.20
  75.8 0.1 fusion
  75.9 2.9 %collective-permute-start.3 = (bf16[352,256]{1,0:T(8,128)(2,1)S(1)}, bf16[352,256]{1,0:T(8,128)(2,1)S(1)}, u32[]{:S(2)}, u32[]{:S(2)}) collective-permute-start(bf16[352,256]{1,0:T(8,128)(2,1)S(1)} %get-tuple-element.81), channel_id=1, source_target_pairs={{0,1},{1,0},{2,3},{3,2},{4,5},{5,4},{6,7},{7,6},{8,9},{9,8},{10,11... | collective-permute-start | bytes 540680 | tf_op jit(solution)/shard_map/ppermute | solution.py:491
  78.8 1.5 %collective-permute-start.5 = (bf16[352,256]{1,0:T(8,128)(2,1)S(1)}, bf16[352,256]{1,0:T(8,128)(2,1)S(1)}, u32[]{:S(2)}, u32[]{:S(2)}) collective-permute-start(bf16[352,256]{1,0:T(8,128)(2,1)S(1)} %get-tuple-element.82), channel_id=1, source_target_pairs={{0,3},{1,2},{2,1},{3,0},{4,7},{5,6},{6,5},{7,4},{8,11},{9,10},{10,... | collective-permute-start | bytes 540680 | tf_op jit(solution)/shard_map/ppermute | solution.py:491
  80.3 0.1 collective-permute-start.4
  80.4 0.0 copy-start.18
  80.4 3.8 %collective-permute-done.3 = bf16[352,256]{1,0:T(8,128)(2,1)S(1)} collective-permute-done((bf16[352,256]{1,0:T(8,128)(2,1)S(1)}, bf16[352,256]{1,0:T(8,128)(2,1)S(1)}, u32[]{:S(2)}, u32[]{:S(2)}) %collective-permute-start.3) | collective-permute-done | bytes 180256 | tf_op jit(solution)/shard_map/ppermute | solution.py:491
  84.1 4.7 %collective-permute-done.5 = bf16[352,256]{1,0:T(8,128)(2,1)S(1)} collective-permute-done((bf16[352,256]{1,0:T(8,128)(2,1)S(1)}, bf16[352,256]{1,0:T(8,128)(2,1)S(1)}, u32[]{:S(2)}, u32[]{:S(2)}) %collective-permute-start.5) | collective-permute-done | bytes 180256 | tf_op jit(solution)/shard_map/ppermute | solution.py:491
  88.8 1.4 %collective-permute-done.4 = bf16[352,256]{1,0:T(8,128)(2,1)S(1)} collective-permute-done((bf16[352,256]{1,0:T(8,128)(2,1)S(1)}, bf16[352,256]{1,0:T(8,128)(2,1)S(1)}, u32[]{:S(2)}, u32[]{:S(2)}) %collective-permute-start.4) | collective-permute-done | bytes 180256 | tf_op jit(solution)/shard_map/ppermute | solution.py:491
  90.2 0.1 add_convert_fusion
  90.3 1.6 %collective-permute-start.6 = (bf16[176,256]{1,0:T(8,128)(2,1)S(1)}, bf16[176,256]{1,0:T(8,128)(2,1)S(1)}, u32[]{:S(2)}, u32[]{:S(2)}) collective-permute-start(bf16[176,256]{1,0:T(8,128)(2,1)S(1)} %broadcast_select_fusion), channel_id=1, source_target_pairs={{0,4},{1,5},{2,6},{3,7},{4,0},{5,1},{6,2},{7,3},{8,12},{9,13},{10,... | collective-permute-start | bytes 270344 | tf_op jit(solution)/shard_map/ppermute | solution.py:491
  91.9 0.0 copy-done.20
  91.9 0.0 collective-permute-start.1
  91.9 2.9 %collective-permute-done.6 = bf16[176,256]{1,0:T(8,128)(2,1)S(1)} collective-permute-done((bf16[176,256]{1,0:T(8,128)(2,1)S(1)}, bf16[176,256]{1,0:T(8,128)(2,1)S(1)}, u32[]{:S(2)}, u32[]{:S(2)}) %collective-permute-start.6) | collective-permute-done | bytes 90144 | tf_op jit(solution)/shard_map/ppermute | solution.py:491
  94.9 3.3 %collective-permute-start.7 = (bf16[176,256]{1,0:T(8,128)(2,1)S(1)}, bf16[176,256]{1,0:T(8,128)(2,1)S(1)}, u32[]{:S(2)}, u32[]{:S(2)}) collective-permute-start(bf16[176,256]{1,0:T(8,128)(2,1)S(1)} %add_convert_fusion.2), channel_id=1, source_target_pairs={{0,8},{1,9},{2,10},{3,11},{4,12},{5,13},{6,14},{7,15},{8,0},{9,1},... | collective-permute-start | bytes 270344 | tf_op jit(solution)/shard_map/ppermute | solution.py:491
  98.3 3.5 %collective-permute-done.7 = bf16[176,256]{1,0:T(8,128)(2,1)S(1)} collective-permute-done((bf16[176,256]{1,0:T(8,128)(2,1)S(1)}, bf16[176,256]{1,0:T(8,128)(2,1)S(1)}, u32[]{:S(2)}, u32[]{:S(2)}) %collective-permute-start.7) | collective-permute-done | bytes 90144 | tf_op jit(solution)/shard_map/ppermute | solution.py:491
  101.8 0.5 collective-permute-start.8
  102.3 0.0 collective-permute-done.1
  102.3 0.1 bitcast_convert_fusion
  102.4 4.0 %collective-permute-done.8 = bf16[176,256]{1,0:T(8,128)(2,1)S(1)} collective-permute-done((bf16[176,256]{1,0:T(8,128)(2,1)S(1)}, bf16[176,256]{1,0:T(8,128)(2,1)S(1)}, u32[]{:S(2)}, u32[]{:S(2)}) %collective-permute-start.8) | collective-permute-done | bytes 90144 | tf_op jit(solution)/shard_map/ppermute | solution.py:491
  106.4 0.1 maximum_select_fusion.1.refs_0_
  106.4 1.5 %collective-permute-start.11 = (bf16[352,256]{1,0:T(8,128)(2,1)S(1)}, bf16[352,256]{1,0:T(8,128)(2,1)S(1)}, u32[]{:S(2)}, u32[]{:S(2)}) collective-permute-start(bf16[352,256]{1,0:T(8,128)(2,1)S(1)} %maximum_select_fusion.1.refs_0_), channel_id=1, source_target_pairs={{0,3},{1,2},{2,1},{3,0},{4,7},{5,6},{6,5},{7,4},{8,11},{9,10},{10,... | collective-permute-start | bytes 540680 | tf_op jit(solution)/shard_map/ppermute | solution.py:491
  107.9 1.5 %collective-permute-start.10 = (bf16[352,256]{1,0:T(8,128)(2,1)S(1)}, bf16[352,256]{1,0:T(8,128)(2,1)S(1)}, u32[]{:S(2)}, u32[]{:S(2)}) collective-permute-start(bf16[352,256]{1,0:T(8,128)(2,1)S(1)} %maximum_select_fusion.1.refs_0_), channel_id=1, source_target_pairs={{0,2},{1,3},{2,0},{3,1},{4,6},{5,7},{6,4},{7,5},{8,10},{9,11},{10,... | collective-permute-start | bytes 540680 | tf_op jit(solution)/shard_map/ppermute | solution.py:491
  109.4 0.5 collective-permute-start.9
  110.0 0.0 copy-done.18
  110.0 0.0 copy-start.3
  110.0 0.0 copy-start.4
  110.0 0.0 copy-start.5
  110.0 0.0 copy-start.6
  110.0 0.0 copy-start.7
  110.1 0.0 copy-start.8
  110.1 0.0 copy-start.9
  110.1 0.0 copy-start.10
  110.1 0.0 copy-start.12
  110.1 0.0 copy-start.13
  110.1 0.0 copy-start.14
  110.1 0.0 copy-start.15
  110.1 0.0 copy-start.16
  110.2 0.0 copy-start.17
  110.2 1.6 %maximum_select_fusion = f32[1,2048,256]{2,1,0:T(8,128)} fusion(f32[1,1024,256]{2,1,0:T(8,128)S(1)} %bitcast_convert_fusion, f32[1,1024,256]{2,1,0:T(8,128)S(1)} %bitcast.30, pred[]{:T(512)S(6)} %eq.11), kind=kLoop, calls=%fused_computation | loop fusion | flops 1572864 | bytes 4194305 | tf_op jit(solution)/shard_map/jit(_where)/select_n | solution.py:633
  111.7 1.3 %collective-permute-done.11.refs_3_ = bf16[352,256]{1,0:T(8,128)(2,1)S(1)} collective-permute-done((bf16[352,256]{1,0:T(8,128)(2,1)S(1)}, bf16[352,256]{1,0:T(8,128)(2,1)S(1)}, u32[]{:S(2)}, u32[]{:S(2)}) %collective-permute-start.11) | collective-permute-done | bytes 180256 | tf_op jit(solution)/shard_map/ppermute | solution.py:491
  113.0 1.8 %collective-permute-done.10.refs_2_ = bf16[352,256]{1,0:T(8,128)(2,1)S(1)} collective-permute-done((bf16[352,256]{1,0:T(8,128)(2,1)S(1)}, bf16[352,256]{1,0:T(8,128)(2,1)S(1)}, u32[]{:S(2)}, u32[]{:S(2)}) %collective-permute-start.10) | collective-permute-done | bytes 180256 | tf_op jit(solution)/shard_map/ppermute | solution.py:491
  114.8 0.1 collective-permute-done.9.refs_1_
  114.9 0.0 copy-done.11
  114.9 0.0 copy-done
  114.9 0.0 copy-done.1
  114.9 0.0 copy-done.2
  115.0 0.0 copy-done.3
  115.0 0.0 copy-done.4
  115.0 0.0 copy-done.5
  115.0 0.0 copy-done.6
  115.0 0.0 copy-done.7
  115.0 0.0 copy-done.8
  115.0 0.0 copy-done.9
  115.1 3.8 %update.1 = (f32[1,32,256]{2,1,0:T(8,128)}, f32[1,32,256]{2,1,0:T(8,128)}, f32[1,32,256]{2,1,0:T(8,128)}, bf16[1,32,256]{2,1,0:T(8,128)(2,1)}, f32[1,256,256]{2,...) custom-call(s32[1]{0:T(128)} %bitcast.7.which, ...), custom_call_target="tpu_custom_call" | custom-call | tf_op jit(solution)/shard_map/update/pallas_call | solution.py:644
  (16 shorter events, 0.1 us)
Async XLA Ops:
  3.1 2.5 %collective-permute-start = (bf16[1408,256]{1,0:T(8,128)(2,1)}, bf16[1408,256]{1,0:T(8,128)(2,1)S(1)}, u32[]{:S(2)}, u32[]{:S(2)}) collective-permute-start(bf16[1408,256]{1,0:T(8,128)(2,1)} %pack.1.mine), channel_id=1, source_target_pairs={{0,16},{16,0},{1,17},{17,1},{2,18},{18,2},{3,19},{19,3},{4,20},{20... | collective-permute-start | bytes 2162696 | tf_op jit(solution)/shard_map/ppermute | solution.py:487
  5.6 0.9 copy-start.19
  73.2 2.4 %collective-permute-start.2 = (bf16[1408,256]{1,0:T(8,128)(2,1)}, bf16[1408,256]{1,0:T(8,128)(2,1)S(1)}, u32[]{:S(2)}, u32[]{:S(2)}) collective-permute-start(bf16[1408,256]{1,0:T(8,128)(2,1)} %get-tuple-element.56), channel_id=1, source_target_pairs={{0,16},{16,0},{1,17},{17,1},{2,18},{18,2},{3,19},{19,3},{4,20},{20... | collective-permute-start | bytes 2162696 | tf_op jit(solution)/shard_map/ppermute | solution.py:487
  75.8 16.2 %copy-start.20 = (bf16[1024,256]{1,0:T(8,128)(2,1)S(1)}, bf16[1024,256]{1,0:T(8,128)(2,1)}, u32[]{:S(2)}) copy-start(bf16[1024,256]{1,0:T(8,128)(2,1)} %get-tuple-element.54) | copy-start | bytes 1572868
  75.9 8.3 %collective-permute-start.3 = (bf16[352,256]{1,0:T(8,128)(2,1)S(1)}, bf16[352,256]{1,0:T(8,128)(2,1)S(1)}, u32[]{:S(2)}, u32[]{:S(2)}) collective-permute-start(bf16[352,256]{1,0:T(8,128)(2,1)S(1)} %get-tuple-element.81), channel_id=1, source_target_pairs={{0,1},{1,0},{2,3},{3,2},{4,5},{5,4},{6,7},{7,6},{8,9},{9,8},{10,11... | collective-permute-start | bytes 540680 | tf_op jit(solution)/shard_map/ppermute | solution.py:491
  78.8 10.0 %collective-permute-start.5 = (bf16[352,256]{1,0:T(8,128)(2,1)S(1)}, bf16[352,256]{1,0:T(8,128)(2,1)S(1)}, u32[]{:S(2)}, u32[]{:S(2)}) collective-permute-start(bf16[352,256]{1,0:T(8,128)(2,1)S(1)} %get-tuple-element.82), channel_id=1, source_target_pairs={{0,3},{1,2},{2,1},{3,0},{4,7},{5,6},{6,5},{7,4},{8,11},{9,10},{10,... | collective-permute-start | bytes 540680 | tf_op jit(solution)/shard_map/ppermute | solution.py:491
  80.3 9.9 %collective-permute-start.4 = (bf16[352,256]{1,0:T(8,128)(2,1)S(1)}, bf16[352,256]{1,0:T(8,128)(2,1)S(1)}, u32[]{:S(2)}, u32[]{:S(2)}) collective-permute-start(bf16[352,256]{1,0:T(8,128)(2,1)S(1)} %get-tuple-element.83), channel_id=1, source_target_pairs={{0,2},{1,3},{2,0},{3,1},{4,6},{5,7},{6,4},{7,5},{8,10},{9,11},{10,... | collective-permute-start | bytes 540680 | tf_op jit(solution)/shard_map/ppermute | solution.py:491
  80.4 29.6 %copy-start.18 = (f32[1024,256]{1,0:T(8,128)S(1)}, f32[1024,256]{1,0:T(8,128)}, u32[]{:S(2)}) copy-start(f32[1024,256]{1,0:T(8,128)} %get-tuple-element.53) | copy-start | bytes 3145732
  90.3 4.6 %collective-permute-start.6 = (bf16[176,256]{1,0:T(8,128)(2,1)S(1)}, bf16[176,256]{1,0:T(8,128)(2,1)S(1)}, u32[]{:S(2)}, u32[]{:S(2)}) collective-permute-start(bf16[176,256]{1,0:T(8,128)(2,1)S(1)} %broadcast_select_fusion), channel_id=1, source_target_pairs={{0,4},{1,5},{2,6},{3,7},{4,0},{5,1},{6,2},{7,3},{8,12},{9,13},{10,... | collective-permute-start | bytes 270344 | tf_op jit(solution)/shard_map/ppermute | solution.py:491
  91.9 10.4 %collective-permute-start.1 = (bf16[1024,256]{1,0:T(8,128)(2,1)S(1)}, bf16[1024,256]{1,0:T(8,128)(2,1)S(1)}, u32[]{:S(2)}, u32[]{:S(2)}) collective-permute-start(bf16[1024,256]{1,0:T(8,128)(2,1)S(1)} %copy-done.20), channel_id=1, source_target_pairs={{0,16},{16,0},{1,17},{17,1},{2,18},{18,2},{3,19},{19,3},{4,20},{20... | collective-permute-start | bytes 1572872 | tf_op jit(solution)/shard_map/ppermute | solution.py:487
  94.9 6.8 %collective-permute-start.7 = (bf16[176,256]{1,0:T(8,128)(2,1)S(1)}, bf16[176,256]{1,0:T(8,128)(2,1)S(1)}, u32[]{:S(2)}, u32[]{:S(2)}) collective-permute-start(bf16[176,256]{1,0:T(8,128)(2,1)S(1)} %add_convert_fusion.2), channel_id=1, source_target_pairs={{0,8},{1,9},{2,10},{3,11},{4,12},{5,13},{6,14},{7,15},{8,0},{9,1},... | collective-permute-start | bytes 270344 | tf_op jit(solution)/shard_map/ppermute | solution.py:491
  101.8 4.6 %collective-permute-start.8 = (bf16[176,256]{1,0:T(8,128)(2,1)S(1)}, bf16[176,256]{1,0:T(8,128)(2,1)S(1)}, u32[]{:S(2)}, u32[]{:S(2)}) collective-permute-start(bf16[176,256]{1,0:T(8,128)(2,1)S(1)} %add_convert_fusion.1), channel_id=1, source_target_pairs={{0,4},{1,5},{2,6},{3,7},{4,0},{5,1},{6,2},{7,3},{8,12},{9,13},{10,... | collective-permute-start | bytes 270344 | tf_op jit(solution)/shard_map/ppermute | solution.py:491
  106.4 8.6 %copy-start.11 = (f32[1,256,256]{2,1,0:T(8,128)S(1)}, f32[1,256,256]{2,1,0:T(8,128)}, u32[]{:S(2)}) copy-start(f32[1,256,256]{2,1,0:T(8,128)} %refs_18_.1) | copy-start | bytes 786436
  106.4 6.6 %collective-permute-start.11 = (bf16[352,256]{1,0:T(8,128)(2,1)S(1)}, bf16[352,256]{1,0:T(8,128)(2,1)S(1)}, u32[]{:S(2)}, u32[]{:S(2)}) collective-permute-start(bf16[352,256]{1,0:T(8,128)(2,1)S(1)} %maximum_select_fusion.1.refs_0_), channel_id=1, source_target_pairs={{0,3},{1,2},{2,1},{3,0},{4,7},{5,6},{6,5},{7,4},{8,11},{9,10},{10,... | collective-permute-start | bytes 540680 | tf_op jit(solution)/shard_map/ppermute | solution.py:491
  107.9 6.9 %collective-permute-start.10 = (bf16[352,256]{1,0:T(8,128)(2,1)S(1)}, bf16[352,256]{1,0:T(8,128)(2,1)S(1)}, u32[]{:S(2)}, u32[]{:S(2)}) collective-permute-start(bf16[352,256]{1,0:T(8,128)(2,1)S(1)} %maximum_select_fusion.1.refs_0_), channel_id=1, source_target_pairs={{0,2},{1,3},{2,0},{3,1},{4,6},{5,7},{6,4},{7,5},{8,10},{9,11},{10,... | collective-permute-start | bytes 540680 | tf_op jit(solution)/shard_map/ppermute | solution.py:491
  109.4 5.5 %collective-permute-start.9 = (bf16[352,256]{1,0:T(8,128)(2,1)S(1)}, bf16[352,256]{1,0:T(8,128)(2,1)S(1)}, u32[]{:S(2)}, u32[]{:S(2)}) collective-permute-start(bf16[352,256]{1,0:T(8,128)(2,1)S(1)} %maximum_select_fusion.1.refs_0_), channel_id=1, source_target_pairs={{0,1},{1,0},{2,3},{3,2},{4,5},{5,4},{6,7},{7,6},{8,9},{9,8},{10,11... | collective-permute-start | bytes 540680 | tf_op jit(solution)/shard_map/ppermute | solution.py:491
  110.0 5.0 %copy-start = (f32[1,256,601]{1,0,2:T(1,128)S(1)}, f32[1,256,601]{1,0,2:T(1,128)}, u32[]{:S(2)}) copy-start(f32[1,256,601]{1,0,2:T(1,128)} %param.41) | copy-start | bytes 1846276
  110.0 5.0 %copy-start.1 = (f32[1,256,256]{2,1,0:T(8,128)S(1)}, f32[1,256,256]{2,1,0:T(8,128)}, u32[]{:S(2)}) copy-start(f32[1,256,256]{2,1,0:T(8,128)} %refs_7_.1) | copy-start | bytes 786436
  110.0 5.0 %copy-start.2 = (f32[1,256,256]{2,1,0:T(8,128)S(1)}, f32[1,256,256]{2,1,0:T(8,128)}, u32[]{:S(2)}) copy-start(f32[1,256,256]{2,1,0:T(8,128)} %refs_13_.1) | copy-start | bytes 786436
  110.0 5.0 %copy-start.3 = (f32[1,256,256]{2,1,0:T(8,128)S(1)}, f32[1,256,256]{2,1,0:T(8,128)}, u32[]{:S(2)}) copy-start(f32[1,256,256]{2,1,0:T(8,128)} %refs_16_.1) | copy-start | bytes 786436
  110.0 5.0 %copy-start.4 = (f32[1,256,601]{1,0,2:T(1,128)S(1)}, f32[1,256,601]{1,0,2:T(1,128)}, u32[]{:S(2)}) copy-start(f32[1,256,601]{1,0,2:T(1,128)} %param.42) | copy-start | bytes 1846276
  110.0 5.0 %copy-start.5 = (f32[1,256,601]{1,0,2:T(1,128)S(1)}, f32[1,256,601]{1,0,2:T(1,128)}, u32[]{:S(2)}) copy-start(f32[1,256,601]{1,0,2:T(1,128)} %param.43) | copy-start | bytes 1846276
  110.0 5.0 %copy-start.6 = (f32[1,256,256]{2,1,0:T(8,128)S(1)}, f32[1,256,256]{2,1,0:T(8,128)}, u32[]{:S(2)}) copy-start(f32[1,256,256]{2,1,0:T(8,128)} %refs_8_.1) | copy-start | bytes 786436
  110.0 5.0 %copy-start.7 = (f32[1,256,256]{2,1,0:T(8,128)S(1)}, f32[1,256,256]{2,1,0:T(8,128)}, u32[]{:S(2)}) copy-start(f32[1,256,256]{2,1,0:T(8,128)} %refs_9_.1) | copy-start | bytes 786436
  110.1 5.0 %copy-start.8 = (f32[1,256,256]{2,1,0:T(8,128)S(1)}, f32[1,256,256]{2,1,0:T(8,128)}, u32[]{:S(2)}) copy-start(f32[1,256,256]{2,1,0:T(8,128)} %refs_14_.1) | copy-start | bytes 786436
  110.1 5.0 %copy-start.9 = (f32[1,256,256]{2,1,0:T(8,128)S(1)}, f32[1,256,256]{2,1,0:T(8,128)}, u32[]{:S(2)}) copy-start(f32[1,256,256]{2,1,0:T(8,128)} %refs_15_.1) | copy-start | bytes 786436
  110.1 4.9 %copy-start.10 = (f32[1,256,256]{2,1,0:T(8,128)S(1)}, f32[1,256,256]{2,1,0:T(8,128)}, u32[]{:S(2)}) copy-start(f32[1,256,256]{2,1,0:T(8,128)} %refs_17_.1) | copy-start | bytes 786436
  110.1 4.9 %copy-start.12 = (f32[1,32,256]{2,1,0:T(8,128)S(1)}, f32[1,32,256]{2,1,0:T(8,128)}, u32[]{:S(2)}) copy-start(f32[1,32,256]{2,1,0:T(8,128)} %refs_4_.1) | copy-start | bytes 98308
  110.1 4.9 %copy-start.13 = (f32[1,32,256]{2,1,0:T(8,128)S(1)}, f32[1,32,256]{2,1,0:T(8,128)}, u32[]{:S(2)}) copy-start(f32[1,32,256]{2,1,0:T(8,128)} %refs_5_.1) | copy-start | bytes 98308
  110.1 4.9 %copy-start.14 = (f32[1,32,256]{2,1,0:T(8,128)S(1)}, f32[1,32,256]{2,1,0:T(8,128)}, u32[]{:S(2)}) copy-start(f32[1,32,256]{2,1,0:T(8,128)} %refs_6_.1) | copy-start | bytes 98308
  110.1 4.9 %copy-start.15 = (f32[1,2,256]{2,1,0:T(2,128)S(1)}, f32[1,2,256]{2,1,0:T(2,128)}, u32[]{:S(2)}) copy-start(f32[1,2,256]{2,1,0:T(2,128)} %refs_10_.1) | copy-start | bytes 6148
  110.1 4.9 %copy-start.16 = (f32[1,2,256]{2,1,0:T(2,128)S(1)}, f32[1,2,256]{2,1,0:T(2,128)}, u32[]{:S(2)}) copy-start(f32[1,2,256]{2,1,0:T(2,128)} %refs_11_.1) | copy-start | bytes 6148
  110.2 4.9 %copy-start.17 = (f32[1,2,256]{2,1,0:T(2,128)S(1)}, f32[1,2,256]{2,1,0:T(2,128)}, u32[]{:S(2)}) copy-start(f32[1,2,256]{2,1,0:T(2,128)} %refs_12_.1) | copy-start | bytes 6148

commit v7 on v6

--- a/solution.py
+++ b/solution.py
@@ -21,8 +21,8 @@
 LANES = 128
 TILE = 16
 BITS = 24
-FIRST, SECOND, HOLD_AT, BACK_FIRST = 4, 4, 1, 0
-CHUNK_ONE, CHUNK_TWO, CHUNK_HEAD, CHUNK_BACK, CHUNK_COPY = 64, 64, 64, 64, 64
+FIRST, SECOND, HOLD_AT, BACK_FIRST = 2, 2, 1, 0
+CHUNK_ONE, CHUNK_TWO, CHUNK_HEAD, CHUNK_BACK, CHUNK_COPY = 128, 128, 128, 64, 128
 LOGITS_FIRST = False
 SPARE = 7
 STEPS = 4

time: 119 us -> 119 us (level)
  no operation moved by 1% of the time
where the time goes in v7:
time: 119 us; the launch traced here: 118 us
  Pallas kernels  72.2 us (61%)
  waiting for transfers between devices  26.3 us (22%)
  starting transfers between devices  14.4 us (12%)
  other arithmetic  3.27 us (3%)
    pallas_call x1, Pallas kernels, on_device(): pl.pallas_call(functools.partial(towers_kernel, lay, steps, chunk), grid_...  65.9 us
    ppermute x9, waiting for transfers between devices, across(): return lax.ppermute(array, 'dp', [(i, i ^ mask) for i in range(length)])  23.4 us
    ppermute x9, starting transfers between devices, across(): return lax.ppermute(array, 'dp', [(i, i ^ mask) for i in range(length)])  13.5 us
    pallas_call x1, Pallas kernels, on_device(): pl.pallas_call(functools.partial(update_kernel, lay, parts), in_specs=[in...  3.82 us
    ppermute x3, waiting for transfers between devices, swap(): return lax.ppermute(value, 'section', [(0, 1), (1, 0)])  2.85 us
    pallas_call x1, Pallas kernels, on_device(): pl.pallas_call(functools.partial(pack_kernel, lay), out_shape=jax.ShapeDt...  2.45 us
  transfers between devices with their start and end apart: 12, of which 11 were waited for; matrix products, arithmetic and copies ran while one was open for 2% of the time, Pallas kernels for 0%

profile of v7, /device:TPU:0, one launch (start us, length us, event | category | flops | bytes accessed | tf_op | source)
XLA Modules:
  0.0 118.3 jit_solution(5918346071398801567)
XLA Ops:
  0.7 2.5 %pack.1.mine = bf16[1408,256]{1,0:T(8,128)(2,1)} custom-call(f32[1,32,256]{2,1,0:T(8,128)} %refs_4_.1, f32[1,256,256]{2,1,0:T(8,128)} %refs_7_.1, f32[1,256,256]{2,1,0:T(8,128)} %refs_13_.1, f32[1,256,256]{2,1,0:T(8,128)} %refs_16_.1, f32[601,1,256]{2,1,0:T(1,128)} %bitcast.24, f32[1,2,256]{2,1,0:T(2,128)} %refs_10_.1), custom_call_target="tpu_custom_call" | custom-call | tf_op jit(solution)/shard_map/pack/pallas_call | solution.py:509
  3.1 0.5 collective-permute-start
  3.6 2.0 %collective-permute-done.theirs = bf16[1408,256]{1,0:T(8,128)(2,1)S(1)} collective-permute-done((bf16[1408,256]{1,0:T(8,128)(2,1)}, bf16[1408,256]{1,0:T(8,128)(2,1)S(1)}, u32[]{:S(2)}, u32[]{:S(2)}) %collective-permute-start) | collective-permute-done | bytes 720928 | tf_op jit(solution)/shard_map/ppermute | solution.py:487
  5.6 0.9 copy-done.19
  6.5 65.9 %towers.1 = (bf16[1408,256]{1,0:T(8,128)(2,1)}, bf16[1408,256]{1,0:T(8,128)(2,1)}, f32[1024,256]{1,0:T(8,128)}, bf16[1024,256]{1,0:T(8,128)(2,1)}) custom-call(s32[1]{0:T(128)} %bitcast.which, bf16[2048,256]{1,0:T(8,128)(2,1)} %latent.1, s32[5,2,2048]{2,1,0:T(2,128)} %bitcast.31, s32[5,2,2048]{2,1,0:T(2,128)} %bitcast.32, s32[5,2048]{1,0:T(8,128)} %whole_valid.1, ...), custom_call_target="tpu_custom_call" | custom-call | tf_op jit(solution)/shard_map/towers/pallas_call | solution.py:536
  72.4 0.4 collective-permute-start.2
  72.8 1.2 %convert_element_type.55 = f32[1408,256]{1,0:T(8,128)S(1)} convert(bf16[1408,256]{1,0:T(8,128)(2,1)} %get-tuple-element.55) | non-fusion elementwise | flops 360448 | bytes 2162688 | tf_op jit(solution)/shard_map/convert_element_type | solution.py:604
  74.0 0.8 collective-permute-done.2
  74.8 0.2 convert_add_fusion
  75.0 0.0 copy-start.20
  75.0 0.1 fusion
  75.1 2.9 %collective-permute-start.3 = (bf16[352,256]{1,0:T(8,128)(2,1)S(1)}, bf16[352,256]{1,0:T(8,128)(2,1)S(1)}, u32[]{:S(2)}, u32[]{:S(2)}) collective-permute-start(bf16[352,256]{1,0:T(8,128)(2,1)S(1)} %get-tuple-element.81), channel_id=1, source_target_pairs={{0,1},{1,0},{2,3},{3,2},{4,5},{5,4},{6,7},{7,6},{8,9},{9,8},{10,11... | collective-permute-start | bytes 540680 | tf_op jit(solution)/shard_map/ppermute | solution.py:491
  78.0 1.5 %collective-permute-start.5 = (bf16[352,256]{1,0:T(8,128)(2,1)S(1)}, bf16[352,256]{1,0:T(8,128)(2,1)S(1)}, u32[]{:S(2)}, u32[]{:S(2)}) collective-permute-start(bf16[352,256]{1,0:T(8,128)(2,1)S(1)} %get-tuple-element.82), channel_id=1, source_target_pairs={{0,3},{1,2},{2,1},{3,0},{4,7},{5,6},{6,5},{7,4},{8,11},{9,10},{10,... | collective-permute-start | bytes 540680 | tf_op jit(solution)/shard_map/ppermute | solution.py:491
  79.5 0.0 collective-permute-start.4
  79.6 0.0 copy-start.18
  79.6 3.8 %collective-permute-done.3 = bf16[352,256]{1,0:T(8,128)(2,1)S(1)} collective-permute-done((bf16[352,256]{1,0:T(8,128)(2,1)S(1)}, bf16[352,256]{1,0:T(8,128)(2,1)S(1)}, u32[]{:S(2)}, u32[]{:S(2)}) %collective-permute-start.3) | collective-permute-done | bytes 180256 | tf_op jit(solution)/shard_map/ppermute | solution.py:491
  83.3 4.7 %collective-permute-done.5 = bf16[352,256]{1,0:T(8,128)(2,1)S(1)} collective-permute-done((bf16[352,256]{1,0:T(8,128)(2,1)S(1)}, bf16[352,256]{1,0:T(8,128)(2,1)S(1)}, u32[]{:S(2)}, u32[]{:S(2)}) %collective-permute-start.5) | collective-permute-done | bytes 180256 | tf_op jit(solution)/shard_map/ppermute | solution.py:491
  88.0 1.4 %collective-permute-done.4 = bf16[352,256]{1,0:T(8,128)(2,1)S(1)} collective-permute-done((bf16[352,256]{1,0:T(8,128)(2,1)S(1)}, bf16[352,256]{1,0:T(8,128)(2,1)S(1)}, u32[]{:S(2)}, u32[]{:S(2)}) %collective-permute-start.4) | collective-permute-done | bytes 180256 | tf_op jit(solution)/shard_map/ppermute | solution.py:491
  89.4 0.1 add_convert_fusion
  89.5 1.6 %collective-permute-start.6 = (bf16[176,256]{1,0:T(8,128)(2,1)S(1)}, bf16[176,256]{1,0:T(8,128)(2,1)S(1)}, u32[]{:S(2)}, u32[]{:S(2)}) collective-permute-start(bf16[176,256]{1,0:T(8,128)(2,1)S(1)} %broadcast_select_fusion), channel_id=1, source_target_pairs={{0,4},{1,5},{2,6},{3,7},{4,0},{5,1},{6,2},{7,3},{8,12},{9,13},{10,... | collective-permute-start | bytes 270344 | tf_op jit(solution)/shard_map/ppermute | solution.py:491
  91.2 0.0 copy-done.20
  91.2 0.0 collective-permute-start.1
  91.2 2.9 %collective-permute-done.6 = bf16[176,256]{1,0:T(8,128)(2,1)S(1)} collective-permute-done((bf16[176,256]{1,0:T(8,128)(2,1)S(1)}, bf16[176,256]{1,0:T(8,128)(2,1)S(1)}, u32[]{:S(2)}, u32[]{:S(2)}) %collective-permute-start.6) | collective-permute-done | bytes 90144 | tf_op jit(solution)/shard_map/ppermute | solution.py:491
  94.2 3.3 %collective-permute-start.7 = (bf16[176,256]{1,0:T(8,128)(2,1)S(1)}, bf16[176,256]{1,0:T(8,128)(2,1)S(1)}, u32[]{:S(2)}, u32[]{:S(2)}) collective-permute-start(bf16[176,256]{1,0:T(8,128)(2,1)S(1)} %add_convert_fusion.2), channel_id=1, source_target_pairs={{0,8},{1,9},{2,10},{3,11},{4,12},{5,13},{6,14},{7,15},{8,0},{9,1},... | collective-permute-start | bytes 270344 | tf_op jit(solution)/shard_map/ppermute | solution.py:491
  97.5 3.5 %collective-permute-done.7 = bf16[176,256]{1,0:T(8,128)(2,1)S(1)} collective-permute-done((bf16[176,256]{1,0:T(8,128)(2,1)S(1)}, bf16[176,256]{1,0:T(8,128)(2,1)S(1)}, u32[]{:S(2)}, u32[]{:S(2)}) %collective-permute-start.7) | collective-permute-done | bytes 90144 | tf_op jit(solution)/shard_map/ppermute | solution.py:491
  101.0 0.5 collective-permute-start.8
  101.5 0.0 collective-permute-done.1
  101.5 0.1 bitcast_convert_fusion
  101.6 4.0 %collective-permute-done.8 = bf16[176,256]{1,0:T(8,128)(2,1)S(1)} collective-permute-done((bf16[176,256]{1,0:T(8,128)(2,1)S(1)}, bf16[176,256]{1,0:T(8,128)(2,1)S(1)}, u32[]{:S(2)}, u32[]{:S(2)}) %collective-permute-start.8) | collective-permute-done | bytes 90144 | tf_op jit(solution)/shard_map/ppermute | solution.py:491
  105.6 0.1 maximum_select_fusion.1.refs_0_
  105.6 1.5 %collective-permute-start.11 = (bf16[352,256]{1,0:T(8,128)(2,1)S(1)}, bf16[352,256]{1,0:T(8,128)(2,1)S(1)}, u32[]{:S(2)}, u32[]{:S(2)}) collective-permute-start(bf16[352,256]{1,0:T(8,128)(2,1)S(1)} %maximum_select_fusion.1.refs_0_), channel_id=1, source_target_pairs={{0,3},{1,2},{2,1},{3,0},{4,7},{5,6},{6,5},{7,4},{8,11},{9,10},{10,... | collective-permute-start | bytes 540680 | tf_op jit(solution)/shard_map/ppermute | solution.py:491
  107.1 1.5 %collective-permute-start.10 = (bf16[352,256]{1,0:T(8,128)(2,1)S(1)}, bf16[352,256]{1,0:T(8,128)(2,1)S(1)}, u32[]{:S(2)}, u32[]{:S(2)}) collective-permute-start(bf16[352,256]{1,0:T(8,128)(2,1)S(1)} %maximum_select_fusion.1.refs_0_), channel_id=1, source_target_pairs={{0,2},{1,3},{2,0},{3,1},{4,6},{5,7},{6,4},{7,5},{8,10},{9,11},{10,... | collective-permute-start | bytes 540680 | tf_op jit(solution)/shard_map/ppermute | solution.py:491
  108.7 0.5 collective-permute-start.9
  109.2 0.0 copy-done.18
  109.2 0.0 copy-start.3
  109.2 0.0 copy-start.4
  109.2 0.0 copy-start.5
  109.2 0.0 copy-start.6
  109.2 0.0 copy-start.7
  109.3 0.0 copy-start.8
  109.3 0.0 copy-start.9
  109.3 0.0 copy-start.10
  109.3 0.0 copy-start.12
  109.3 0.0 copy-start.13
  109.3 0.0 copy-start.14
  109.3 0.0 copy-start.15
  109.3 0.0 copy-start.16
  109.4 0.0 copy-start.17
  109.4 1.6 %maximum_select_fusion = f32[1,2048,256]{2,1,0:T(8,128)} fusion(f32[1,1024,256]{2,1,0:T(8,128)S(1)} %bitcast_convert_fusion, f32[1,1024,256]{2,1,0:T(8,128)S(1)} %bitcast.30, pred[]{:T(512)S(6)} %eq.11), kind=kLoop, calls=%fused_computation | loop fusion | flops 1572864 | bytes 4194305 | tf_op jit(solution)/shard_map/jit(_where)/select_n | solution.py:633
  110.9 1.3 %collective-permute-done.11.refs_3_ = bf16[352,256]{1,0:T(8,128)(2,1)S(1)} collective-permute-done((bf16[352,256]{1,0:T(8,128)(2,1)S(1)}, bf16[352,256]{1,0:T(8,128)(2,1)S(1)}, u32[]{:S(2)}, u32[]{:S(2)}) %collective-permute-start.11) | collective-permute-done | bytes 180256 | tf_op jit(solution)/shard_map/ppermute | solution.py:491
  112.2 1.8 %collective-permute-done.10.refs_2_ = bf16[352,256]{1,0:T(8,128)(2,1)S(1)} collective-permute-done((bf16[352,256]{1,0:T(8,128)(2,1)S(1)}, bf16[352,256]{1,0:T(8,128)(2,1)S(1)}, u32[]{:S(2)}, u32[]{:S(2)}) %collective-permute-start.10) | collective-permute-done | bytes 180256 | tf_op jit(solution)/shard_map/ppermute | solution.py:491
  114.0 0.1 collective-permute-done.9.refs_1_
  114.2 0.0 copy-done.11
  114.2 0.0 copy-done
  114.2 0.0 copy-done.1
  114.2 0.0 copy-done.2
  114.2 0.0 copy-done.3
  114.2 0.0 copy-done.4
  114.2 0.0 copy-done.5
  114.2 0.0 copy-done.6
  114.2 0.0 copy-done.7
  114.2 0.0 copy-done.8
  114.2 0.0 copy-done.9
  114.3 3.8 %update.1 = (f32[1,32,256]{2,1,0:T(8,128)}, f32[1,32,256]{2,1,0:T(8,128)}, f32[1,32,256]{2,1,0:T(8,128)}, bf16[1,32,256]{2,1,0:T(8,128)(2,1)}, f32[1,256,256]{2,...) custom-call(s32[1]{0:T(128)} %bitcast.7.which, ...), custom_call_target="tpu_custom_call" | custom-call | tf_op jit(solution)/shard_map/update/pallas_call | solution.py:644
  (16 shorter events, 0.1 us)
Async XLA Ops:
  3.1 2.5 %collective-permute-start = (bf16[1408,256]{1,0:T(8,128)(2,1)}, bf16[1408,256]{1,0:T(8,128)(2,1)S(1)}, u32[]{:S(2)}, u32[]{:S(2)}) collective-permute-start(bf16[1408,256]{1,0:T(8,128)(2,1)} %pack.1.mine), channel_id=1, source_target_pairs={{0,16},{16,0},{1,17},{17,1},{2,18},{18,2},{3,19},{19,3},{4,20},{20... | collective-permute-start | bytes 2162696 | tf_op jit(solution)/shard_map/ppermute | solution.py:487
  5.6 0.9 copy-start.19
  72.4 2.4 %collective-permute-start.2 = (bf16[1408,256]{1,0:T(8,128)(2,1)}, bf16[1408,256]{1,0:T(8,128)(2,1)S(1)}, u32[]{:S(2)}, u32[]{:S(2)}) collective-permute-start(bf16[1408,256]{1,0:T(8,128)(2,1)} %get-tuple-element.56), channel_id=1, source_target_pairs={{0,16},{16,0},{1,17},{17,1},{2,18},{18,2},{3,19},{19,3},{4,20},{20... | collective-permute-start | bytes 2162696 | tf_op jit(solution)/shard_map/ppermute | solution.py:487
  75.0 16.2 %copy-start.20 = (bf16[1024,256]{1,0:T(8,128)(2,1)S(1)}, bf16[1024,256]{1,0:T(8,128)(2,1)}, u32[]{:S(2)}) copy-start(bf16[1024,256]{1,0:T(8,128)(2,1)} %get-tuple-element.54) | copy-start | bytes 1572868
  75.1 8.3 %collective-permute-start.3 = (bf16[352,256]{1,0:T(8,128)(2,1)S(1)}, bf16[352,256]{1,0:T(8,128)(2,1)S(1)}, u32[]{:S(2)}, u32[]{:S(2)}) collective-permute-start(bf16[352,256]{1,0:T(8,128)(2,1)S(1)} %get-tuple-element.81), channel_id=1, source_target_pairs={{0,1},{1,0},{2,3},{3,2},{4,5},{5,4},{6,7},{7,6},{8,9},{9,8},{10,11... | collective-permute-start | bytes 540680 | tf_op jit(solution)/shard_map/ppermute | solution.py:491
  78.0 10.0 %collective-permute-start.5 = (bf16[352,256]{1,0:T(8,128)(2,1)S(1)}, bf16[352,256]{1,0:T(8,128)(2,1)S(1)}, u32[]{:S(2)}, u32[]{:S(2)}) collective-permute-start(bf16[352,256]{1,0:T(8,128)(2,1)S(1)} %get-tuple-element.82), channel_id=1, source_target_pairs={{0,3},{1,2},{2,1},{3,0},{4,7},{5,6},{6,5},{7,4},{8,11},{9,10},{10,... | collective-permute-start | bytes 540680 | tf_op jit(solution)/shard_map/ppermute | solution.py:491
  79.5 9.9 %collective-permute-start.4 = (bf16[352,256]{1,0:T(8,128)(2,1)S(1)}, bf16[352,256]{1,0:T(8,128)(2,1)S(1)}, u32[]{:S(2)}, u32[]{:S(2)}) collective-permute-start(bf16[352,256]{1,0:T(8,128)(2,1)S(1)} %get-tuple-element.83), channel_id=1, source_target_pairs={{0,2},{1,3},{2,0},{3,1},{4,6},{5,7},{6,4},{7,5},{8,10},{9,11},{10,... | collective-permute-start | bytes 540680 | tf_op jit(solution)/shard_map/ppermute | solution.py:491
  79.6 29.6 %copy-start.18 = (f32[1024,256]{1,0:T(8,128)S(1)}, f32[1024,256]{1,0:T(8,128)}, u32[]{:S(2)}) copy-start(f32[1024,256]{1,0:T(8,128)} %get-tuple-element.53) | copy-start | bytes 3145732
  89.5 4.6 %collective-permute-start.6 = (bf16[176,256]{1,0:T(8,128)(2,1)S(1)}, bf16[176,256]{1,0:T(8,128)(2,1)S(1)}, u32[]{:S(2)}, u32[]{:S(2)}) collective-permute-start(bf16[176,256]{1,0:T(8,128)(2,1)S(1)} %broadcast_select_fusion), channel_id=1, source_target_pairs={{0,4},{1,5},{2,6},{3,7},{4,0},{5,1},{6,2},{7,3},{8,12},{9,13},{10,... | collective-permute-start | bytes 270344 | tf_op jit(solution)/shard_map/ppermute | solution.py:491
  91.2 10.4 %collective-permute-start.1 = (bf16[1024,256]{1,0:T(8,128)(2,1)S(1)}, bf16[1024,256]{1,0:T(8,128)(2,1)S(1)}, u32[]{:S(2)}, u32[]{:S(2)}) collective-permute-start(bf16[1024,256]{1,0:T(8,128)(2,1)S(1)} %copy-done.20), channel_id=1, source_target_pairs={{0,16},{16,0},{1,17},{17,1},{2,18},{18,2},{3,19},{19,3},{4,20},{20... | collective-permute-start | bytes 1572872 | tf_op jit(solution)/shard_map/ppermute | solution.py:487
  94.2 6.8 %collective-permute-start.7 = (bf16[176,256]{1,0:T(8,128)(2,1)S(1)}, bf16[176,256]{1,0:T(8,128)(2,1)S(1)}, u32[]{:S(2)}, u32[]{:S(2)}) collective-permute-start(bf16[176,256]{1,0:T(8,128)(2,1)S(1)} %add_convert_fusion.2), channel_id=1, source_target_pairs={{0,8},{1,9},{2,10},{3,11},{4,12},{5,13},{6,14},{7,15},{8,0},{9,1},... | collective-permute-start | bytes 270344 | tf_op jit(solution)/shard_map/ppermute | solution.py:491
  101.0 4.6 %collective-permute-start.8 = (bf16[176,256]{1,0:T(8,128)(2,1)S(1)}, bf16[176,256]{1,0:T(8,128)(2,1)S(1)}, u32[]{:S(2)}, u32[]{:S(2)}) collective-permute-start(bf16[176,256]{1,0:T(8,128)(2,1)S(1)} %add_convert_fusion.1), channel_id=1, source_target_pairs={{0,4},{1,5},{2,6},{3,7},{4,0},{5,1},{6,2},{7,3},{8,12},{9,13},{10,... | collective-permute-start | bytes 270344 | tf_op jit(solution)/shard_map/ppermute | solution.py:491
  105.6 8.6 %copy-start.11 = (f32[1,256,256]{2,1,0:T(8,128)S(1)}, f32[1,256,256]{2,1,0:T(8,128)}, u32[]{:S(2)}) copy-start(f32[1,256,256]{2,1,0:T(8,128)} %refs_18_.1) | copy-start | bytes 786436
  105.6 6.6 %collective-permute-start.11 = (bf16[352,256]{1,0:T(8,128)(2,1)S(1)}, bf16[352,256]{1,0:T(8,128)(2,1)S(1)}, u32[]{:S(2)}, u32[]{:S(2)}) collective-permute-start(bf16[352,256]{1,0:T(8,128)(2,1)S(1)} %maximum_select_fusion.1.refs_0_), channel_id=1, source_target_pairs={{0,3},{1,2},{2,1},{3,0},{4,7},{5,6},{6,5},{7,4},{8,11},{9,10},{10,... | collective-permute-start | bytes 540680 | tf_op jit(solution)/shard_map/ppermute | solution.py:491
  107.1 6.9 %collective-permute-start.10 = (bf16[352,256]{1,0:T(8,128)(2,1)S(1)}, bf16[352,256]{1,0:T(8,128)(2,1)S(1)}, u32[]{:S(2)}, u32[]{:S(2)}) collective-permute-start(bf16[352,256]{1,0:T(8,128)(2,1)S(1)} %maximum_select_fusion.1.refs_0_), channel_id=1, source_target_pairs={{0,2},{1,3},{2,0},{3,1},{4,6},{5,7},{6,4},{7,5},{8,10},{9,11},{10,... | collective-permute-start | bytes 540680 | tf_op jit(solution)/shard_map/ppermute | solution.py:491
  108.7 5.5 %collective-permute-start.9 = (bf16[352,256]{1,0:T(8,128)(2,1)S(1)}, bf16[352,256]{1,0:T(8,128)(2,1)S(1)}, u32[]{:S(2)}, u32[]{:S(2)}) collective-permute-start(bf16[352,256]{1,0:T(8,128)(2,1)S(1)} %maximum_select_fusion.1.refs_0_), channel_id=1, source_target_pairs={{0,1},{1,0},{2,3},{3,2},{4,5},{5,4},{6,7},{7,6},{8,9},{9,8},{10,11... | collective-permute-start | bytes 540680 | tf_op jit(solution)/shard_map/ppermute | solution.py:491
  109.2 5.0 %copy-start = (f32[1,256,601]{1,0,2:T(1,128)S(1)}, f32[1,256,601]{1,0,2:T(1,128)}, u32[]{:S(2)}) copy-start(f32[1,256,601]{1,0,2:T(1,128)} %param.41) | copy-start | bytes 1846276
  109.2 5.0 %copy-start.1 = (f32[1,256,256]{2,1,0:T(8,128)S(1)}, f32[1,256,256]{2,1,0:T(8,128)}, u32[]{:S(2)}) copy-start(f32[1,256,256]{2,1,0:T(8,128)} %refs_7_.1) | copy-start | bytes 786436
  109.2 5.0 %copy-start.2 = (f32[1,256,256]{2,1,0:T(8,128)S(1)}, f32[1,256,256]{2,1,0:T(8,128)}, u32[]{:S(2)}) copy-start(f32[1,256,256]{2,1,0:T(8,128)} %refs_13_.1) | copy-start | bytes 786436
  109.2 5.0 %copy-start.3 = (f32[1,256,256]{2,1,0:T(8,128)S(1)}, f32[1,256,256]{2,1,0:T(8,128)}, u32[]{:S(2)}) copy-start(f32[1,256,256]{2,1,0:T(8,128)} %refs_16_.1) | copy-start | bytes 786436
  109.2 5.0 %copy-start.4 = (f32[1,256,601]{1,0,2:T(1,128)S(1)}, f32[1,256,601]{1,0,2:T(1,128)}, u32[]{:S(2)}) copy-start(f32[1,256,601]{1,0,2:T(1,128)} %param.42) | copy-start | bytes 1846276
  109.2 5.0 %copy-start.5 = (f32[1,256,601]{1,0,2:T(1,128)S(1)}, f32[1,256,601]{1,0,2:T(1,128)}, u32[]{:S(2)}) copy-start(f32[1,256,601]{1,0,2:T(1,128)} %param.43) | copy-start | bytes 1846276
  109.2 5.0 %copy-start.6 = (f32[1,256,256]{2,1,0:T(8,128)S(1)}, f32[1,256,256]{2,1,0:T(8,128)}, u32[]{:S(2)}) copy-start(f32[1,256,256]{2,1,0:T(8,128)} %refs_8_.1) | copy-start | bytes 786436
  109.2 5.0 %copy-start.7 = (f32[1,256,256]{2,1,0:T(8,128)S(1)}, f32[1,256,256]{2,1,0:T(8,128)}, u32[]{:S(2)}) copy-start(f32[1,256,256]{2,1,0:T(8,128)} %refs_9_.1) | copy-start | bytes 786436
  109.3 5.0 %copy-start.8 = (f32[1,256,256]{2,1,0:T(8,128)S(1)}, f32[1,256,256]{2,1,0:T(8,128)}, u32[]{:S(2)}) copy-start(f32[1,256,256]{2,1,0:T(8,128)} %refs_14_.1) | copy-start | bytes 786436
  109.3 5.0 %copy-start.9 = (f32[1,256,256]{2,1,0:T(8,128)S(1)}, f32[1,256,256]{2,1,0:T(8,128)}, u32[]{:S(2)}) copy-start(f32[1,256,256]{2,1,0:T(8,128)} %refs_15_.1) | copy-start | bytes 786436
  109.3 5.0 %copy-start.10 = (f32[1,256,256]{2,1,0:T(8,128)S(1)}, f32[1,256,256]{2,1,0:T(8,128)}, u32[]{:S(2)}) copy-start(f32[1,256,256]{2,1,0:T(8,128)} %refs_17_.1) | copy-start | bytes 786436
  109.3 5.0 %copy-start.12 = (f32[1,32,256]{2,1,0:T(8,128)S(1)}, f32[1,32,256]{2,1,0:T(8,128)}, u32[]{:S(2)}) copy-start(f32[1,32,256]{2,1,0:T(8,128)} %refs_4_.1) | copy-start | bytes 98308
  109.3 5.0 %copy-start.13 = (f32[1,32,256]{2,1,0:T(8,128)S(1)}, f32[1,32,256]{2,1,0:T(8,128)}, u32[]{:S(2)}) copy-start(f32[1,32,256]{2,1,0:T(8,128)} %refs_5_.1) | copy-start | bytes 98308
  109.3 5.0 %copy-start.14 = (f32[1,32,256]{2,1,0:T(8,128)S(1)}, f32[1,32,256]{2,1,0:T(8,128)}, u32[]{:S(2)}) copy-start(f32[1,32,256]{2,1,0:T(8,128)} %refs_6_.1) | copy-start | bytes 98308
  109.3 5.0 %copy-start.15 = (f32[1,2,256]{2,1,0:T(2,128)S(1)}, f32[1,2,256]{2,1,0:T(2,128)}, u32[]{:S(2)}) copy-start(f32[1,2,256]{2,1,0:T(2,128)} %refs_10_.1) | copy-start | bytes 6148
  109.3 5.0 %copy-start.16 = (f32[1,2,256]{2,1,0:T(2,128)S(1)}, f32[1,2,256]{2,1,0:T(2,128)}, u32[]{:S(2)}) copy-start(f32[1,2,256]{2,1,0:T(2,128)} %refs_11_.1) | copy-start | bytes 6148
  109.4 5.0 %copy-start.17 = (f32[1,2,256]{2,1,0:T(2,128)S(1)}, f32[1,2,256]{2,1,0:T(2,128)}, u32[]{:S(2)}) copy-start(f32[1,2,256]{2,1,0:T(2,128)} %refs_12_.1) | copy-start | bytes 6148

commit v8 on v7

--- a/solution.py
+++ b/solution.py
@@ -614,19 +614,8 @@
         current = current + arrived.astype(F32)
     current = current.astype(BF16)
     masks = [1 << bit for bit in range(length.bit_length() - 1)][parts.bit_length() - 1 :]
-    halved = masks[:1] if len(masks) > 1 else []
-    for mask in halved:
-        half = current.shape[0] // 2
-        upper = (index // mask) % 2 == 1
-        sent = jnp.where(upper, current[:half], current[half:])
-        kept = jnp.where(upper, current[half:], current[:half])
-        current = (kept.astype(F32) + across(sent, mask, length).astype(F32)).astype(BF16)
-    for mask in masks[len(halved) :]:
+    for mask in masks:
         current = (current.astype(F32) + across(current, mask, length).astype(F32)).astype(BF16)
-    for mask in halved:
-        upper = (index // mask) % 2 == 1
-        found = across(current, mask, length)
-        current = jnp.where(upper, jnp.concatenate([found, current]), jnp.concatenate([current, found]))
     pieces = [current] + [across(current, mask, length) for mask in range(1, parts)]
 
     other = swap(ends_send).astype(F32)

time: 119 us -> 118 us (level)
    ppermute x9 -> x8, waiting for transfers between devices: 23.4 us -> 22.4 us  [across(): return lax.ppermute(array, 'dp', [(i, i ^ mask) for i in range(length)])]
    ppermute x9 -> x8, starting transfers between devices: 13.5 us -> 12.9 us  [across(): return lax.ppermute(array, 'dp', [(i, i ^ mask) for i in range(length)])]
  transfers between devices with their start and end apart: 12 -> 11, of which waited for: 11 -> 10; matrix products, arithmetic and copies ran while one was open for 2% -> 3% of each run, Pallas kernels for 0% -> 0%
where the time goes in v8:
time: 118 us
  Pallas kernels  72.2 us (61%)
  waiting for transfers between devices  25.2 us (21%)
  starting transfers between devices  13.8 us (12%)
  other arithmetic  4.32 us (4%)
    pallas_call x1, Pallas kernels, on_device(): pl.pallas_call(functools.partial(towers_kernel, lay, steps, chunk), grid_...  65.9 us
    ppermute x8, waiting for transfers between devices, across(): return lax.ppermute(array, 'dp', [(i, i ^ mask) for i in range(length)])  22.4 us
    ppermute x8, starting transfers between devices, across(): return lax.ppermute(array, 'dp', [(i, i ^ mask) for i in range(length)])  12.9 us
    pallas_call x1, Pallas kernels, on_device(): pl.pallas_call(functools.partial(update_kernel, lay, parts), in_specs=[in...  3.82 us
    ppermute x3, waiting for transfers between devices, swap(): return lax.ppermute(value, 'section', [(0, 1), (1, 0)])  2.85 us
    pallas_call x1, Pallas kernels, on_device(): pl.pallas_call(functools.partial(pack_kernel, lay), out_shape=jax.ShapeDt...  2.44 us
  transfers between devices with their start and end apart: 11, of which 10 were waited for; matrix products, arithmetic and copies ran while one was open for 3% of the time, Pallas kernels for 0%

profile of v8, /device:TPU:0, one launch (start us, length us, event | category | flops | bytes accessed | tf_op | source)
XLA Modules:
  0.0 117.7 jit_solution(13779616842779725170)
XLA Ops:
  0.7 2.4 %pack.1.mine = bf16[1408,256]{1,0:T(8,128)(2,1)} custom-call(f32[1,32,256]{2,1,0:T(8,128)} %refs_4_.1, f32[1,256,256]{2,1,0:T(8,128)} %refs_7_.1, f32[1,256,256]{2,1,0:T(8,128)} %refs_13_.1, f32[1,256,256]{2,1,0:T(8,128)} %refs_16_.1, f32[601,1,256]{2,1,0:T(1,128)} %bitcast.24, f32[1,2,256]{2,1,0:T(2,128)} %refs_10_.1), custom_call_target="tpu_custom_call" | custom-call | tf_op jit(solution)/shard_map/pack/pallas_call | solution.py:509
  3.1 0.5 collective-permute-start
  3.6 2.0 %collective-permute-done.theirs = bf16[1408,256]{1,0:T(8,128)(2,1)S(1)} collective-permute-done((bf16[1408,256]{1,0:T(8,128)(2,1)}, bf16[1408,256]{1,0:T(8,128)(2,1)S(1)}, u32[]{:S(2)}, u32[]{:S(2)}) %collective-permute-start) | collective-permute-done | bytes 720928 | tf_op jit(solution)/shard_map/ppermute | solution.py:487
  5.6 0.9 copy-done.19
  6.5 65.9 %towers.1 = (bf16[1408,256]{1,0:T(8,128)(2,1)}, bf16[1408,256]{1,0:T(8,128)(2,1)}, f32[1024,256]{1,0:T(8,128)}, bf16[1024,256]{1,0:T(8,128)(2,1)}) custom-call(s32[1]{0:T(128)} %bitcast.which, bf16[2048,256]{1,0:T(8,128)(2,1)} %latent.1, s32[5,2,2048]{2,1,0:T(2,128)} %bitcast.31, s32[5,2,2048]{2,1,0:T(2,128)} %bitcast.32, s32[5,2048]{1,0:T(8,128)} %whole_valid.1, ...), custom_call_target="tpu_custom_call" | custom-call | tf_op jit(solution)/shard_map/towers/pallas_call | solution.py:536
  72.4 0.4 collective-permute-start.2
  72.8 1.2 %convert_element_type.55 = f32[1408,256]{1,0:T(8,128)S(1)} convert(bf16[1408,256]{1,0:T(8,128)(2,1)} %get-tuple-element.55) | non-fusion elementwise | flops 360448 | bytes 2162688 | tf_op jit(solution)/shard_map/convert_element_type | solution.py:604
  74.0 0.8 collective-permute-done.2
  74.8 0.2 convert_add_fusion
  75.0 0.1 fusion
  75.1 2.9 %collective-permute-start.3 = (bf16[352,256]{1,0:T(8,128)(2,1)S(1)}, bf16[352,256]{1,0:T(8,128)(2,1)}, u32[]{:S(2)}, u32[]{:S(2)}) collective-permute-start(bf16[352,256]{1,0:T(8,128)(2,1)S(1)} %get-tuple-element.81), channel_id=1, source_target_pairs={{0,1},{1,0},{2,3},{3,2},{4,5},{5,4},{6,7},{7,6},{8,9},{9,8},{10,11... | collective-permute-start | bytes 540680 | tf_op jit(solution)/shard_map/ppermute | solution.py:491
  78.0 1.5 %collective-permute-start.5 = (bf16[352,256]{1,0:T(8,128)(2,1)S(1)}, bf16[352,256]{1,0:T(8,128)(2,1)}, u32[]{:S(2)}, u32[]{:S(2)}) collective-permute-start(bf16[352,256]{1,0:T(8,128)(2,1)S(1)} %get-tuple-element.82), channel_id=1, source_target_pairs={{0,3},{1,2},{2,1},{3,0},{4,7},{5,6},{6,5},{7,4},{8,11},{9,10},{10,... | collective-permute-start | bytes 540680 | tf_op jit(solution)/shard_map/ppermute | solution.py:491
  79.5 0.1 collective-permute-start.4
  79.5 0.0 collective-permute-start.1
  79.6 3.9 %collective-permute-done.3 = bf16[352,256]{1,0:T(8,128)(2,1)} collective-permute-done((bf16[352,256]{1,0:T(8,128)(2,1)S(1)}, bf16[352,256]{1,0:T(8,128)(2,1)}, u32[]{:S(2)}, u32[]{:S(2)}) %collective-permute-start.3) | collective-permute-done | bytes 180256 | tf_op jit(solution)/shard_map/ppermute | solution.py:491
  83.4 4.7 %collective-permute-done.5 = bf16[352,256]{1,0:T(8,128)(2,1)} collective-permute-done((bf16[352,256]{1,0:T(8,128)(2,1)S(1)}, bf16[352,256]{1,0:T(8,128)(2,1)}, u32[]{:S(2)}, u32[]{:S(2)}) %collective-permute-start.5) | collective-permute-done | bytes 180256 | tf_op jit(solution)/shard_map/ppermute | solution.py:491
  88.1 1.4 %collective-permute-done.4 = bf16[352,256]{1,0:T(8,128)(2,1)} collective-permute-done((bf16[352,256]{1,0:T(8,128)(2,1)S(1)}, bf16[352,256]{1,0:T(8,128)(2,1)}, u32[]{:S(2)}, u32[]{:S(2)}) %collective-permute-start.4) | collective-permute-done | bytes 180256 | tf_op jit(solution)/shard_map/ppermute | solution.py:491
  89.5 1.2 %add_convert_fusion.2 = bf16[352,256]{1,0:T(8,128)(2,1)S(1)} fusion(bf16[352,256]{1,0:T(8,128)(2,1)} %collective-permute-done.5, bf16[352,256]{1,0:T(8,128)(2,1)} %collective-permute-done.4, f32[352,256]{1,0:T(8,128)S(1)} %dynamic-slice_bitcast_fusion, bf16[352,256]{1,0:T(8,128)(2,1)} %collective-permute-done.3), kind=kLoop, calls=%fused_computation.5 | loop fusion | flops 630784 | bytes 1081344 | tf_op jit(solution)/shard_map/convert_element_type | solution.py:615
  90.7 1.6 %collective-permute-start.6 = (bf16[352,256]{1,0:T(8,128)(2,1)S(1)}, bf16[352,256]{1,0:T(8,128)(2,1)S(1)}, u32[]{:S(2)}, u32[]{:S(2)}) collective-permute-start(bf16[352,256]{1,0:T(8,128)(2,1)S(1)} %add_convert_fusion.2), channel_id=1, source_target_pairs={{0,4},{1,5},{2,6},{3,7},{4,0},{5,1},{6,2},{7,3},{8,12},{9,13},{10,... | collective-permute-start | bytes 540680 | tf_op jit(solution)/shard_map/ppermute | solution.py:491
  92.3 3.9 %collective-permute-done.6 = bf16[352,256]{1,0:T(8,128)(2,1)S(1)} collective-permute-done((bf16[352,256]{1,0:T(8,128)(2,1)S(1)}, bf16[352,256]{1,0:T(8,128)(2,1)S(1)}, u32[]{:S(2)}, u32[]{:S(2)}) %collective-permute-start.6) | collective-permute-done | bytes 180256 | tf_op jit(solution)/shard_map/ppermute | solution.py:491
  96.3 3.3 %collective-permute-start.7 = (bf16[352,256]{1,0:T(8,128)(2,1)S(1)}, bf16[352,256]{1,0:T(8,128)(2,1)S(1)}, u32[]{:S(2)}, u32[]{:S(2)}) collective-permute-start(bf16[352,256]{1,0:T(8,128)(2,1)S(1)} %add_convert_fusion.1), channel_id=1, source_target_pairs={{0,8},{1,9},{2,10},{3,11},{4,12},{5,13},{6,14},{7,15},{8,0},{9,1},... | collective-permute-start | bytes 540680 | tf_op jit(solution)/shard_map/ppermute | solution.py:491
  99.5 0.0 collective-permute-done.1
  99.6 0.1 bitcast_convert_fusion
  99.6 5.3 %collective-permute-done.7 = bf16[352,256]{1,0:T(8,128)(2,1)S(1)} collective-permute-done((bf16[352,256]{1,0:T(8,128)(2,1)S(1)}, bf16[352,256]{1,0:T(8,128)(2,1)S(1)}, u32[]{:S(2)}, u32[]{:S(2)}) %collective-permute-start.7) | collective-permute-done | bytes 180256 | tf_op jit(solution)/shard_map/ppermute | solution.py:491
  105.0 1.5 %collective-permute-start.10 = (bf16[352,256]{1,0:T(8,128)(2,1)S(1)}, bf16[352,256]{1,0:T(8,128)(2,1)S(1)}, u32[]{:S(2)}, u32[]{:S(2)}) collective-permute-start(bf16[352,256]{1,0:T(8,128)(2,1)S(1)} %add_convert_fusion.refs_0_), channel_id=1, source_target_pairs={{0,3},{1,2},{2,1},{3,0},{4,7},{5,6},{6,5},{7,4},{8,11},{9,10},{10,... | collective-permute-start | bytes 540680 | tf_op jit(solution)/shard_map/ppermute | solution.py:491
  106.5 1.5 %collective-permute-start.9 = (bf16[352,256]{1,0:T(8,128)(2,1)S(1)}, bf16[352,256]{1,0:T(8,128)(2,1)S(1)}, u32[]{:S(2)}, u32[]{:S(2)}) collective-permute-start(bf16[352,256]{1,0:T(8,128)(2,1)S(1)} %add_convert_fusion.refs_0_), channel_id=1, source_target_pairs={{0,2},{1,3},{2,0},{3,1},{4,6},{5,7},{6,4},{7,5},{8,10},{9,11},{10,... | collective-permute-start | bytes 540680 | tf_op jit(solution)/shard_map/ppermute | solution.py:491
  108.0 0.5 collective-permute-start.8
  108.6 0.0 copy-done.18
  108.6 0.0 copy-start.3
  108.6 0.0 copy-start.4
  108.6 0.0 copy-start.5
  108.6 0.0 copy-start.6
  108.6 0.0 copy-start.7
  108.6 0.0 copy-start.8
  108.6 0.0 copy-start.9
  108.7 0.0 copy-start.10
  108.7 0.0 copy-start.12
  108.7 0.0 copy-start.13
  108.7 0.0 copy-start.14
  108.7 0.0 copy-start.15
  108.7 0.0 copy-start.16
  108.7 0.0 copy-start.17
  108.7 1.6 %maximum_select_fusion = f32[1,2048,256]{2,1,0:T(8,128)} fusion(f32[1,1024,256]{2,1,0:T(8,128)S(1)} %bitcast_convert_fusion, f32[1,1024,256]{2,1,0:T(8,128)S(1)} %bitcast.30, pred[]{:T(512)S(6)} %eq.5), kind=kLoop, calls=%fused_computation | loop fusion | flops 1572864 | bytes 4194305 | tf_op jit(solution)/shard_map/jit(_where)/select_n | solution.py:622
  110.3 1.3 %collective-permute-done.10.refs_3_ = bf16[352,256]{1,0:T(8,128)(2,1)S(1)} collective-permute-done((bf16[352,256]{1,0:T(8,128)(2,1)S(1)}, bf16[352,256]{1,0:T(8,128)(2,1)S(1)}, u32[]{:S(2)}, u32[]{:S(2)}) %collective-permute-start.10) | collective-permute-done | bytes 180256 | tf_op jit(solution)/shard_map/ppermute | solution.py:491
  111.6 1.8 %collective-permute-done.9.refs_2_ = bf16[352,256]{1,0:T(8,128)(2,1)S(1)} collective-permute-done((bf16[352,256]{1,0:T(8,128)(2,1)S(1)}, bf16[352,256]{1,0:T(8,128)(2,1)S(1)}, u32[]{:S(2)}, u32[]{:S(2)}) %collective-permute-start.9) | collective-permute-done | bytes 180256 | tf_op jit(solution)/shard_map/ppermute | solution.py:491
  113.4 0.1 collective-permute-done.8.refs_1_
  113.5 0.0 copy-done.11
  113.5 0.0 copy-done
  113.5 0.0 copy-done.1
  113.6 0.0 copy-done.2
  113.6 0.0 copy-done.3
  113.6 0.0 copy-done.4
  113.6 0.0 copy-done.5
  113.6 0.0 copy-done.6
  113.6 0.0 copy-done.7
  113.6 0.0 copy-done.8
  113.6 0.0 copy-done.9
  113.6 0.0 copy-done.10
  113.6 0.0 copy-done.12
  113.7 0.0 copy-done.13
  113.7 0.0 copy-done.14
  113.7 0.0 copy-done.15
  113.7 0.0 copy-done.16
  113.7 3.8 %update.1 = (f32[1,32,256]{2,1,0:T(8,128)}, f32[1,32,256]{2,1,0:T(8,128)}, f32[1,32,256]{2,1,0:T(8,128)}, bf16[1,32,256]{2,1,0:T(8,128)(2,1)}, f32[1,256,256]{2,...) custom-call(s32[1]{0:T(128)} %bitcast.7.which, ...), custom_call_target="tpu_custom_call" | custom-call | tf_op jit(solution)/shard_map/update/pallas_call | solution.py:633
  (10 shorter events, 0.1 us)
Async XLA Ops:
  3.1 2.5 %collective-permute-start = (bf16[1408,256]{1,0:T(8,128)(2,1)}, bf16[1408,256]{1,0:T(8,128)(2,1)S(1)}, u32[]{:S(2)}, u32[]{:S(2)}) collective-permute-start(bf16[1408,256]{1,0:T(8,128)(2,1)} %pack.1.mine), channel_id=1, source_target_pairs={{0,16},{16,0},{1,17},{17,1},{2,18},{18,2},{3,19},{19,3},{4,20},{20... | collective-permute-start | bytes 2162696 | tf_op jit(solution)/shard_map/ppermute | solution.py:487
  5.6 0.9 copy-start.19
  72.4 2.4 %collective-permute-start.2 = (bf16[1408,256]{1,0:T(8,128)(2,1)}, bf16[1408,256]{1,0:T(8,128)(2,1)S(1)}, u32[]{:S(2)}, u32[]{:S(2)}) collective-permute-start(bf16[1408,256]{1,0:T(8,128)(2,1)} %get-tuple-element.56), channel_id=1, source_target_pairs={{0,16},{16,0},{1,17},{17,1},{2,18},{18,2},{3,19},{19,3},{4,20},{20... | collective-permute-start | bytes 2162696 | tf_op jit(solution)/shard_map/ppermute | solution.py:487
  75.1 8.4 %collective-permute-start.3 = (bf16[352,256]{1,0:T(8,128)(2,1)S(1)}, bf16[352,256]{1,0:T(8,128)(2,1)}, u32[]{:S(2)}, u32[]{:S(2)}) collective-permute-start(bf16[352,256]{1,0:T(8,128)(2,1)S(1)} %get-tuple-element.81), channel_id=1, source_target_pairs={{0,1},{1,0},{2,3},{3,2},{4,5},{5,4},{6,7},{7,6},{8,9},{9,8},{10,11... | collective-permute-start | bytes 540680 | tf_op jit(solution)/shard_map/ppermute | solution.py:491
  78.0 10.1 %collective-permute-start.5 = (bf16[352,256]{1,0:T(8,128)(2,1)S(1)}, bf16[352,256]{1,0:T(8,128)(2,1)}, u32[]{:S(2)}, u32[]{:S(2)}) collective-permute-start(bf16[352,256]{1,0:T(8,128)(2,1)S(1)} %get-tuple-element.82), channel_id=1, source_target_pairs={{0,3},{1,2},{2,1},{3,0},{4,7},{5,6},{6,5},{7,4},{8,11},{9,10},{10,... | collective-permute-start | bytes 540680 | tf_op jit(solution)/shard_map/ppermute | solution.py:491
  79.5 10.0 %collective-permute-start.4 = (bf16[352,256]{1,0:T(8,128)(2,1)S(1)}, bf16[352,256]{1,0:T(8,128)(2,1)}, u32[]{:S(2)}, u32[]{:S(2)}) collective-permute-start(bf16[352,256]{1,0:T(8,128)(2,1)S(1)} %get-tuple-element.83), channel_id=1, source_target_pairs={{0,2},{1,3},{2,0},{3,1},{4,6},{5,7},{6,4},{7,5},{8,10},{9,11},{10,... | collective-permute-start | bytes 540680 | tf_op jit(solution)/shard_map/ppermute | solution.py:491
  79.5 29.0 %copy-start.18 = (f32[1024,256]{1,0:T(8,128)S(1)}, f32[1024,256]{1,0:T(8,128)}, u32[]{:S(2)}) copy-start(f32[1024,256]{1,0:T(8,128)} %get-tuple-element.53) | copy-start | bytes 3145732
  79.5 20.0 %collective-permute-start.1 = (bf16[1024,256]{1,0:T(8,128)(2,1)}, bf16[1024,256]{1,0:T(8,128)(2,1)S(1)}, u32[]{:S(2)}, u32[]{:S(2)}) collective-permute-start(bf16[1024,256]{1,0:T(8,128)(2,1)} %get-tuple-element.54), channel_id=1, source_target_pairs={{0,16},{16,0},{1,17},{17,1},{2,18},{18,2},{3,19},{19,3},{4,20},{20... | collective-permute-start | bytes 1572872 | tf_op jit(solution)/shard_map/ppermute | solution.py:487
  90.7 5.6 %collective-permute-start.6 = (bf16[352,256]{1,0:T(8,128)(2,1)S(1)}, bf16[352,256]{1,0:T(8,128)(2,1)S(1)}, u32[]{:S(2)}, u32[]{:S(2)}) collective-permute-start(bf16[352,256]{1,0:T(8,128)(2,1)S(1)} %add_convert_fusion.2), channel_id=1, source_target_pairs={{0,4},{1,5},{2,6},{3,7},{4,0},{5,1},{6,2},{7,3},{8,12},{9,13},{10,... | collective-permute-start | bytes 540680 | tf_op jit(solution)/shard_map/ppermute | solution.py:491
  96.3 8.7 %collective-permute-start.7 = (bf16[352,256]{1,0:T(8,128)(2,1)S(1)}, bf16[352,256]{1,0:T(8,128)(2,1)S(1)}, u32[]{:S(2)}, u32[]{:S(2)}) collective-permute-start(bf16[352,256]{1,0:T(8,128)(2,1)S(1)} %add_convert_fusion.1), channel_id=1, source_target_pairs={{0,8},{1,9},{2,10},{3,11},{4,12},{5,13},{6,14},{7,15},{8,0},{9,1},... | collective-permute-start | bytes 540680 | tf_op jit(solution)/shard_map/ppermute | solution.py:491
  105.0 8.6 %copy-start.11 = (f32[1,256,256]{2,1,0:T(8,128)S(1)}, f32[1,256,256]{2,1,0:T(8,128)}, u32[]{:S(2)}) copy-start(f32[1,256,256]{2,1,0:T(8,128)} %refs_18_.1) | copy-start | bytes 786436
  105.0 6.6 %collective-permute-start.10 = (bf16[352,256]{1,0:T(8,128)(2,1)S(1)}, bf16[352,256]{1,0:T(8,128)(2,1)S(1)}, u32[]{:S(2)}, u32[]{:S(2)}) collective-permute-start(bf16[352,256]{1,0:T(8,128)(2,1)S(1)} %add_convert_fusion.refs_0_), channel_id=1, source_target_pairs={{0,3},{1,2},{2,1},{3,0},{4,7},{5,6},{6,5},{7,4},{8,11},{9,10},{10,... | collective-permute-start | bytes 540680 | tf_op jit(solution)/shard_map/ppermute | solution.py:491
  106.5 6.9 %collective-permute-start.9 = (bf16[352,256]{1,0:T(8,128)(2,1)S(1)}, bf16[352,256]{1,0:T(8,128)(2,1)S(1)}, u32[]{:S(2)}, u32[]{:S(2)}) collective-permute-start(bf16[352,256]{1,0:T(8,128)(2,1)S(1)} %add_convert_fusion.refs_0_), channel_id=1, source_target_pairs={{0,2},{1,3},{2,0},{3,1},{4,6},{5,7},{6,4},{7,5},{8,10},{9,11},{10,... | collective-permute-start | bytes 540680 | tf_op jit(solution)/shard_map/ppermute | solution.py:491
  108.0 5.5 %collective-permute-start.8 = (bf16[352,256]{1,0:T(8,128)(2,1)S(1)}, bf16[352,256]{1,0:T(8,128)(2,1)S(1)}, u32[]{:S(2)}, u32[]{:S(2)}) collective-permute-start(bf16[352,256]{1,0:T(8,128)(2,1)S(1)} %add_convert_fusion.refs_0_), channel_id=1, source_target_pairs={{0,1},{1,0},{2,3},{3,2},{4,5},{5,4},{6,7},{7,6},{8,9},{9,8},{10,11... | collective-permute-start | bytes 540680 | tf_op jit(solution)/shard_map/ppermute | solution.py:491
  108.6 5.0 %copy-start = (f32[1,256,601]{1,0,2:T(1,128)S(1)}, f32[1,256,601]{1,0,2:T(1,128)}, u32[]{:S(2)}) copy-start(f32[1,256,601]{1,0,2:T(1,128)} %param.41) | copy-start | bytes 1846276
  108.6 5.0 %copy-start.1 = (f32[1,256,256]{2,1,0:T(8,128)S(1)}, f32[1,256,256]{2,1,0:T(8,128)}, u32[]{:S(2)}) copy-start(f32[1,256,256]{2,1,0:T(8,128)} %refs_7_.1) | copy-start | bytes 786436
  108.6 5.0 %copy-start.2 = (f32[1,256,256]{2,1,0:T(8,128)S(1)}, f32[1,256,256]{2,1,0:T(8,128)}, u32[]{:S(2)}) copy-start(f32[1,256,256]{2,1,0:T(8,128)} %refs_13_.1) | copy-start | bytes 786436
  108.6 5.0 %copy-start.3 = (f32[1,256,256]{2,1,0:T(8,128)S(1)}, f32[1,256,256]{2,1,0:T(8,128)}, u32[]{:S(2)}) copy-start(f32[1,256,256]{2,1,0:T(8,128)} %refs_16_.1) | copy-start | bytes 786436
  108.6 5.0 %copy-start.4 = (f32[1,256,601]{1,0,2:T(1,128)S(1)}, f32[1,256,601]{1,0,2:T(1,128)}, u32[]{:S(2)}) copy-start(f32[1,256,601]{1,0,2:T(1,128)} %param.42) | copy-start | bytes 1846276
  108.6 5.0 %copy-start.5 = (f32[1,256,601]{1,0,2:T(1,128)S(1)}, f32[1,256,601]{1,0,2:T(1,128)}, u32[]{:S(2)}) copy-start(f32[1,256,601]{1,0,2:T(1,128)} %param.43) | copy-start | bytes 1846276
  108.6 5.0 %copy-start.6 = (f32[1,256,256]{2,1,0:T(8,128)S(1)}, f32[1,256,256]{2,1,0:T(8,128)}, u32[]{:S(2)}) copy-start(f32[1,256,256]{2,1,0:T(8,128)} %refs_8_.1) | copy-start | bytes 786436
  108.6 5.0 %copy-start.7 = (f32[1,256,256]{2,1,0:T(8,128)S(1)}, f32[1,256,256]{2,1,0:T(8,128)}, u32[]{:S(2)}) copy-start(f32[1,256,256]{2,1,0:T(8,128)} %refs_9_.1) | copy-start | bytes 786436
  108.6 5.0 %copy-start.8 = (f32[1,256,256]{2,1,0:T(8,128)S(1)}, f32[1,256,256]{2,1,0:T(8,128)}, u32[]{:S(2)}) copy-start(f32[1,256,256]{2,1,0:T(8,128)} %refs_14_.1) | copy-start | bytes 786436
  108.6 5.0 %copy-start.9 = (f32[1,256,256]{2,1,0:T(8,128)S(1)}, f32[1,256,256]{2,1,0:T(8,128)}, u32[]{:S(2)}) copy-start(f32[1,256,256]{2,1,0:T(8,128)} %refs_15_.1) | copy-start | bytes 786436
  108.7 5.0 %copy-start.10 = (f32[1,256,256]{2,1,0:T(8,128)S(1)}, f32[1,256,256]{2,1,0:T(8,128)}, u32[]{:S(2)}) copy-start(f32[1,256,256]{2,1,0:T(8,128)} %refs_17_.1) | copy-start | bytes 786436
  108.7 5.0 %copy-start.12 = (f32[1,32,256]{2,1,0:T(8,128)S(1)}, f32[1,32,256]{2,1,0:T(8,128)}, u32[]{:S(2)}) copy-start(f32[1,32,256]{2,1,0:T(8,128)} %refs_4_.1) | copy-start | bytes 98308
  108.7 5.0 %copy-start.13 = (f32[1,32,256]{2,1,0:T(8,128)S(1)}, f32[1,32,256]{2,1,0:T(8,128)}, u32[]{:S(2)}) copy-start(f32[1,32,256]{2,1,0:T(8,128)} %refs_5_.1) | copy-start | bytes 98308
  108.7 5.0 %copy-start.14 = (f32[1,32,256]{2,1,0:T(8,128)S(1)}, f32[1,32,256]{2,1,0:T(8,128)}, u32[]{:S(2)}) copy-start(f32[1,32,256]{2,1,0:T(8,128)} %refs_6_.1) | copy-start | bytes 98308
  108.7 5.0 %copy-start.15 = (f32[1,2,256]{2,1,0:T(2,128)S(1)}, f32[1,2,256]{2,1,0:T(2,128)}, u32[]{:S(2)}) copy-start(f32[1,2,256]{2,1,0:T(2,128)} %refs_10_.1) | copy-start | bytes 6148
  108.7 5.0 %copy-start.16 = (f32[1,2,256]{2,1,0:T(2,128)S(1)}, f32[1,2,256]{2,1,0:T(2,128)}, u32[]{:S(2)}) copy-start(f32[1,2,256]{2,1,0:T(2,128)} %refs_11_.1) | copy-start | bytes 6148
  108.7 5.0 %copy-start.17 = (f32[1,2,256]{2,1,0:T(2,128)S(1)}, f32[1,2,256]{2,1,0:T(2,128)}, u32[]{:S(2)}) copy-start(f32[1,2,256]{2,1,0:T(2,128)} %refs_12_.1) | copy-start | bytes 6148
